TPU v7x, 512 devices: a whole 4x4x16 slice. The times are simulated.
512 devices in a mesh: leaf: 16 (over y, x), src: 32 (over z, core).
Axes of the slice: x: 4, y: 4, z: 16, core: 2. Of those that a mesh axis runs over, the one named last changes fastest.
Arguments:
- leaf_rhs: float32 [16, 8192, 1024], P('leaf', 'src'), may hold values from -6 to 6
- leaf_factor: float32 [16, 1536, 1024], P('leaf', 'src'), may hold values from -0.1875 to 0.1875
- pivot_count: int32 [16], P('leaf'), may hold values from 128 to 1024, as said below
- parent: int32 [16], replicated, may hold values from 0 to 3, as said below
- leaf_index: int32 [16, 512], replicated, may hold values from 0 to 1023, as said below
- separator_rhs: float32 [16, 512, 4, 512], P('leaf', 'src'), may hold values from -6 to 6
- separator_factor: float32 [4, 1024, 512], P(None, 'src'), may hold values from -0.25 to 0.25
- separator_index: int32 [4, 512], replicated, may hold values from 0 to 511, as said below
- root_rhs: float32 [16, 512, 512], P('leaf', 'src'), may hold values from -6 to 6
- root_factor: float32 [512, 512], P('src'), may hold values from -0.25 to 0.25
Outputs:
- leaf_solution: float32 [16, 8192, 1024], P('leaf', 'src')
- separator_solution: float32 [16, 512, 4, 512], P('leaf', 'src')
- root_solution: float32 [16, 512, 512], P('leaf', 'src')
Inputs may be any that keep to these rules, and one draw needn't show every extreme that they name: Every separator is the parent of exactly 4 leaves. `pivot_count`: multiples of 128. `leaf_index`: each row holds distinct values. `separator_index`: each row holds distinct values.
All inputs are finite; a program needn't handle non-finite values.
Results may differ from a plain program's by a relative error of at most 0.0003.
Values sent between devices are 32-bit elements; how exact they have to be, the bound alone decides.
No kernel may reach another device: no remote copies, remote signals or barrier semaphores. Data moves between devices by JAX's collectives and lax.ppermute only.
A program may use at most 128 MiB of HBM per device.

v0:
```python
import jax
import jax.numpy as jnp
from jax import lax
from jax.sharding import PartitionSpec as P


def front_matrix(block_rows, first_row, pivots, top_rows):
    row_ids = first_row + jnp.arange(block_rows.shape[0], dtype=jnp.int32)[:, None]
    col_ids = jnp.arange(block_rows.shape[1], dtype=jnp.int32)[None, :]
    in_pivot = row_ids < top_rows
    within = jnp.where(in_pivot, (row_ids < pivots) & (col_ids < row_ids), True)
    keeper = (col_ids < pivots) & within
    diagonal = in_pivot & (col_ids == row_ids) & (col_ids < pivots)
    return jnp.where(keeper, block_rows, 0.0) + diagonal.astype(block_rows.dtype)


def against_rows(left_side, matrix):
    return lax.dot_general(
        left_side,
        matrix,
        (((1,), (1,)), ((), ())),
        precision=lax.Precision.HIGHEST,
        preferred_element_type=jnp.float32,
    )


def against_cols(left_side, matrix):
    return jnp.dot(
        left_side, matrix, precision=lax.Precision.HIGHEST, preferred_element_type=jnp.float32
    )


def local(
    leaf_rhs,
    leaf_factor,
    pivot_count,
    parent,
    leaf_index,
    separator_rhs,
    separator_factor,
    separator_index,
    root_rhs,
    root_factor,
):
    leaves = lax.axis_size("leaf")
    sources = lax.axis_size("src")
    separators = separator_factor.shape[0]
    right_side = leaf_rhs[0]
    columns = right_side.shape[0]
    pivot_slots = right_side.shape[1]
    block_cols = columns // leaves
    border_rows = leaf_index.shape[1]
    pivots = pivot_count[0]
    leaf_whole = lax.all_gather(leaf_factor[0], "src", axis=0, tiled=True)
    leaf_operator = front_matrix(leaf_whole, 0, pivots, pivot_slots)
    forward = against_rows(right_side, leaf_operator)
    leaf_solved = forward[:, :pivot_slots]
    leaf_border = forward[:, pivot_slots:]
    outgoing = leaf_border.reshape(leaves, block_cols, border_rows)
    incoming = lax.all_to_all(outgoing, "leaf", split_axis=0, concat_axis=0, tiled=True)
    sep_width = separator_factor.shape[2]
    sep_height = separator_factor.shape[1] * sources
    targets = (parent[:, None] * sep_height + leaf_index).reshape(-1)
    border_terms = jnp.transpose(incoming, (1, 0, 2)).reshape(block_cols, leaves * border_rows)
    updates = (
        jnp.zeros((block_cols, separators * sep_height), jnp.float32)
        .at[:, targets]
        .add(border_terms)
    )
    updates = updates.reshape(block_cols, separators, sep_height)
    sep_pivot = separator_rhs[0] + updates[:, :, :sep_width]
    sep_whole = lax.all_gather(separator_factor, "src", axis=1, tiled=True)
    sep_operator = jax.vmap(front_matrix, in_axes=(0, None, None, None))(
        sep_whole, 0, sep_width, sep_width
    )
    sep_forward = jnp.einsum(
        "cjp,jrp->cjr",
        sep_pivot,
        sep_operator,
        precision=lax.Precision.HIGHEST,
        preferred_element_type=jnp.float32,
    )
    sep_solved = sep_forward[:, :, :sep_width]
    sep_border = sep_forward[:, :, sep_width:] + updates[:, :, sep_width:]
    root_whole = lax.all_gather(root_factor, "src", axis=0, tiled=True)
    root_extent = root_whole.shape[0]
    root_operator = front_matrix(root_whole, 0, root_extent, root_extent)
    sep_border_width = separator_index.shape[1]
    root_terms = (
        jnp.zeros((block_cols, root_extent), jnp.float32)
        .at[:, separator_index.reshape(-1)]
        .add(sep_border.reshape(block_cols, separators * sep_border_width))
    )
    root_total = root_rhs[0] + root_terms
    root_solved = against_rows(root_total, root_operator)
    root_answer = against_cols(root_solved, root_operator)
    root_border = root_answer[:, separator_index]
    sep_joined = jnp.concatenate([sep_solved, root_border], axis=2)
    sep_answer = jnp.einsum(
        "cjr,jrp->cjp",
        sep_joined,
        sep_operator,
        precision=lax.Precision.HIGHEST,
        preferred_element_type=jnp.float32,
    )
    sep_full = jnp.concatenate([sep_answer, root_border], axis=2)
    picked_down = sep_full.reshape(block_cols, separators * sep_height)[:, targets]
    send_down = jnp.transpose(picked_down.reshape(block_cols, leaves, border_rows), (1, 0, 2))
    received = lax.all_to_all(send_down, "leaf", split_axis=0, concat_axis=0, tiled=True)
    parent_border = received.reshape(columns, border_rows)
    leaf_joined = jnp.concatenate([leaf_solved, parent_border], axis=1)
    leaf_answer = against_cols(leaf_joined, leaf_operator)
    return (leaf_answer[None], sep_answer[None], root_answer[None])


def solution(mesh):
    return jax.shard_map(
        local,
        mesh=mesh,
        in_specs=(
            P("leaf", "src", None),
            P("leaf", "src", None),
            P("leaf"),
            P(),
            P(),
            P("leaf", "src", None, None),
            P(None, "src", None),
            P(),
            P("leaf", "src", None),
            P("src", None),
        ),
        out_specs=(P("leaf", "src", None), P("leaf", "src", None, None), P("leaf", "src", None)),
        check_vma=False,
    )
```

profile of v0, /device:TPU:1, one launch (start us, length us, event | category | flops | bytes accessed | tf_op | source)
XLA Modules:
  0.0 330.5 jit_solution(18047587120019130155)
XLA Ops:
  7.2 0.0 copy-start
  7.2 0.0 all-gather.9.cloned.1.call-start
  7.2 0.7 all-gather.9.cloned.1.call-update
  7.9 0.0 all-gather.5.cloned.1.call-start
  8.0 0.7 all-gather.5.cloned.1.call-update
  8.7 0.0 all-gather.7.cloned.1.call-start
  8.7 0.7 all-gather.7.cloned.1.call-update
  10.1 0.0 copy-start.13
  10.1 0.7 broadcast_multiply_fusion
  10.8 0.8 add_bitcast_fusion
  11.7 0.7 fusion.41
  12.4 0.6 broadcast_clamp_fusion
  13.0 1.4 fusion.16
  14.5 78.3 %all-gather.9.cloned.1.call-done = f32[1,1536,1024]{2,1,0:T(8,128)} async-done(((f32[1,48,1024]{2,1,0:T(8,128)}), f32[1,1536,1024]{2,1,0:T(8,128)}) %all-gather.9.cloned.1.call-update) | async-done | bytes 6291472 | tf_op jit(solution)/shard_map/all_gather | solution.py:54
  92.8 11.4 %convolution_bitcast_fusion = f32[256,1536]{1,0:T(8,128)S(1)} fusion(f32[1,256,1024]{2,1,0:T(8,128)S(1)} %copy-done, f32[1,1536,1024]{2,1,0:T(8,128)} %all-gather.9.cloned.1.call-done, pred[1536]{0:T(1024)(128)(4,1)S(1)} %get-tuple-element.15, pred[1536]{0:T(1024)(128)(4,1)S(1)} %get-tuple-element.16, pred[1024]{0:T(1024)(128)(4,1)S(1)} %iota_compare_fusion.9), kind=kOutput, calls=%fused_computation.22 | convolution fusion | flops 4847566848 | bytes 8916992 | tf_op jit(solution)/shard_map/dot_general | solution.py:18
  104.3 1.2 copy-done.1
  105.4 0.8 slice.29
  106.3 6.6 %all-to-all-start = ((f32[16,16,512]{2,1,0:T(8,128)}), f32[16,16,512]{2,1,0:T(8,128)}, u32[]{:S(2)}, u32[]{:S(2)}) async-start(f32[16,16,512]{2,1,0:T(8,128)} %bitcast.65), calls=%async_computation | async-start | bytes 1048576 | tf_op jit(solution)/shard_map/all_to_all | solution.py:60
  112.9 0.1 copy.22
  113.0 10.7 %all-to-all-done = f32[16,16,512]{2,1,0:T(8,128)} async-done(((f32[16,16,512]{2,1,0:T(8,128)}), f32[16,16,512]{2,1,0:T(8,128)}, u32[]{:S(2)}, u32[]{:S(2)}) %all-to-all-start) | async-done | bytes 524320 | tf_op jit(solution)/shard_map/all_to_all | solution.py:60
  123.7 3.5 %copy.19 = f32[16,16,512]{0,2,1:T(8,128)} copy(f32[16,16,512]{2,0,1:T(8,128)} %bitcast.7) | data formatting | bytes 1048576 | tf_op jit(solution)/shard_map/transpose | solution.py:64
  127.3 45.7 %scatter_custom_fusion = f32[16,4096]{0,1:T(8,128)} fusion(s32[8192]{0:T(1024)S(1)} %bitcast.74, f32[8192,16]{1,0:T(8,128)} %bitcast.64, f32[]{:T(128)} %constant.8.clone.1), kind=kCustom, calls=%fused_computation.41 | custom fusion | flops 131072 | bytes 262656 | tf_op jit(solution)/shard_map/scatter-add | solution.py:68
  173.0 3.0 fusion.52
  176.0 2.2 copy.39
  178.2 2.2 copy.40
  180.4 1.0 bitcast_add_fusion
  181.4 0.0 all-gather.5.cloned.1.call-done
  181.4 0.0 copy-start.2
  181.4 10.5 %fusion.27 = f32[16,4,1024]{2,0,1:T(8,128)S(1)} fusion(f32[4,1024,512]{2,1,0:T(8,128)} %all-gather.5.cloned.1.call-done, f32[1024,512]{1,0:T(8,128)S(1)} %get-tuple-element.14, pred[1024,512]{1,0:T(8,128)(4,1)} %get-tuple-element.13, f32[16,4,512]{2,1,0:T(4,128)S(1)} %bitcast_add_fusion), kind=kOutput, calls=%fused_computation.36 | convolution fusion | flops 406847488 | bytes 11403264 | tf_op jit(solution)/shard_map/cjp,jrp->cjr/dot_general | solution.py:76
  191.9 0.0 copy-done.2
  192.0 0.7 copy.41
  192.7 2.2 copy.25
  194.9 12.1 %scatter_fusion = f32[16,512]{0,1:T(8,128)S(1)} fusion(f32[16,512]{0,1:T(8,128)S(1)} %bitcast.62, s32[2048]{0:T(1024)S(1)} %bitcast.76, f32[2048,16]{1,0:T(8,128)} %copy.25), kind=kCustom, calls=%fused_computation.3 | custom fusion | flops 32768 | bytes 401408 | tf_op jit(solution)/shard_map/scatter-add | solution.py:92
  207.0 34.1 %all-gather.7.cloned.1.call-done = f32[512,512]{1,0:T(8,128)} async-done(((f32[16,512]{1,0:T(8,128)}), f32[512,512]{1,0:T(8,128)}) %all-gather.7.cloned.1.call-update) | async-done | bytes 1048592 | tf_op jit(solution)/shard_map/all_gather | solution.py:85
  241.1 2.5 fusion.38
  243.6 1.5 fusion.37
  245.1 0.9 copy.26
  246.0 7.6 %gather_fusion = f32[2048,16]{1,0:T(8,128)} fusion(f32[16,512]{0,1:T(8,128)S(1)} %copy.26, s32[2048]{0:T(1024)S(1)} %broadcast_clamp_fusion.1), kind=kCustom, calls=%fused_computation | custom fusion | bytes 270336 | tf_op jit(solution)/shard_map/gather | solution.py:97
  253.7 1.5 copy.28
  255.2 7.7 %fusion = f32[4,512,16]{1,2,0:T(8,128)S(1)} fusion(f32[4,1024,512]{2,1,0:T(8,128)} %all-gather.5.cloned.1.call-done, f32[1024,512]{1,0:T(8,128)S(1)} %get-tuple-element.14, pred[1024,512]{1,0:T(8,128)(4,1)} %get-tuple-element.13, f32[16,4,512]{2,0,1:T(8,128)S(1)} %bitcast.67, f32[16,4,512]{2,0,1:T(8,128)S(1)} %get-tuple-element.11), kind=kOutput, calls=%fused_computation.5 | convolution fusion | flops 406913024 | bytes 11403264 | tf_op jit(solution)/shard_map/cjr,jrp->cjp/dot_general | solution.py:99
  262.9 0.7 pad_maximum_fusion
  263.6 1.5 copy.37
  265.2 27.8 %gather_fusion.1 = f32[8192,16]{1,0:T(8,128)} fusion(f32[16,4096]{0,1:T(8,128)S(1)} %bitcast.60, s32[8192]{0:T(1024)S(1)} %copy-done.3), kind=kCustom, calls=%fused_computation.1 | custom fusion | bytes 1081344 | tf_op jit(solution)/shard_map/gather | solution.py:107
  293.1 3.5 %copy.31 = f32[16,16,512]{2,0,1:T(8,128)} copy(f32[16,16,512]{0,2,1:T(8,128)} %bitcast.63) | data formatting | bytes 1048576 | tf_op jit(solution)/shard_map/reshape | solution.py:108
  296.6 6.7 %all-to-all-start.1 = ((f32[16,16,512]{2,1,0:T(8,128)}), f32[16,16,512]{2,1,0:T(8,128)S(1)}, u32[]{:S(2)}, u32[]{:S(2)}) async-start(f32[16,16,512]{2,1,0:T(8,128)} %bitcast.21), calls=%async_computation.1 | async-start | bytes 1048576 | tf_op jit(solution)/shard_map/all_to_all | solution.py:109
  303.2 0.7 copy.32
  304.0 10.1 %all-to-all-done.1 = f32[16,16,512]{2,1,0:T(8,128)S(1)} async-done(((f32[16,16,512]{2,1,0:T(8,128)}), f32[16,16,512]{2,1,0:T(8,128)S(1)}, u32[]{:S(2)}, u32[]{:S(2)}) %all-to-all-start.1) | async-done | bytes 524320 | tf_op jit(solution)/shard_map/all_to_all | solution.py:109
  314.1 9.9 %fusion.24 = f32[1,256,1024]{2,1,0:T(8,128)} fusion(f32[256,512]{1,0:T(8,128)S(1)} %bitcast.72, f32[256,1024]{1,0:T(8,128)S(1)} %slice-done, f32[1,1536,1024]{2,1,0:T(8,128)} %all-gather.9.cloned.1.call-done, pred[1536]{0:T(1024)(128)(4,1)S(1)} %copy-done.7, pred[1536]{0:T(1024)(128)(4,1)S(1)} %copy-done.9, pred[1024]{0:T(1024)(128)(4,1)S(1)} %copy-done.14), kind=kOutput, calls=%fused_computation.35 | convolution fusion | flops 4847960064 | bytes 8916992 | tf_op jit(solution)/shard_map/dot_general | solution.py:28
  (38 shorter events, 0.2 us)
Async XLA Ops:
  7.2 85.6 %copy-start = (f32[1,256,1024]{2,1,0:T(8,128)S(1)}, f32[1,256,1024]{2,1,0:T(8,128)}, u32[]{:S(2)}) copy-start(f32[1,256,1024]{2,1,0:T(8,128)} %param.10) | copy-start | bytes 3145732
  7.2 85.6 %all-gather.9.cloned.1.call-start = ((), (), s32[]{:S(2)}) async-start(), calls=%async_computation.4 | async-start | bytes 6488064 | tf_op jit(solution)/shard_map/all_gather | solution.py:54
  7.9 173.5 %all-gather.5.cloned.1.call-start = ((), (), s32[]{:S(2)}) async-start(), calls=%async_computation.2 | async-start | bytes 8650752 | tf_op jit(solution)/shard_map/all_gather | solution.py:72
  8.7 232.4 %all-gather.7.cloned.1.call-start = ((), (), s32[]{:S(2)}) async-start(), calls=%async_computation.3 | async-start | bytes 1081344 | tf_op jit(solution)/shard_map/all_gather | solution.py:85
  9.4 83.4 %copy-start.10 = (pred[512]{0:T(512)(128)(4,1)}, pred[512]{0:T(512)(128)(4,1)S(1)}, u32[]{:S(2)}) copy-start(pred[512]{0:T(512)(128)(4,1)S(1)} %iota_compare_fusion.10) | copy-start | bytes 1540
  10.1 82.7 %copy-start.6 = (pred[1536]{0:T(1024)(128)(4,1)}, pred[1536]{0:T(1024)(128)(4,1)S(1)}, u32[]{:S(2)}) copy-start(pred[1536]{0:T(1024)(128)(4,1)S(1)} %get-tuple-element.15) | copy-start | bytes 4612
  10.1 82.7 %copy-start.8 = (pred[1536]{0:T(1024)(128)(4,1)}, pred[1536]{0:T(1024)(128)(4,1)S(1)}, u32[]{:S(2)}) copy-start(pred[1536]{0:T(1024)(128)(4,1)S(1)} %get-tuple-element.16) | copy-start | bytes 4612
  10.1 82.7 %copy-start.13 = (pred[1024]{0:T(1024)(128)(4,1)}, pred[1024]{0:T(1024)(128)(4,1)S(1)}, u32[]{:S(2)}) copy-start(pred[1024]{0:T(1024)(128)(4,1)S(1)} %iota_compare_fusion.9) | copy-start | bytes 3076
  104.2 1.2 copy-start.1
  105.4 7.4 %copy-start.4 = (f32[1,16,512]{2,1,0:T(8,128)S(1)}, f32[1,16,512]{2,1,0:T(8,128)}, u32[]{:S(2)}) copy-start(f32[1,16,512]{2,1,0:T(8,128)} %param.18) | copy-start | bytes 98308
  105.4 7.6 %copy-start.5 = (s32[4,512]{1,0:T(4,128)S(1)}, s32[4,512]{1,0:T(4,128)}, u32[]{:S(2)}) copy-start(s32[4,512]{1,0:T(4,128)} %param.17) | copy-start | bytes 24580
  106.3 17.5 %all-to-all-start = ((f32[16,16,512]{2,1,0:T(8,128)}), f32[16,16,512]{2,1,0:T(8,128)}, u32[]{:S(2)}, u32[]{:S(2)}) async-start(f32[16,16,512]{2,1,0:T(8,128)} %bitcast.65), calls=%async_computation | async-start | bytes 1048576 | tf_op jit(solution)/shard_map/all_to_all | solution.py:60
  181.4 10.5 %copy-start.2 = (f32[16,4,512]{2,0,1:T(8,128)S(1)}, f32[16,4,512]{2,0,1:T(8,128)}, u32[]{:S(2)}) copy-start(f32[16,4,512]{2,0,1:T(8,128)} %copy.40) | copy-start | bytes 393220
  207.0 36.6 %copy-start.11 = (pred[512]{0:T(512)(128)(4,1)S(1)}, pred[512]{0:T(512)(128)(4,1)}, u32[]{:S(2)}) copy-start(pred[512]{0:T(512)(128)(4,1)} %copy-done.10) | copy-start | bytes 1540
  241.1 2.5 copy-start.12
  262.9 2.3 copy-start.3
  296.6 17.5 %slice-start = ((f32[256,1536]{1,0:T(8,128)}), f32[256,1024]{1,0:T(8,128)S(1)}, s32[]{:S(2)}) async-start(f32[256,1536]{1,0:T(8,128)} %copy-done.1), calls=%async_computation.5 | async-start | bytes 2097152 | tf_op jit(solution)/shard_map/slice | solution.py:57
  296.6 17.5 %copy-start.7 = (pred[1536]{0:T(1024)(128)(4,1)S(1)}, pred[1536]{0:T(1024)(128)(4,1)}, u32[]{:S(2)}) copy-start(pred[1536]{0:T(1024)(128)(4,1)} %copy-done.6) | copy-start | bytes 4612
  296.6 17.5 %copy-start.9 = (pred[1536]{0:T(1024)(128)(4,1)S(1)}, pred[1536]{0:T(1024)(128)(4,1)}, u32[]{:S(2)}) copy-start(pred[1536]{0:T(1024)(128)(4,1)} %copy-done.8) | copy-start | bytes 4612
  296.6 17.5 %copy-start.14 = (pred[1024]{0:T(1024)(128)(4,1)S(1)}, pred[1024]{0:T(1024)(128)(4,1)}, u32[]{:S(2)}) copy-start(pred[1024]{0:T(1024)(128)(4,1)} %copy-done.13) | copy-start | bytes 3076
  296.6 17.5 %all-to-all-start.1 = ((f32[16,16,512]{2,1,0:T(8,128)}), f32[16,16,512]{2,1,0:T(8,128)S(1)}, u32[]{:S(2)}, u32[]{:S(2)}) async-start(f32[16,16,512]{2,1,0:T(8,128)} %bitcast.21), calls=%async_computation.1 | async-start | bytes 1048576 | tf_op jit(solution)/shard_map/all_to_all | solution.py:109
Sparse Core Ops, SparseCore 0:
  10.1 82.6 all-gather.8
  94.9 76.7 all-gather.4
  173.8 67.2 all-gather.6
where the time goes:
time: 331 us
  waiting for transfers between devices  135 us (41%)
  other arithmetic  63.9 us (19%)
  local copies, waits for them, and re-layouts  59.7 us (18%)
  matrix products  43.6 us (13%)
  between operations  14.7 us (4%)
  starting transfers between devices  13.3 us (4%)
    all_gather x1, waiting for transfers between devices, local(): leaf_whole = lax.all_gather(leaf_factor[0], 'src', axis=0, tiled=True)  78.3 us
    scatter-add x1, other arithmetic, local(): updates = jnp.zeros((block_cols, separators * sep_height), jnp.float32).a...  45.7 us
    all_gather x1, waiting for transfers between devices, local(): root_whole = lax.all_gather(root_factor, 'src', axis=0, tiled=True)  34.1 us
    gather x1, local copies, waits for them, and re-layouts, local(): sep_full.reshape(block_cols, separators * sep_height)[:, targets]  27.8 us
    dot_general x2, matrix products, against_rows(): lax.dot_general(left_side, matrix, (((1,), (1,)), ((), ())), precision=la...  13.9 us
    scatter-add x1, other arithmetic, local(): root_terms = jnp.zeros((block_cols, root_extent), jnp.float32).at[:, sepa...  12.1 us
    dot_general x2, matrix products, against_cols(): jnp.dot(left_side, matrix, precision=lax.Precision.HIGHEST, preferred_ele...  11.4 us
    all_to_all x1, waiting for transfers between devices, local(): lax.all_to_all(outgoing, 'leaf', split_axis=0, concat_axis=0, tiled=True)  10.7 us
  transfers between devices with their start and end apart: 5, of which 4 were waited for; matrix products, arithmetic and copies ran while one was open for 30% of the time, Pallas kernels for 0%

commit v1 on v0

v1 whole, which is shorter than its diff:
```python
import jax
import jax.numpy as jnp
from jax import lax
from jax.experimental import pallas as pl
from jax.experimental.pallas import tpu as pltpu
from jax.sharding import Mesh, PartitionSpec as P

NY, NX, NZ, NC = 4, 4, 16, 2
F32, BF16 = jnp.float32, jnp.bfloat16
LANES = 128


def split2(value):
    high = value.astype(BF16)
    return high, (value - high.astype(F32)).astype(BF16)


def dot_nt(a, b):
    return lax.dot_general(a, b, (((1,), (1,)), ((), ())), preferred_element_type=F32)


def dot_nn(a, b):
    return lax.dot_general(a, b, (((1,), (0,)), ((), ())), preferred_element_type=F32)


def three_products(dot, a, b):
    return dot(a[0], b[0]) + (dot(a[1], b[0]) + dot(a[0], b[1]))


def stacked_products(dot, a, b):
    rows = a[0].shape[0]
    both = dot(jnp.concatenate([a[0], a[1]], axis=0), b[0])
    return both[:rows] + (both[rows:] + dot(a[0], b[1]))


def params(mebibytes):
    return pltpu.CompilerParams(vmem_limit_bytes=mebibytes * 1024 * 1024)


def full_vmem():
    return pl.BlockSpec(memory_space=pltpu.VMEM)


def full_smem():
    return pl.BlockSpec(memory_space=pltpu.SMEM)


def anywhere():
    return pl.BlockSpec(memory_space=pl.ANY)


def line_copies(c, own_ref, other_ref, buffer, shards, sem):
    first, last = shards
    copies = []
    for ref, parity in ((own_ref, c), (other_ref, 1 - c)):
        for z in range(first // 2, last // 2 + 1):
            shard = 2 * z + parity
            row = pl.multiple_of((shard - first) * 48, 16)
            at = z - (NZ - ref.shape[0])
            copies.append(((shard >= first) & (shard <= last), ref, at, row))

    def each(action):
        for wanted, ref, at, row in copies:
            @pl.when(wanted)
            def _():
                for half in range(2):
                    action(pltpu.make_async_copy(
                        ref.at[at, pl.ds(48 * half, 48), :],
                        buffer.at[pl.ds(row, 48), pl.ds(512 * half, 512)],
                        sem,
                    ))

    return each


def leaf_border_kernel(place_ref, count_ref, rhs_ref, own_ref, other_ref, border_ref, buffer, sem):
    each = line_copies(place_ref[0], own_ref, other_ref, buffer, (21, 31), sem)
    each(lambda copy: copy.start())
    cols = lax.broadcasted_iota(jnp.int32, rhs_ref.shape, 1)
    rhs = split2(jnp.where(cols < count_ref[0], rhs_ref[...], 0.0))
    each(lambda copy: copy.wait())
    for block in range(2):
        rows = split2(buffer[pl.ds(16 + 256 * block, 256), :])
        border_ref[:, 256 * block : 256 * (block + 1)] = three_products(dot_nt, rhs, rows)


def leaf_border(place, count, rhs, own, other):
    return pl.pallas_call(
        leaf_border_kernel,
        out_shape=jax.ShapeDtypeStruct((256, 512), F32),
        in_specs=[full_smem(), full_smem(), full_vmem(), anywhere(), anywhere()],
        out_specs=full_vmem(),
        scratch_shapes=[pltpu.VMEM((528, 1024), F32), pltpu.SemaphoreType.DMA],
        compiler_params=params(16),
        name="leaf_border",
    )(place, count, rhs, own, other)


def leaf_pivot_kernel(
    place_ref, count_ref, rhs_ref, own_ref, other_ref,
    part_ref, border_high_ref, border_low_ref,
    buffer, border_buffer, high_ref, low_ref, sem,
):
    c = place_ref[0]
    each = line_copies(c, own_ref, other_ref, buffer, (0, 21), sem.at[0])
    each_border = line_copies(c, own_ref, other_ref, border_buffer, (21, 31), sem.at[1])
    each(lambda copy: copy.start())
    each_border(lambda copy: copy.start())
    count = count_ref[0]
    cols = lax.broadcasted_iota(jnp.int32, rhs_ref.shape, 1)
    rhs = split2(jnp.where(cols < count, rhs_ref[...], 0.0))
    each(lambda copy: copy.wait())
    solved = []
    for block in range(4):
        first, wide = 256 * block, 256 * (block + 1)
        rows = first + lax.broadcasted_iota(jnp.int32, (256, wide), 0)
        columns = lax.broadcasted_iota(jnp.int32, (256, wide), 1)
        values = jnp.where(columns < rows, buffer[first:wide, :wide], 0.0)
        values = jnp.where(columns == rows, 1.0, values)
        values = jnp.where(rows < count, values, 0.0)
        high, low = split2(values)
        high_ref[first:wide, :wide] = high
        low_ref[first:wide, :wide] = low
        solved.append(three_products(dot_nt, (rhs[0][:, :wide], rhs[1][:, :wide]), (high, low)))
    solved = split2(jnp.concatenate(solved, axis=1))
    for block in range(4):
        first, wide = 256 * block, 256 * (block + 1)
        part_ref[:, first:wide] = three_products(
            dot_nn,
            (solved[0][:, first:], solved[1][:, first:]),
            (high_ref[first:, first:wide], low_ref[first:, first:wide]),
        )
    each_border(lambda copy: copy.wait())
    border_high_ref[...], border_low_ref[...] = split2(border_buffer[16:, :])


def leaf_pivot(place, count, rhs, own, other):
    return pl.pallas_call(
        leaf_pivot_kernel,
        out_shape=(
            jax.ShapeDtypeStruct((256, 1024), F32),
            jax.ShapeDtypeStruct((512, 1024), BF16),
            jax.ShapeDtypeStruct((512, 1024), BF16),
        ),
        in_specs=[full_smem(), full_smem(), full_vmem(), anywhere(), anywhere()],
        out_specs=(full_vmem(),) * 3,
        scratch_shapes=[
            pltpu.VMEM((1056, 1024), F32),
            pltpu.VMEM((528, 1024), F32),
            pltpu.VMEM((1024, 1024), BF16),
            pltpu.VMEM((1024, 1024), BF16),
            pltpu.SemaphoreType.DMA((2,)),
        ],
        compiler_params=params(24),
        name="leaf_pivot",
    )(place, count, rhs, own, other)


def leaf_last_kernel(count_ref, part_ref, border_ref, high_ref, low_ref, out_ref):
    border = split2(border_ref[...])
    answer = part_ref[...] + three_products(dot_nn, border, (high_ref[...], low_ref[...]))
    width = answer.shape[1]
    cols = pl.program_id(0) * width + lax.broadcasted_iota(jnp.int32, answer.shape, 1)
    out_ref[...] = jnp.where(cols < count_ref[0], answer, 0.0)


def leaf_last(count, part, border, high, low):
    width = 256
    return pl.pallas_call(
        leaf_last_kernel,
        out_shape=jax.ShapeDtypeStruct((256, 1024), F32),
        grid=(1024 // width,),
        in_specs=[
            full_smem(),
            pl.BlockSpec((256, width), lambda i: (0, i)),
            pl.BlockSpec((256, 512), lambda i: (0, 0)),
            pl.BlockSpec((512, width), lambda i: (0, i)),
            pl.BlockSpec((512, width), lambda i: (0, i)),
        ],
        out_specs=pl.BlockSpec((256, width), lambda i: (0, i)),
        compiler_params=params(12),
        name="leaf_last",
    )(count, part, border, high, low)


def pick(values, index_row):
    out = []
    for block in range(index_row.shape[1] // LANES):
        index = jnp.broadcast_to(index_row[:, block * LANES : (block + 1) * LANES], (16, LANES))
        lane, source = index & (LANES - 1), index >> 7
        total = jnp.zeros((16, LANES), F32)
        for at, value in enumerate(values):
            taken = jnp.take_along_axis(value, lane, axis=1)
            total = jnp.where(source == at, taken, total)
        out.append(total)
    return out


def blocks(value):
    return [value[:, at * LANES : (at + 1) * LANES] for at in range(value.shape[1] // LANES)]


def spread_kernel(parent_ref, incoming_ref, slot_ref, updates_ref):
    updates_ref[...] = jnp.zeros(updates_ref.shape, F32)

    def spread(leaf, _):
        to = parent_ref[leaf]
        picked = pick(blocks(incoming_ref[leaf]), slot_ref[leaf])
        for at, value in enumerate(picked):
            part = slice(at * LANES, (at + 1) * LANES)
            updates_ref[to, :, part] = updates_ref[to, :, part] + value
        return 0

    lax.fori_loop(0, 16, spread, 0)


def spread_updates(parent, incoming, slots):
    return pl.pallas_call(
        spread_kernel,
        out_shape=jax.ShapeDtypeStruct((4, 16, 1024), F32),
        in_specs=[full_smem(), full_vmem(), full_vmem()],
        out_specs=full_vmem(),
        compiler_params=params(8),
        name="spread_updates",
    )(parent, incoming, slots)


def lower_unit(value, row_ids, col_ids):
    return jnp.where(col_ids == row_ids, 1.0, jnp.where(col_ids < row_ids, value, 0.0))


def upper_kernel(
    place_ref, parent_ref, updates_ref, index_ref, sep_rhs_ref, sep_slot_ref, sep_index_ref, root_rhs_ref,
    own_ref, other_ref,
    down_ref, sep_out_ref, root_out_ref,
    solved, full, sep_buffer, root_buffer, high_ref, low_ref, sem,
):
    c = place_ref[0]
    loads = []
    for sep in range(4):
        rows = pl.ds(96 + 32 * sep, 32)
        loads.append([
            pltpu.make_async_copy(ref.at[:, rows, :], sep_buffer.at[sep, :, parity], sem.at[2 * sep + at])
            for at, (ref, parity) in enumerate(((own_ref, c), (other_ref, 1 - c)))
        ])
    loads.append([
        pltpu.make_async_copy(ref.at[:, pl.ds(224, 16), :], root_buffer.at[:, parity], sem.at[8 + at])
        for at, (ref, parity) in enumerate(((own_ref, c), (other_ref, 1 - c)))
    ])
    for pair in loads:
        for load in pair:
            load.start()
    row_ids = lax.broadcasted_iota(jnp.int32, (512, 512), 0)
    col_ids = lax.broadcasted_iota(jnp.int32, (512, 512), 1)
    root_total = root_rhs_ref[...]
    for sep in range(4):
        for load in loads[sep]:
            load.wait()
        top = lower_unit(sep_buffer[sep, :8].reshape(512, 512), row_ids, col_ids)
        high_ref[sep, :512], low_ref[sep, :512] = split2(top)
        high_ref[sep, 512:], low_ref[sep, 512:] = split2(sep_buffer[sep, 8:].reshape(512, 512))
        pivot = split2(sep_rhs_ref[sep] + updates_ref[sep, :, :512])
        forward = stacked_products(dot_nt, pivot, (high_ref[sep], low_ref[sep]))
        solved[sep] = forward[:, :512]
        border = forward[:, 512:] + updates_ref[sep, :, 512:]
        root_total = root_total + jnp.concatenate(pick(blocks(border), sep_slot_ref[sep]), axis=1)
    for load in loads[4]:
        load.wait()
    root = split2(lower_unit(root_buffer[...].reshape(512, 512), row_ids, col_ids))
    root_solved = stacked_products(dot_nt, split2(root_total), root)
    root_answer = stacked_products(dot_nn, split2(root_solved), root)
    root_out_ref[...] = root_answer
    for sep in range(4):
        border = jnp.concatenate(pick(blocks(root_answer), sep_index_ref[sep]), axis=1)
        joined = split2(jnp.concatenate([solved[sep], border], axis=1))
        answer = stacked_products(dot_nn, joined, (high_ref[sep], low_ref[sep]))
        sep_out_ref[sep] = answer
        full[sep, :, :512] = answer
        full[sep, :, 512:] = border

    def gather(leaf, _):
        picked = pick(blocks(full[parent_ref[leaf]]), index_ref[leaf])
        down_ref[leaf] = jnp.concatenate(picked, axis=1)
        return 0

    lax.fori_loop(0, 16, gather, 0)


def upper_solve(place, parent, updates, index, sep_rhs, sep_slots, sep_index, root_rhs, own, other):
    return pl.pallas_call(
        upper_kernel,
        out_shape=(
            jax.ShapeDtypeStruct((16, 16, 512), F32),
            jax.ShapeDtypeStruct((4, 16, 512), F32),
            jax.ShapeDtypeStruct((16, 512), F32),
        ),
        in_specs=[full_smem()] * 2 + [full_vmem()] * 6 + [anywhere()] * 2,
        out_specs=(full_vmem(),) * 3,
        scratch_shapes=[
            pltpu.VMEM((4, 16, 512), F32),
            pltpu.VMEM((4, 16, 1024), F32),
            pltpu.VMEM((4, NZ, NC, 32, 512), F32),
            pltpu.VMEM((NZ, NC, 16, 512), F32),
            pltpu.VMEM((4, 1024, 512), BF16),
            pltpu.VMEM((4, 1024, 512), BF16),
            pltpu.SemaphoreType.DMA((10,)),
        ],
        compiler_params=params(28),
        name="upper_solve",
    )(place, parent, updates, index, sep_rhs, sep_slots, sep_index, root_rhs, own, other)


def inverse_rows(index, extent):
    place = jnp.arange(index.shape[1], dtype=jnp.int32)[None, :, None]
    slot = jnp.arange(extent, dtype=jnp.int32)[None, None, :]
    return jnp.max(jnp.where(index[:, :, None] == slot, place, -1), axis=1)


def swap_cores(value):
    return lax.ppermute(value, "c", [(0, 1), (1, 0)])


def local(
    leaf_rhs,
    leaf_factor,
    pivot_count,
    parent,
    leaf_index,
    separator_rhs,
    separator_factor,
    separator_index,
    root_rhs,
    root_factor,
):
    place = lax.axis_index("c").astype(jnp.int32)[None]
    rhs = leaf_rhs[0]
    slots = inverse_rows(leaf_index, 1024)[:, None, :]
    sep_slots = inverse_rows(separator_index, 512)[:, None, :]
    sep_rhs = jnp.transpose(separator_rhs[0], (1, 0, 2))
    shard = jnp.concatenate(
        [leaf_factor[0, :, :512], leaf_factor[0, :, 512:], separator_factor.reshape(128, 512), root_factor],
        axis=0,
    )
    line = lax.all_gather(shard, "z", axis=0, tiled=False)
    line, slots, sep_slots, sep_rhs = lax.optimization_barrier((line, slots, sep_slots, sep_rhs))
    own_border = line[10:, :96]
    other_border = swap_cores(own_border)
    line, own_border, other_border = lax.optimization_barrier((line, own_border, other_border))
    other_line = swap_cores(line)

    border = leaf_border(place, pivot_count, rhs, own_border, other_border)
    incoming = lax.all_to_all(
        border.reshape(16, 16, 512), ("y", "x"), split_axis=0, concat_axis=0, tiled=True
    )
    part, high, low = leaf_pivot(place, pivot_count, rhs, line, other_line)
    updates = spread_updates(parent, incoming, slots)
    down, sep_answer, root_answer = upper_solve(
        place, parent, updates, leaf_index[:, None, :], sep_rhs, sep_slots,
        separator_index[:, None, :], root_rhs[0], line, other_line,
    )
    received = lax.all_to_all(down, ("y", "x"), split_axis=0, concat_axis=0, tiled=True)
    leaf_answer = leaf_last(pivot_count, part, received.reshape(256, 512), high, low)
    return leaf_answer[None], jnp.transpose(sep_answer, (1, 0, 2))[None], root_answer[None]


def solution(mesh):
    fine = Mesh(mesh.devices.reshape(NY, NX, NZ, NC), ("y", "x", "z", "c"))
    leaf, src = ("y", "x"), ("z", "c")
    return jax.shard_map(
        local,
        mesh=fine,
        in_specs=(
            P(leaf, src, None),
            P(leaf, src, None),
            P(leaf),
            P(),
            P(),
            P(leaf, src, None, None),
            P(None, src, None),
            P(),
            P(leaf, src, None),
            P(src, None),
        ),
        out_specs=(P(leaf, src, None), P(leaf, src, None, None), P(leaf, src, None)),
        check_vma=False,
    )
```

time: 331 us -> 193 us (0.58)
  other arithmetic: 63.9 us -> 10 us
  matrix products: 43.6 us -> 0 us
  local copies, waits for them, and re-layouts: 59.7 us -> 16.2 us
  Pallas kernels: 0 us -> 25.1 us
  waiting for transfers between devices: 135 us -> 111 us
    scatter-add x2 -> x0, other arithmetic: 57.8 us -> none  [the longest x1 45.7 us: local(): updates = jnp.zeros((block_cols, separators * sep_height), jnp.float32).a...]
    dot_general x6 -> x0, matrix products: 43.6 us -> none  [the longest x2 13.9 us: against_rows(): lax.dot_general(left_side, matrix, (((1,), (1,)), ((), ())), precision=la...]
    gather x3 -> x0, local copies, waits for them, and re-layouts: 37 us -> none  [the longest x1 27.8 us: local(): sep_full.reshape(block_cols, separators * sep_height)[:, targets]]
    pallas_call x0 -> x5, Pallas kernels: none -> 25.1 us  [the longest x1 11.1 us: upper_solve(): pl.pallas_call(upper_kernel, out_shape=(jax.ShapeDtypeStruct((16, 16, 512...]
    all_gather x3 -> x1, waiting for transfers between devices: 112 us -> 97.4 us  [local(): line = lax.all_gather(shard, 'z', axis=0, tiled=False)]
    all_to_all x2, waiting for transfers between devices: 20.8 us -> 10.9 us  [the longest x1 10.9 us: local(): lax.all_to_all(border.reshape(16, 16, 512), ('y', 'x'), split_axis=0, con...]
    reduce_max x0 -> x2, other arithmetic: none -> 8.21 us  [inverse_rows(): return jnp.max(jnp.where(index[:, :, None] == slot, place, -1), axis=1)]
    reshape x4 -> x0, local copies, waits for them, and re-layouts: 7.93 us -> none  [the longest x1 3.5 us: local(): picked_down.reshape(block_cols, leaves, border_rows)]
  transfers between devices with their start and end apart: 5 -> 5, of which waited for: 4 -> 3; matrix products, arithmetic and copies ran while one was open for 30% -> 5% of each run, Pallas kernels for 0% -> 6%
where the time goes in v1:
time: 193 us; the launch traced here: 192 us
  waiting for transfers between devices  111 us (58%)
  Pallas kernels  25.1 us (13%)
  local copies, waits for them, and re-layouts  16.2 us (8%)
  starting transfers between devices  15 us (8%)
  between operations  14.9 us (8%)
  other arithmetic  10 us (5%)
    all_gather x1, waiting for transfers between devices, local(): line = lax.all_gather(shard, 'z', axis=0, tiled=False)  97.4 us
    unnamed x26, local copies, waits for them, and re-layouts  13.8 us
    pallas_call x1, Pallas kernels, upper_solve(): pl.pallas_call(upper_kernel, out_shape=(jax.ShapeDtypeStruct((16, 16, 512...  11.1 us
    all_to_all x1, waiting for transfers between devices, local(): lax.all_to_all(border.reshape(16, 16, 512), ('y', 'x'), split_axis=0, con...  10.9 us
    reduce_max x2, other arithmetic, inverse_rows(): return jnp.max(jnp.where(index[:, :, None] == slot, place, -1), axis=1)  8.21 us
    all_to_all x1, starting transfers between devices, local(): lax.all_to_all(border.reshape(16, 16, 512), ('y', 'x'), split_axis=0, con...  6.55 us
    pallas_call x1, Pallas kernels, leaf_pivot(): pl.pallas_call(leaf_pivot_kernel, out_shape=(jax.ShapeDtypeStruct((256, 1...  5.04 us
    ppermute x2, starting transfers between devices, swap_cores(): return lax.ppermute(value, 'c', [(0, 1), (1, 0)])  4.85 us
  transfers between devices with their start and end apart: 5, of which 3 were waited for; matrix products, arithmetic and copies ran while one was open for 5% of the time, Pallas kernels for 6%

profile of v1, /device:TPU:1, one launch (start us, length us, event | category | flops | bytes accessed | tf_op | source)
XLA Modules:
  0.0 192.0 jit_solution(517777990961208534)
XLA Ops:
  7.2 0.0 copy-start.11
  7.2 0.0 copy-start.10
  7.2 0.0 copy-start.9
  7.2 0.0 copy-start.8
  7.2 0.0 all-gather.3.cloned.1.call-start
  7.3 1.0 slice_bitcast_fusion.1
  8.2 1.8 pad_maximum_fusion
  10.0 0.0 all-gather.3.cloned.1.call-update
  10.0 1.4 select_reduce_fusion.1
  11.5 6.8 %select_reduce_fusion = s32[16,1024]{1,0:T(8,128)S(1)} fusion(s32[16,512]{1,0:T(8,128)} %param.14), kind=kLoop, calls=%fused_computation | loop fusion | flops 25149440 | bytes 98304 | tf_op jit(solution)/shard_map/reduce_max | solution.py:316
  18.3 1.0 copy.18
  19.3 97.4 %all-gather.3.cloned.1.call-done = f32[3840,512]{1,0:T(8,128)} async-done(((f32[240,512]{1,0:T(8,128)}), f32[3840,512]{1,0:T(8,128)}) %all-gather.3.cloned.1.call-update) | async-done | bytes 7864336 | tf_op jit(solution)/shard_map/all_gather | solution.py:344
  116.7 1.4 slice.11.own_ref
  118.1 2.6 %collective-permute-start = (f32[6,96,512]{2,1,0:T(8,128)S(1)}, f32[6,96,512]{2,1,0:T(8,128)S(1)}, u32[]{:S(2)}, u32[]{:S(2)}) collective-permute-start(f32[6,96,512]{2,1,0:T(8,128)S(1)} %slice.11.own_ref), channel_id=1, source_target_pairs={{0,1},{1,0},{2,3},{3,2},{4,5},{5,4},{6,7},{7,6},{8,9},{9,8},{10,11... | collective-permute-start | bytes 3538952 | tf_op jit(solution)/shard_map/ppermute | solution.py:320
  120.7 2.5 %collective-permute-done.other_ref = f32[6,96,512]{2,1,0:T(8,128)S(1)} collective-permute-done((f32[6,96,512]{2,1,0:T(8,128)S(1)}, f32[6,96,512]{2,1,0:T(8,128)S(1)}, u32[]{:S(2)}, u32[]{:S(2)}) %collective-permute-start) | collective-permute-done | bytes 1179680 | tf_op jit(solution)/shard_map/ppermute | solution.py:320
  123.1 2.3 %collective-permute-start.1 = (f32[16,240,512]{2,1,0:T(8,128)}, f32[16,240,512]{2,1,0:T(8,128)}, u32[]{:S(2)}, u32[]{:S(2)}) collective-permute-start(f32[16,240,512]{2,1,0:T(8,128)} %bitcast.22), channel_id=1, source_target_pairs={{0,1},{1,0},{2,3},{3,2},{4,5},{5,4},{6,7},{7,6},{8,9},{9,8},{10,11... | collective-permute-start | bytes 23592968 | tf_op jit(solution)/shard_map/ppermute | solution.py:320
  126.0 0.0 copy-start.2
  126.1 1.2 copy-done.2
  127.3 2.6 %leaf_border.1 = f32[256,512]{1,0:T(8,128)} custom-call(s32[1]{0:T(128)} %bitcast.place_ref, s32[1]{0:T(128)S(6)} %copy.19.count_ref, f32[256,1024]{1,0:T(8,128)S(1)} %bitcast.25, f32[6,96,512]{2,1,0:T(8,128)S(1)} %slice.11.own_ref, f32[6,96,512]{2,1,0:T(8,128)S(1)} %collective-permute-done.other_ref), custom_call_target="tpu_custom_call" | custom-call | tf_op jit(solution)/shard_map/leaf_border/pallas_call | solution.py:88
  129.9 6.5 %all-to-all-start = ((f32[16,16,512]{2,1,0:T(8,128)}), f32[16,16,512]{2,1,0:T(8,128)S(1)}, u32[]{:S(2)}, u32[]{:S(2)}) async-start(f32[16,16,512]{2,1,0:T(8,128)} %bitcast.8), calls=%async_computation | async-start | bytes 1048576 | tf_op jit(solution)/shard_map/all_to_all | solution.py:352
  136.5 0.0 copy-done.11
  136.5 0.0 copy-done.10
  136.5 10.9 %all-to-all-done.incoming_ref = f32[16,16,512]{2,1,0:T(8,128)S(1)} async-done(((f32[16,16,512]{2,1,0:T(8,128)}), f32[16,16,512]{2,1,0:T(8,128)S(1)}, u32[]{:S(2)}, u32[]{:S(2)}) %all-to-all-start) | async-done | bytes 524320 | tf_op jit(solution)/shard_map/all_to_all | solution.py:352
  147.4 0.0 copy-done.9
  147.4 3.4 %spread_updates.1.updates_ref = f32[4,16,1024]{2,1,0:T(8,128)S(1)} custom-call(s32[16]{0:T(128)S(1)} %copy-done.9, f32[16,16,512]{2,1,0:T(8,128)S(1)} %all-to-all-done.incoming_ref, s32[16,1,1024]{2,1,0:T(1,128)S(1)} %broadcast_in_dim.57.slot_ref), custom_call_target="tpu_custom_call" | custom-call | tf_op jit(solution)/shard_map/spread_updates/pallas_call | solution.py:218
  150.8 0.0 collective-permute-done.1.other_ref
  150.8 0.0 copy-done.8
  150.9 0.0 copy-start
  150.9 3.2 %copy-done = f32[3840,512]{1,0:T(8,128)S(1)} copy-done((f32[3840,512]{1,0:T(8,128)S(1)}, f32[3840,512]{1,0:T(8,128)}, u32[]{:S(2)}) %copy-start) | copy-done | bytes 7864344
  154.1 0.0 copy-start.3
  154.1 11.1 %upper_solve.1 = (f32[16,16,512]{2,1,0:T(8,128)}, f32[4,16,512]{2,1,0:T(8,128)S(1)}, f32[16,512]{1,0:T(8,128)}) custom-call(s32[1]{0:T(128)} %bitcast.place_ref, s32[16]{0:T(128)S(1)} %copy-done.9, f32[4,16,1024]{2,1,0:T(8,128)S(1)} %spread_updates.1.updates_ref, s32[16,1,512]{2,1,0:T(1,128)S(1)} %broadcast_in_dim.61.index_ref, f32[4,16,512]{2,1,0:T(8,128)S(1)} %bitcast.28, ...), custom_call_target="tpu_custom_call" | custom-call | tf_op jit(solution)/shard_map/upper_solve/pallas_call | solution.py:290
  165.2 3.6 %all-to-all-start.1 = ((f32[16,16,512]{2,1,0:T(8,128)}), f32[16,16,512]{2,1,0:T(8,128)S(1)}, u32[]{:S(2)}, u32[]{:S(2)}) async-start(f32[16,16,512]{2,1,0:T(8,128)} %get-tuple-element.24), calls=%async_computation.1 | async-start | bytes 1048576 | tf_op jit(solution)/shard_map/all_to_all | solution.py:361
  168.8 0.7 copy.16
  169.6 0.0 copy-done.3
  169.6 0.0 copy-start.1
  169.6 3.2 %copy-done.1 = f32[3840,512]{1,0:T(8,128)S(1)} copy-done((f32[3840,512]{1,0:T(8,128)S(1)}, f32[3840,512]{1,0:T(8,128)}, u32[]{:S(2)}) %copy-start.1) | copy-done | bytes 7864344
  172.8 5.0 %leaf_pivot.1 = (f32[256,1024]{1,0:T(8,128)S(1)}, bf16[512,1024]{1,0:T(8,128)(2,1)S(1)}, bf16[512,1024]{1,0:T(8,128)(2,1)S(1)}) custom-call(s32[1]{0:T(128)} %bitcast.place_ref, s32[1]{0:T(128)S(6)} %copy.19.count_ref, f32[256,1024]{1,0:T(8,128)S(1)} %bitcast.26, f32[16,240,512]{2,1,0:T(8,128)S(1)} %bitcast.24, f32[16,240,512]{2,1,0:T(8,128)} %collective-permute-done.1.other_ref), custom_call_target="tpu_custom_call" | custom-call | tf_op jit(solution)/shard_map/leaf_pivot/pallas_call | solution.py:138
  177.9 0.0 copy-start.4
  177.9 1.0 copy-done.4
  178.8 0.0 copy-start.6
  178.8 1.0 copy-done.6
  179.8 0.0 all-to-all-done.1
  179.8 0.0 copy-start.5
  179.8 1.2 copy-done.5
  181.0 0.0 copy-start.7
  181.0 1.2 copy-done.7
  182.3 2.9 %leaf_last.1 = f32[256,1024]{1,0:T(8,128)} custom-call(s32[1]{0:T(128)S(6)} %copy.19.count_ref, f32[256,1024]{1,0:T(8,128)S(1)} %get-tuple-element.18.part_ref, f32[256,512]{1,0:T(8,128)S(1)} %bitcast.27, bf16[512,1024]{1,0:T(8,128)(2,1)S(1)} %copy-done.5, bf16[512,1024]{1,0:T(8,128)(2,1)S(1)} %copy-done.7), custom_call_target="tpu_custom_call" | custom-call | tf_op jit(solution)/shard_map/leaf_last/pallas_call | solution.py:169
  (4 shorter events, 0.1 us)
Async XLA Ops:
  7.2 129.3 %copy-start.11 = (s32[4,512]{1,0:T(4,128)S(1)}, s32[4,512]{1,0:T(4,128)}, u32[]{:S(2)}) copy-start(s32[4,512]{1,0:T(4,128)} %param.17) | copy-start | bytes 24580
  7.2 129.3 %copy-start.10 = (s32[16,512]{1,0:T(8,128)S(1)}, s32[16,512]{1,0:T(8,128)}, u32[]{:S(2)}) copy-start(s32[16,512]{1,0:T(8,128)} %param.14) | copy-start | bytes 98308
  7.2 140.2 %copy-start.9 = (s32[16]{0:T(128)S(1)}, s32[16]{0:T(128)}, u32[]{:S(2)}) copy-start(s32[16]{0:T(128)} %parent_ref.3) | copy-start | bytes 196
  7.2 143.7 %copy-start.8 = (f32[1,16,512]{2,1,0:T(8,128)S(1)}, f32[1,16,512]{2,1,0:T(8,128)}, u32[]{:S(2)}) copy-start(f32[1,16,512]{2,1,0:T(8,128)} %param.18) | copy-start | bytes 98308
  7.2 109.5 %all-gather.3.cloned.1.call-start = ((), (), s32[]{:S(2)}) async-start(), calls=%async_computation.2 | async-start | bytes 8355840 | tf_op jit(solution)/shard_map/all_gather | solution.py:344
  118.1 5.0 %collective-permute-start = (f32[6,96,512]{2,1,0:T(8,128)S(1)}, f32[6,96,512]{2,1,0:T(8,128)S(1)}, u32[]{:S(2)}, u32[]{:S(2)}) collective-permute-start(f32[6,96,512]{2,1,0:T(8,128)S(1)} %slice.11.own_ref), channel_id=1, source_target_pairs={{0,1},{1,0},{2,3},{3,2},{4,5},{5,4},{6,7},{7,6},{8,9},{9,8},{10,11... | collective-permute-start | bytes 3538952 | tf_op jit(solution)/shard_map/ppermute | solution.py:320
  123.1 27.7 %collective-permute-start.1 = (f32[16,240,512]{2,1,0:T(8,128)}, f32[16,240,512]{2,1,0:T(8,128)}, u32[]{:S(2)}, u32[]{:S(2)}) collective-permute-start(f32[16,240,512]{2,1,0:T(8,128)} %bitcast.22), channel_id=1, source_target_pairs={{0,1},{1,0},{2,3},{3,2},{4,5},{5,4},{6,7},{7,6},{8,9},{9,8},{10,11... | collective-permute-start | bytes 23592968 | tf_op jit(solution)/shard_map/ppermute | solution.py:320
  126.0 1.2 copy-start.2
  129.9 17.5 %all-to-all-start = ((f32[16,16,512]{2,1,0:T(8,128)}), f32[16,16,512]{2,1,0:T(8,128)S(1)}, u32[]{:S(2)}, u32[]{:S(2)}) async-start(f32[16,16,512]{2,1,0:T(8,128)} %bitcast.8), calls=%async_computation | async-start | bytes 1048576 | tf_op jit(solution)/shard_map/all_to_all | solution.py:352
  150.9 3.2 %copy-start = (f32[3840,512]{1,0:T(8,128)S(1)}, f32[3840,512]{1,0:T(8,128)}, u32[]{:S(2)}) copy-start(f32[3840,512]{1,0:T(8,128)} %all-gather.3.cloned.1.call-done) | copy-start | bytes 23592964
  154.1 15.5 %copy-start.3 = (f32[1,256,1024]{2,1,0:T(8,128)S(1)}, f32[1,256,1024]{2,1,0:T(8,128)}, u32[]{:S(2)}) copy-start(f32[1,256,1024]{2,1,0:T(8,128)} %param.10) | copy-start | bytes 3145732
  165.2 14.6 %all-to-all-start.1 = ((f32[16,16,512]{2,1,0:T(8,128)}), f32[16,16,512]{2,1,0:T(8,128)S(1)}, u32[]{:S(2)}, u32[]{:S(2)}) async-start(f32[16,16,512]{2,1,0:T(8,128)} %get-tuple-element.24), calls=%async_computation.1 | async-start | bytes 1048576 | tf_op jit(solution)/shard_map/all_to_all | solution.py:361
  169.6 3.2 %copy-start.1 = (f32[3840,512]{1,0:T(8,128)S(1)}, f32[3840,512]{1,0:T(8,128)}, u32[]{:S(2)}) copy-start(f32[3840,512]{1,0:T(8,128)} %all-gather.3.cloned.1.call-done) | copy-start | bytes 23592964
  177.9 1.0 copy-start.4
  178.8 1.0 copy-start.6
  179.8 1.2 copy-start.5
  181.0 1.2 copy-start.7
Sparse Core Ops, SparseCore 0:
  10.7 105.9 all-gather.2

commit v2 on v1

v2 whole, which is shorter than its diff:
```python
import jax
import jax.numpy as jnp
from jax import lax
from jax.experimental import pallas as pl
from jax.experimental.pallas import tpu as pltpu
from jax.sharding import Mesh, PartitionSpec as P

NY, NX, NZ, NC = 4, 4, 16, 2
F32, BF16 = jnp.float32, jnp.bfloat16
LANES = 128


def split2(value):
    high = value.astype(BF16)
    return high, (value - high.astype(F32)).astype(BF16)


def dot_nt(a, b):
    return lax.dot_general(a, b, (((1,), (1,)), ((), ())), preferred_element_type=F32)


def dot_nn(a, b):
    return lax.dot_general(a, b, (((1,), (0,)), ((), ())), preferred_element_type=F32)


def three_products(dot, a, b):
    return dot(a[0], b[0]) + (dot(a[1], b[0]) + dot(a[0], b[1]))


def stacked_products(dot, a, b):
    rows = a[0].shape[0]
    both = dot(jnp.concatenate([a[0], a[1]], axis=0), b[0])
    return both[:rows] + (both[rows:] + dot(a[0], b[1]))


def params(mebibytes):
    return pltpu.CompilerParams(vmem_limit_bytes=mebibytes * 1024 * 1024)


def full_vmem():
    return pl.BlockSpec(memory_space=pltpu.VMEM)


def full_smem():
    return pl.BlockSpec(memory_space=pltpu.SMEM)


def in_hbm():
    return pl.BlockSpec(memory_space=pltpu.HBM)


def anywhere():
    return pl.BlockSpec(memory_space=pl.ANY)


def start_all(copies):
    for copy in copies:
        copy.start()


def wait_all(copies):
    for copy in copies:
        copy.wait()


LEAF_ROWS, SHARD = 48, 56


def join_kernel(leaf_ref, root_ref, out_ref):
    out_ref[:LEAF_ROWS] = leaf_ref[...]
    out_ref[LEAF_ROWS:, :512] = root_ref[:8]
    out_ref[LEAF_ROWS:, 512:] = root_ref[8:]


def join(leaf, root):
    return pl.pallas_call(
        join_kernel,
        out_shape=jax.ShapeDtypeStruct((SHARD, 1024), F32),
        in_specs=[full_vmem()] * 2,
        out_specs=full_vmem(),
        compiler_params=params(60),
        name="join",
    )(leaf, root)


def leaf_copy(line_ref, buffer, first, count, sem):
    return pltpu.make_async_copy(line_ref.at[pl.ds(first, count), pl.ds(0, LEAF_ROWS), :], buffer, sem)


def leaf_border_kernel(count_ref, rhs_hbm, line_ref, border_ref, rhs_ref, buffer, sem, rhs_sem):
    copy = leaf_copy(line_ref, buffer, 21, 11, sem)
    load = pltpu.make_async_copy(rhs_hbm, rhs_ref, rhs_sem)
    load.start()
    copy.start()
    load.wait()
    cols = lax.broadcasted_iota(jnp.int32, rhs_ref.shape, 1)
    rhs = split2(jnp.where(cols < count_ref[0], rhs_ref[...], 0.0))
    copy.wait()
    rows = buffer[...].reshape(528, 1024)
    for block in range(2):
        first = 16 + 256 * block
        border_ref[:, 256 * block : 256 * (block + 1)] = three_products(
            dot_nt, rhs, split2(rows[first : first + 256])
        )


def leaf_border(count, rhs, line):
    return pl.pallas_call(
        leaf_border_kernel,
        out_shape=jax.ShapeDtypeStruct((256, 512), F32),
        in_specs=[full_smem(), in_hbm(), in_hbm()],
        out_specs=full_vmem(),
        scratch_shapes=[
            pltpu.VMEM((256, 1024), F32),
            pltpu.VMEM((11, 48, 1024), F32),
            pltpu.SemaphoreType.DMA,
            pltpu.SemaphoreType.DMA,
        ],
        compiler_params=params(60),
        name="leaf_border",
    )(count, rhs, line)


def leaf_pivot_kernel(
    count_ref, rhs_hbm, line_ref,
    part_hbm, border_high_hbm, border_low_hbm,
    rhs_ref, buffer, border_buffer, high_ref, low_ref, part_ref, border_high_ref, border_low_ref, sem, out_sem,
):
    copy = leaf_copy(line_ref, buffer, 0, 22, sem.at[0])
    border_copy = leaf_copy(line_ref, border_buffer, 21, 11, sem.at[1])
    load = pltpu.make_async_copy(rhs_hbm, rhs_ref, sem.at[2])
    load.start()
    copy.start()
    border_copy.start()
    count = count_ref[0]
    load.wait()
    cols = lax.broadcasted_iota(jnp.int32, rhs_ref.shape, 1)
    rhs = split2(jnp.where(cols < count, rhs_ref[...], 0.0))
    copy.wait()
    top = buffer[...].reshape(1056, 1024)
    solved = []
    for block in range(4):
        first, wide = 256 * block, 256 * (block + 1)
        rows = first + lax.broadcasted_iota(jnp.int32, (256, wide), 0)
        columns = lax.broadcasted_iota(jnp.int32, (256, wide), 1)
        values = jnp.where(columns < rows, top[first:wide, :wide], 0.0)
        values = jnp.where(columns == rows, 1.0, values)
        values = jnp.where(rows < count, values, 0.0)
        high, low = split2(values)
        high_ref[first:wide, :wide] = high
        low_ref[first:wide, :wide] = low
        solved.append(three_products(dot_nt, (rhs[0][:, :wide], rhs[1][:, :wide]), (high, low)))
    solved = split2(jnp.concatenate(solved, axis=1))
    border_copy.wait()
    border = border_buffer[...].reshape(528, 1024)
    stores = []
    for block in range(4):
        first, wide = 256 * block, 256 * (block + 1)
        border_high_ref[block], border_low_ref[block] = split2(border[16:, first:wide])
        part_ref[block] = three_products(
            dot_nn,
            (solved[0][:, first:], solved[1][:, first:]),
            (high_ref[first:, first:wide], low_ref[first:, first:wide]),
        )
        stores += [
            pltpu.make_async_copy(part_ref.at[block], part_hbm.at[block], out_sem.at[block, 0]),
            pltpu.make_async_copy(border_high_ref.at[block], border_high_hbm.at[block], out_sem.at[block, 1]),
            pltpu.make_async_copy(border_low_ref.at[block], border_low_hbm.at[block], out_sem.at[block, 2]),
        ]
        start_all(stores[-3:])
    wait_all(stores)


def leaf_pivot(count, rhs, line):
    return pl.pallas_call(
        leaf_pivot_kernel,
        out_shape=(
            jax.ShapeDtypeStruct((4, 256, 256), F32),
            jax.ShapeDtypeStruct((4, 512, 256), BF16),
            jax.ShapeDtypeStruct((4, 512, 256), BF16),
        ),
        in_specs=[full_smem(), in_hbm(), in_hbm()],
        out_specs=(in_hbm(),) * 3,
        scratch_shapes=[
            pltpu.VMEM((256, 1024), F32),
            pltpu.VMEM((22, 48, 1024), F32),
            pltpu.VMEM((11, 48, 1024), F32),
            pltpu.VMEM((1024, 1024), BF16),
            pltpu.VMEM((1024, 1024), BF16),
            pltpu.VMEM((4, 256, 256), F32),
            pltpu.VMEM((4, 512, 256), BF16),
            pltpu.VMEM((4, 512, 256), BF16),
            pltpu.SemaphoreType.DMA((3,)),
            pltpu.SemaphoreType.DMA((4, 3)),
        ],
        compiler_params=params(60),
        name="leaf_pivot",
    )(count, rhs, line)


def leaf_last_kernel(
    count_ref, part_hbm, border_ref, high_hbm, low_hbm, out_hbm,
    part_ref, high_ref, low_ref, out_ref, sem, out_sem,
):
    copies = [
        [
            pltpu.make_async_copy(source.at[block], to.at[block], sem.at[block, at])
            for at, (source, to) in enumerate(((high_hbm, high_ref), (low_hbm, low_ref), (part_hbm, part_ref)))
        ]
        for block in range(4)
    ]
    for group in copies:
        start_all(group)
    border = split2(border_ref[...])
    stores = []
    for block in range(4):
        wait_all(copies[block])
        answer = part_ref[block] + three_products(dot_nn, border, (high_ref[block], low_ref[block]))
        cols = 256 * block + lax.broadcasted_iota(jnp.int32, answer.shape, 1)
        out_ref[block] = jnp.where(cols < count_ref[0], answer, 0.0)
        stores.append(
            pltpu.make_async_copy(out_ref.at[block], out_hbm.at[:, pl.ds(256 * block, 256)], out_sem.at[block])
        )
        stores[-1].start()
    wait_all(stores)


def leaf_last(count, part, border, high, low):
    return pl.pallas_call(
        leaf_last_kernel,
        out_shape=jax.ShapeDtypeStruct((256, 1024), F32),
        in_specs=[full_smem(), in_hbm(), full_vmem(), in_hbm(), in_hbm()],
        out_specs=in_hbm(),
        scratch_shapes=[
            pltpu.VMEM((4, 256, 256), F32),
            pltpu.VMEM((4, 512, 256), BF16),
            pltpu.VMEM((4, 512, 256), BF16),
            pltpu.VMEM((4, 256, 256), F32),
            pltpu.SemaphoreType.DMA((4, 3)),
            pltpu.SemaphoreType.DMA((4,)),
        ],
        compiler_params=params(60),
        name="leaf_last",
    )(count, part, border, high, low)


def pick(values, index_row):
    out = []
    for block in range(index_row.shape[1] // LANES):
        index = jnp.broadcast_to(index_row[:, block * LANES : (block + 1) * LANES], (16, LANES))
        lane, source = index & (LANES - 1), index >> 7
        total = jnp.zeros((16, LANES), F32)
        for at, value in enumerate(values):
            taken = jnp.take_along_axis(value, lane, axis=1)
            total = jnp.where(source == at, taken, total)
        out.append(total)
    return out


def blocks(value):
    return [value[:, at * LANES : (at + 1) * LANES] for at in range(value.shape[1] // LANES)]


OFFSETS = (0, -1, 1, -2)


def upper_operator_kernel(place_ref, *refs):
    own_refs, other_refs, line_ref = refs[:5], refs[5:10], refs[10]
    high_hbm, low_hbm, root_high_hbm, root_low_hbm = refs[11:15]
    buffer, root_buffer, high_ref, low_ref, root_high_ref, root_low_ref, sem, root_sem, out_sem = refs[15:]
    y, x, c = place_ref[0], place_ref[1], place_ref[2]
    for piece_refs, parity in ((own_refs, c), (other_refs, 1 - c)):
        for outer in range(4):
            for inner in range(4):
                if outer < 3:
                    source = piece_refs[outer].at[inner]
                else:
                    source = piece_refs[3 + inner // 2].at[inner % 2]
                along_y = jnp.where(parity == 0, OFFSETS[outer], OFFSETS[inner])
                along_x = jnp.where(parity == 0, OFFSETS[inner], OFFSETS[outer])
                group = jnp.where(parity == 0, outer, inner)
                to_y = lax.rem(y + along_y + 8, 4)
                to_x = lax.rem(x + along_x + 8, 4)
                pltpu.make_async_copy(source, buffer.at[to_y, to_x, parity], sem.at[group]).start()
    root_copies = [
        pltpu.make_async_copy(
            line_ref.at[:, pl.ds(LEAF_ROWS, 8), pl.ds(512 * half, 512)],
            root_buffer.at[:, pl.ds(8 * half, 8), :],
            root_sem.at[half],
        )
        for half in range(2)
    ]
    start_all(root_copies)
    stores = []

    def send(value_ref, to_ref, at):
        stores.append(pltpu.make_async_copy(value_ref, to_ref, out_sem.at[at]))
        stores[-1].start()

    for group in range(4):
        for _ in range(8):
            pltpu.make_async_copy(own_refs[0].at[0], buffer.at[0, 0, 0], sem.at[group]).wait()
        sep = lax.rem(y + OFFSETS[group] + 8, 4)

        def rows(z, parity):
            return jnp.concatenate([buffer[sep, q, parity, z] for q in range(4)], axis=0)

        def pivot_rows(z, _):
            for parity in range(2):
                shard = 2 * z + parity
                row_ids = shard * 32 + lax.broadcasted_iota(jnp.int32, (32, 512), 0)
                col_ids = lax.broadcasted_iota(jnp.int32, (32, 512), 1)
                value = lower_unit(rows(z, parity), row_ids, col_ids)
                to = pl.ds(pl.multiple_of(shard * 32, 32), 32)
                high_ref[sep, to], low_ref[sep, to] = split2(value)
            return 0

        def border_rows(z, _):
            for parity in range(2):
                to = pl.ds(pl.multiple_of((2 * z + parity) * 32, 32), 32)
                high_ref[sep, to], low_ref[sep, to] = split2(rows(z, parity))
            return 0

        lax.fori_loop(0, 8, pivot_rows, 0)
        lax.fori_loop(8, 16, border_rows, 0)
        send(high_ref.at[sep], high_hbm.at[sep], 2 * group)
        send(low_ref.at[sep], low_hbm.at[sep], 2 * group + 1)
    wait_all(root_copies)
    row_ids = lax.broadcasted_iota(jnp.int32, (512, 512), 0)
    col_ids = lax.broadcasted_iota(jnp.int32, (512, 512), 1)
    value = lower_unit(root_buffer[...].reshape(512, 512), row_ids, col_ids)
    root_high_ref[...], root_low_ref[...] = split2(value)
    send(root_high_ref, root_high_hbm, 8)
    send(root_low_ref, root_low_hbm, 9)
    wait_all(stores)


def lower_unit(value, row_ids, col_ids):
    return jnp.where(col_ids == row_ids, 1.0, jnp.where(col_ids < row_ids, value, 0.0))


def upper_operators(place, own, other, line):
    return pl.pallas_call(
        upper_operator_kernel,
        out_shape=(
            jax.ShapeDtypeStruct((4, 1024, 512), BF16),
            jax.ShapeDtypeStruct((4, 1024, 512), BF16),
            jax.ShapeDtypeStruct((512, 512), BF16),
            jax.ShapeDtypeStruct((512, 512), BF16),
        ),
        in_specs=[full_smem()] + [in_hbm()] * 11,
        out_specs=(in_hbm(),) * 4,
        scratch_shapes=[
            pltpu.VMEM((NY, NX, NC, NZ, 8, 512), F32),
            pltpu.VMEM((32, 16, 512), F32),
            pltpu.VMEM((4, 1024, 512), BF16),
            pltpu.VMEM((4, 1024, 512), BF16),
            pltpu.VMEM((512, 512), BF16),
            pltpu.VMEM((512, 512), BF16),
            pltpu.SemaphoreType.DMA((4,)),
            pltpu.SemaphoreType.DMA((2,)),
            pltpu.SemaphoreType.DMA((10,)),
        ],
        compiler_params=params(60),
        name="upper_operators",
    )(place, *own, *other, line)


def upper_kernel(
    parent_ref, incoming_ref, slot_ref, index_ref, sep_rhs_ref, sep_slot_ref, sep_index_ref, root_rhs_ref,
    high_hbm, low_hbm, root_high_hbm, root_low_hbm,
    down_ref, sep_out_ref, root_out_ref,
    updates, solved, full, high_ref, low_ref, root_high_ref, root_low_ref, sem,
):
    loads = []
    for sep in range(4):
        loads.append([
            pltpu.make_async_copy(high_hbm.at[sep], high_ref.at[sep], sem.at[sep, 0]),
            pltpu.make_async_copy(low_hbm.at[sep], low_ref.at[sep], sem.at[sep, 1]),
        ])
    loads.append([
        pltpu.make_async_copy(root_high_hbm, root_high_ref, sem.at[4, 0]),
        pltpu.make_async_copy(root_low_hbm, root_low_ref, sem.at[4, 1]),
    ])
    for group in loads:
        start_all(group)
    updates[...] = jnp.zeros(updates.shape, F32)

    def spread(leaf, _):
        to = parent_ref[leaf]
        picked = pick(blocks(incoming_ref[leaf]), slot_ref[leaf])
        for at, value in enumerate(picked):
            part = slice(at * LANES, (at + 1) * LANES)
            updates[to, :, part] = updates[to, :, part] + value
        return 0

    lax.fori_loop(0, 16, spread, 0, unroll=4)
    root_total = root_rhs_ref[...]
    for sep in range(4):
        wait_all(loads[sep])
        pivot = split2(sep_rhs_ref[sep] + updates[sep, :, :512])
        forward = stacked_products(dot_nt, pivot, (high_ref[sep], low_ref[sep]))
        solved[sep] = forward[:, :512]
        border = forward[:, 512:] + updates[sep, :, 512:]
        root_total = root_total + jnp.concatenate(pick(blocks(border), sep_slot_ref[sep]), axis=1)
    wait_all(loads[4])
    root = (root_high_ref[...], root_low_ref[...])
    root_solved = stacked_products(dot_nt, split2(root_total), root)
    root_answer = stacked_products(dot_nn, split2(root_solved), root)
    root_out_ref[...] = root_answer
    for sep in range(4):
        border = jnp.concatenate(pick(blocks(root_answer), sep_index_ref[sep]), axis=1)
        joined = split2(jnp.concatenate([solved[sep], border], axis=1))
        answer = stacked_products(dot_nn, joined, (high_ref[sep], low_ref[sep]))
        sep_out_ref[sep] = answer
        full[sep, :, :512] = answer
        full[sep, :, 512:] = border

    def gather(leaf, _):
        picked = pick(blocks(full[parent_ref[leaf]]), index_ref[leaf])
        down_ref[leaf] = jnp.concatenate(picked, axis=1)
        return 0

    lax.fori_loop(0, 16, gather, 0, unroll=4)


def upper_solve(parent, incoming, slots, index, sep_rhs, sep_slots, sep_index, root_rhs, operators):
    return pl.pallas_call(
        upper_kernel,
        out_shape=(
            jax.ShapeDtypeStruct((16, 16, 512), F32),
            jax.ShapeDtypeStruct((4, 16, 512), F32),
            jax.ShapeDtypeStruct((16, 512), F32),
        ),
        in_specs=[full_smem()] + [full_vmem()] * 7 + [in_hbm()] * 4,
        out_specs=(full_vmem(),) * 3,
        scratch_shapes=[
            pltpu.VMEM((4, 16, 1024), F32),
            pltpu.VMEM((4, 16, 512), F32),
            pltpu.VMEM((4, 16, 1024), F32),
            pltpu.VMEM((4, 1024, 512), BF16),
            pltpu.VMEM((4, 1024, 512), BF16),
            pltpu.VMEM((512, 512), BF16),
            pltpu.VMEM((512, 512), BF16),
            pltpu.SemaphoreType.DMA((5, 2)),
        ],
        compiler_params=params(60),
        name="upper_solve",
    )(parent, incoming, slots, index, sep_rhs, sep_slots, sep_index, root_rhs, *operators)


def inverse_rows(index, extent):
    place = jnp.arange(index.shape[1], dtype=jnp.int32)[None, :, None]
    slot = jnp.arange(extent, dtype=jnp.int32)[None, None, :]
    return jnp.max(jnp.where(index[:, :, None] == slot, place, -1), axis=1)


def swap_cores(value):
    return lax.ppermute(value, "c", [(0, 1), (1, 0)])


def along_plane(value, step, first):
    pairs = []
    for y in range(NY):
        for x in range(NX):
            for c in range(NC):
                by_x = (c == 0) == first
                to_y, to_x = (y, (x + step) % NX) if by_x else ((y + step) % NY, x)
                pairs.append(((y * NX + x) * NC + c, (to_y * NX + to_x) * NC + c))
    return lax.ppermute(value, ("y", "x", "c"), pairs)


def gather_plane(value, first, beside):
    ahead = along_plane(value, 1, first)
    back = along_plane(value, -1, first)
    ahead, back, beside = lax.optimization_barrier((ahead, back, beside))
    half = value.shape[0] // 2
    far_low = along_plane(ahead[:half], 1, first)
    far_high = along_plane(back[half:], -1, first)
    return (value, ahead, back, far_low, far_high), beside


def gather_line(separator_factor, y, x):
    mine = lax.dynamic_slice(separator_factor, (y, 8 * x, 0), (1, 8, 512))
    return lax.all_to_all(
        jnp.broadcast_to(mine, (NZ, 8, 512)), "z", split_axis=0, concat_axis=0, tiled=True
    )


def spread_line(line, beside):
    rows = jnp.stack([line, along_plane(line, 1, True), along_plane(line, -1, True), along_plane(line, 2, True)])
    return gather_plane(rows, False, beside)


def local(
    leaf_rhs,
    leaf_factor,
    pivot_count,
    parent,
    leaf_index,
    separator_rhs,
    separator_factor,
    separator_index,
    root_rhs,
    root_factor,
):
    rhs = leaf_rhs[0]
    slots = inverse_rows(leaf_index, 1024)[:, None, :]
    sep_slots = inverse_rows(separator_index, 512)[:, None, :]
    sep_rhs = jnp.transpose(separator_rhs[0], (1, 0, 2))
    y, x, c = lax.axis_index("y"), lax.axis_index("x"), lax.axis_index("c")
    place = jnp.stack([y, x, c]).astype(jnp.int32)
    line = lax.all_gather(join(leaf_factor[0], root_factor), ("z", "c"), axis=0, tiled=False)
    sep_line = gather_line(separator_factor, y, x)
    (rows, ahead, back, far_low, far_high), slots = spread_line(sep_line, slots)
    near_swapped = (swap_cores(rows), swap_cores(ahead), swap_cores(back))

    line, sep_slots, sep_rhs = lax.optimization_barrier((line, sep_slots, sep_rhs))
    border = leaf_border(pivot_count, rhs, line)
    far_low, far_high, line, border = lax.optimization_barrier((far_low, far_high, line, border))
    own_set = (rows, ahead, back, far_low, far_high)
    other_set = near_swapped + (swap_cores(far_low), swap_cores(far_high))
    incoming = lax.all_to_all(
        border.reshape(16, 16, 512), ("y", "x"), split_axis=0, concat_axis=0, tiled=True
    )
    operators = upper_operators(place, own_set, other_set, line)
    down, sep_answer, root_answer = upper_solve(
        parent, incoming, slots, leaf_index[:, None, :], sep_rhs, sep_slots,
        separator_index[:, None, :], root_rhs[0], operators,
    )
    line, down = lax.optimization_barrier((line, down))
    received = lax.all_to_all(down, ("y", "x"), split_axis=0, concat_axis=0, tiled=True)
    part, high, low = leaf_pivot(pivot_count, rhs, line)
    leaf_answer = leaf_last(pivot_count, part, received.reshape(256, 512), high, low)
    return leaf_answer[None], jnp.transpose(sep_answer, (1, 0, 2))[None], root_answer[None]


def solution(mesh):
    fine = Mesh(mesh.devices.reshape(NY, NX, NZ, NC), ("y", "x", "z", "c"))
    leaf, src = ("y", "x"), ("z", "c")
    return jax.shard_map(
        local,
        mesh=fine,
        in_specs=(
            P(leaf, src, None),
            P(leaf, src, None),
            P(leaf),
            P(),
            P(),
            P(leaf, src, None, None),
            P(None, src, None),
            P(),
            P(leaf, src, None),
            P(src, None),
        ),
        out_specs=(P(leaf, src, None), P(leaf, src, None, None), P(leaf, src, None)),
        check_vma=False,
    )
```

time: 193 us -> 167 us (0.87)
  waiting for transfers between devices: 111 us -> 14.8 us
  starting transfers between devices: 15 us -> 55.6 us
  blocking collectives: 0 us -> 28.7 us
  Pallas kernels: 25.1 us -> 35.8 us
  local copies, waits for them, and re-layouts: 16.2 us -> 7.47 us
    all_gather x1, waiting for transfers between devices: 97.4 us -> 0.02 us  [local(): lax.all_gather(join(leaf_factor[0], root_factor), ('z', 'c'), axis=0, til...]
    all_to_all x0 -> x1, blocking collectives: none -> 28.7 us  [gather_line(): lax.all_to_all(jnp.broadcast_to(mine, (NZ, 8, 512)), 'z', split_axis=0, c...]
    ppermute x0 -> x7, starting transfers between devices: none -> 23.1 us  [along_plane(): return lax.ppermute(value, ('y', 'x', 'c'), pairs)]
    ppermute x2 -> x5, starting transfers between devices: 4.85 us -> 23.1 us  [swap_cores(): return lax.ppermute(value, 'c', [(0, 1), (1, 0)])]
    unnamed x26 -> x18, local copies, waits for them, and re-layouts: 13.8 us -> 3.19 us
    ppermute x0 -> x7, waiting for transfers between devices: none -> 10.5 us  [along_plane(): return lax.ppermute(value, ('y', 'x', 'c'), pairs)]
    all_to_all x1, waiting for transfers between devices: 10.9 us -> 1.87 us  [local(): lax.all_to_all(border.reshape(16, 16, 512), ('y', 'x'), split_axis=0, con...]
    pallas_call x2 -> x3, Pallas kernels: 8.47 us -> 16 us  [the longest x1 7.33 us: upper_operators(): pl.pallas_call(upper_operator_kernel, out_shape=(jax.ShapeDtypeStruct((4,...]
  transfers between devices with their start and end apart: 5 -> 15, of which waited for: 3 -> 5; matrix products, arithmetic and copies ran while one was open for 5% -> 9% of each run, Pallas kernels for 6% -> 11%
where the time goes in v2:
time: 167 us; the launch traced here: 166 us
  starting transfers between devices  55.6 us (33%)
  Pallas kernels  35.8 us (21%)
  blocking collectives  28.7 us (17%)
  between operations  15 us (9%)
  waiting for transfers between devices  14.8 us (9%)
  other arithmetic  8.89 us (5%)
  local copies, waits for them, and re-layouts  7.47 us (4%)
    all_to_all x1, blocking collectives, gather_line(): lax.all_to_all(jnp.broadcast_to(mine, (NZ, 8, 512)), 'z', split_axis=0, c...  28.7 us
    ppermute x5, starting transfers between devices, swap_cores(): return lax.ppermute(value, 'c', [(0, 1), (1, 0)])  23.1 us
    ppermute x7, starting transfers between devices, along_plane(): return lax.ppermute(value, ('y', 'x', 'c'), pairs)  23.1 us
    pallas_call x1, Pallas kernels, upper_solve(): pl.pallas_call(upper_kernel, out_shape=(jax.ShapeDtypeStruct((16, 16, 512...  10.7 us
    ppermute x7, waiting for transfers between devices, along_plane(): return lax.ppermute(value, ('y', 'x', 'c'), pairs)  10.5 us
    reduce_max x2, other arithmetic, inverse_rows(): return jnp.max(jnp.where(index[:, :, None] == slot, place, -1), axis=1)  8.2 us
    pallas_call x1, Pallas kernels, upper_operators(): pl.pallas_call(upper_operator_kernel, out_shape=(jax.ShapeDtypeStruct((4,...  7.33 us
    pallas_call x1, Pallas kernels, leaf_pivot(): pl.pallas_call(leaf_pivot_kernel, out_shape=(jax.ShapeDtypeStruct((4, 256...  7.04 us
  transfers between devices with their start and end apart: 15, of which 5 were waited for; matrix products, arithmetic and copies ran while one was open for 9% of the time, Pallas kernels for 11%

profile of v2, /device:TPU:1, one launch (start us, length us, event | category | flops | bytes accessed | tf_op | source)
XLA Modules:
  0.0 166.2 jit_solution(11477394422943208424)
XLA Ops:
  7.2 0.0 copy-start
  7.2 0.0 all-gather.3.cloned.1.call-start
  7.2 1.7 %join.1 = f32[56,1024]{1,0:T(8,128)} custom-call(f32[48,1024]{1,0:T(8,128)} %bitcast.38, f32[16,512]{1,0:T(8,128)} %root_ref.1), custom_call_target="tpu_custom_call" | custom-call | tf_op jit(solution)/shard_map/join/pallas_call | solution.py:76
  8.9 0.0 all-gather.3.cloned.1.call-update
  9.0 28.7 %all_to_all.15 = f32[16,8,512]{2,1,0:T(8,128)S(1)} all-to-all(f32[16,8,512]{2,1,0:T(8,128)S(1)} %broadcast_in_dim.59), channel_id=1, replica_groups=mesh['y'=4,'x'=4,'z'=16,'c'=2] {'z'}, dimensions={0} | all-to-all | bytes 524288 | tf_op jit(solution)/shard_map/all_to_all | solution.py:485
  37.7 3.2 %collective-permute-start = (f32[16,8,512]{2,1,0:T(8,128)S(1)}, f32[16,8,512]{2,1,0:T(8,128)S(1)}, u32[]{:S(2)}, u32[]{:S(2)}) collective-permute-start(f32[16,8,512]{2,1,0:T(8,128)S(1)} %all_to_all.15), channel_id=1, source_target_pairs={{0,32},{1,129},{32,64},{33,161},{64,96},{65,193},{96,0},{97,225},{... | collective-permute-start | bytes 786440 | tf_op jit(solution)/shard_map/ppermute | solution.py:470
  40.9 3.4 %collective-permute-start.1 = (f32[16,8,512]{2,1,0:T(8,128)S(1)}, f32[16,8,512]{2,1,0:T(8,128)S(1)}, u32[]{:S(2)}, u32[]{:S(2)}) collective-permute-start(f32[16,8,512]{2,1,0:T(8,128)S(1)} %all_to_all.15), channel_id=1, source_target_pairs={{0,96},{1,385},{32,0},{33,417},{64,32},{65,449},{96,64},{97,481},{... | collective-permute-start | bytes 786440 | tf_op jit(solution)/shard_map/ppermute | solution.py:470
  44.2 3.5 %collective-permute-start.2 = (f32[16,8,512]{2,1,0:T(8,128)S(1)}, f32[16,8,512]{2,1,0:T(8,128)S(1)}, u32[]{:S(2)}, u32[]{:S(2)}) collective-permute-start(f32[16,8,512]{2,1,0:T(8,128)S(1)} %all_to_all.15), channel_id=1, source_target_pairs={{0,64},{1,257},{32,96},{33,289},{64,0},{65,321},{96,32},{97,353},{... | collective-permute-start | bytes 786440 | tf_op jit(solution)/shard_map/ppermute | solution.py:470
  47.8 0.6 collective-permute-done.1
  48.4 4.5 %collective-permute-done.2 = f32[16,8,512]{2,1,0:T(8,128)S(1)} collective-permute-done((f32[16,8,512]{2,1,0:T(8,128)S(1)}, f32[16,8,512]{2,1,0:T(8,128)S(1)}, u32[]{:S(2)}, u32[]{:S(2)}) %collective-permute-start.2) | collective-permute-done | bytes 262176 | tf_op jit(solution)/shard_map/ppermute | solution.py:470
  52.9 0.1 pad_maximum_fusion.refs_0_
  52.9 0.0 copy-start.1
  52.9 3.1 %collective-permute-start.3 = (f32[4,16,8,512]{3,2,1,0:T(8,128)S(1)}, f32[4,16,8,512]{3,2,1,0:T(8,128)S(1)}, u32[]{:S(2)}, u32[]{:S(2)}) collective-permute-start(f32[4,16,8,512]{3,2,1,0:T(8,128)S(1)} %pad_maximum_fusion.refs_0_), channel_id=1, source_target_pairs={{0,128},{1,33},{32,160},{33,65},{64,192},{65,97},{96,224},{97,1},{... | collective-permute-start | bytes 3145736 | tf_op jit(solution)/shard_map/ppermute | solution.py:470
  56.1 3.4 %collective-permute-start.4 = (f32[4,16,8,512]{3,2,1,0:T(8,128)S(1)}, f32[4,16,8,512]{3,2,1,0:T(8,128)S(1)}, u32[]{:S(2)}, u32[]{:S(2)}) collective-permute-start(f32[4,16,8,512]{3,2,1,0:T(8,128)S(1)} %pad_maximum_fusion.refs_0_), channel_id=1, source_target_pairs={{0,384},{1,97},{32,416},{33,1},{64,448},{65,33},{96,480},{97,65},{... | collective-permute-start | bytes 3145736 | tf_op jit(solution)/shard_map/ppermute | solution.py:470
  59.5 6.8 %select_reduce_fusion = s32[16,1024]{1,0:T(8,128)S(1)} fusion(s32[16,512]{1,0:T(8,128)} %param.14), kind=kLoop, calls=%fused_computation | loop fusion | flops 25149440 | bytes 98304 | tf_op jit(solution)/shard_map/reduce_max | solution.py:455
  66.2 0.7 broadcast_in_dim.62.slot_ref
  66.9 5.5 %collective-permute-done.3.refs_1_ = f32[4,16,8,512]{3,2,1,0:T(8,128)S(1)} collective-permute-done((f32[4,16,8,512]{3,2,1,0:T(8,128)S(1)}, f32[4,16,8,512]{3,2,1,0:T(8,128)S(1)}, u32[]{:S(2)}, u32[]{:S(2)}) %collective-permute-start.3) | collective-permute-done | bytes 1048608 | tf_op jit(solution)/shard_map/ppermute | solution.py:470
  72.4 0.0 collective-permute-done.4.refs_2_
  72.4 0.9 slice.6
  73.3 2.7 %collective-permute-start.5 = (f32[2,16,8,512]{3,2,1,0:T(8,128)}, f32[2,16,8,512]{3,2,1,0:T(8,128)}, u32[]{:S(2)}, u32[]{:S(2)}) collective-permute-start(f32[2,16,8,512]{3,2,1,0:T(8,128)} %slice.6), channel_id=1, source_target_pairs={{0,128},{1,33},{32,160},{33,65},{64,192},{65,97},{96,224},{97,1},{... | collective-permute-start | bytes 1572872 | tf_op jit(solution)/shard_map/ppermute | solution.py:470
  76.0 0.8 slice.7
  76.9 3.8 %collective-permute-start.6 = (f32[2,16,8,512]{3,2,1,0:T(8,128)}, f32[2,16,8,512]{3,2,1,0:T(8,128)}, u32[]{:S(2)}, u32[]{:S(2)}) collective-permute-start(f32[2,16,8,512]{3,2,1,0:T(8,128)} %slice.7), channel_id=1, source_target_pairs={{0,384},{1,97},{32,416},{33,1},{64,448},{65,33},{96,480},{97,65},{... | collective-permute-start | bytes 1572872 | tf_op jit(solution)/shard_map/ppermute | solution.py:470
  80.6 14.4 %collective-permute-start.7 = (f32[4,16,8,512]{3,2,1,0:T(8,128)S(1)}, f32[4,16,8,512]{3,2,1,0:T(8,128)}, u32[]{:S(2)}, u32[]{:S(2)}) collective-permute-start(f32[4,16,8,512]{3,2,1,0:T(8,128)S(1)} %pad_maximum_fusion.refs_0_), channel_id=1, source_target_pairs={{0,1},{1,0},{2,3},{3,2},{4,5},{5,4},{6,7},{7,6},{8,9},{9,8},{10,11... | collective-permute-start | bytes 3145736 | tf_op jit(solution)/shard_map/ppermute | solution.py:459
  95.1 1.9 %collective-permute-start.8 = (f32[4,16,8,512]{3,2,1,0:T(8,128)S(1)}, f32[4,16,8,512]{3,2,1,0:T(8,128)}, u32[]{:S(2)}, u32[]{:S(2)}) collective-permute-start(f32[4,16,8,512]{3,2,1,0:T(8,128)S(1)} %collective-permute-done.3.refs_1_), channel_id=1, source_target_pairs={{0,1},{1,0},{2,3},{3,2},{4,5},{5,4},{6,7},{7,6},{8,9},{9,8},{10,11... | collective-permute-start | bytes 3145736 | tf_op jit(solution)/shard_map/ppermute | solution.py:459
  97.0 2.4 %collective-permute-start.9 = (f32[4,16,8,512]{3,2,1,0:T(8,128)S(1)}, f32[4,16,8,512]{3,2,1,0:T(8,128)}, u32[]{:S(2)}, u32[]{:S(2)}) collective-permute-start(f32[4,16,8,512]{3,2,1,0:T(8,128)S(1)} %collective-permute-done.4.refs_2_), channel_id=1, source_target_pairs={{0,1},{1,0},{2,3},{3,2},{4,5},{5,4},{6,7},{7,6},{8,9},{9,8},{10,11... | collective-permute-start | bytes 3145736 | tf_op jit(solution)/shard_map/ppermute | solution.py:459
  99.4 1.6 copy.18
  101.0 1.4 select_reduce_fusion.1
  102.4 0.6 broadcast_in_dim.65.sep_slot_ref
  103.7 0.0 all-gather.3.cloned.1.call-done
  103.7 3.8 %leaf_border.1 = f32[256,512]{1,0:T(8,128)} custom-call(s32[1]{0:T(128)S(6)} %copy.19.count_ref, f32[256,1024]{1,0:T(8,128)} %bitcast.28, f32[32,56,1024]{2,1,0:T(8,128)} %bitcast.25), custom_call_target="tpu_custom_call" | custom-call | tf_op jit(solution)/shard_map/leaf_border/pallas_call | solution.py:108
  107.5 1.9 %collective-permute-start.10 = (f32[2,16,8,512]{3,2,1,0:T(8,128)}, f32[2,16,8,512]{3,2,1,0:T(8,128)}, u32[]{:S(2)}, u32[]{:S(2)}) collective-permute-start(f32[2,16,8,512]{3,2,1,0:T(8,128)} %collective-permute-done.5.refs_3_), channel_id=1, source_target_pairs={{0,1},{1,0},{2,3},{3,2},{4,5},{5,4},{6,7},{7,6},{8,9},{9,8},{10,11... | collective-permute-start | bytes 1572872 | tf_op jit(solution)/shard_map/ppermute | solution.py:459
  109.5 2.4 %collective-permute-start.11 = (f32[2,16,8,512]{3,2,1,0:T(8,128)}, f32[2,16,8,512]{3,2,1,0:T(8,128)}, u32[]{:S(2)}, u32[]{:S(2)}) collective-permute-start(f32[2,16,8,512]{3,2,1,0:T(8,128)} %collective-permute-done.6.refs_4_), channel_id=1, source_target_pairs={{0,1},{1,0},{2,3},{3,2},{4,5},{5,4},{6,7},{7,6},{8,9},{9,8},{10,11... | collective-permute-start | bytes 1572872 | tf_op jit(solution)/shard_map/ppermute | solution.py:459
  111.9 4.5 %all-to-all-start.1 = ((f32[16,16,512]{2,1,0:T(8,128)}), f32[16,16,512]{2,1,0:T(8,128)}, u32[]{:S(2)}, u32[]{:S(2)}) async-start(f32[16,16,512]{2,1,0:T(8,128)} %bitcast.30), calls=%async_computation.1 | async-start | bytes 1048576 | tf_op jit(solution)/shard_map/all_to_all | solution.py:523
  116.4 0.6 broadcast_in_dim.66.index_ref
  117.0 0.6 broadcast_in_dim.67.sep_index_ref
  117.6 0.6 pad_add_fusion.place_ref
  118.2 0.0 collective-permute-done.7.refs_5_
  118.2 0.0 collective-permute-done.8.refs_6_
  118.3 0.0 collective-permute-done.10.refs_8_
  118.3 7.3 %upper_operators.1 = (bf16[4,1024,512]{2,1,0:T(8,128)(2,1)}, bf16[4,1024,512]{2,1,0:T(8,128)(2,1)}, bf16[512,512]{1,0:T(8,128)(2,1)}, bf16[512,512]{1,0:T(8,128)(2,1)}) custom-call(s32[3]{0:T(128)} %pad_add_fusion.place_ref, f32[4,16,8,512]{3,2,1,0:T(8,128)} %copy-done.1, f32[4,16,8,512]{3,2,1,0:T(8,128)} %copy-done.2, f32[4,16,8,512]{3,2,1,0:T(8,128)} %copy-done.3, ...), custom_call_target="tpu_custom_call" | custom-call | tf_op jit(solution)/shard_map/upper_operators/pallas_call | solution.py:343
  125.7 1.9 %all-to-all-done.1.incoming_ref = f32[16,16,512]{2,1,0:T(8,128)} async-done(((f32[16,16,512]{2,1,0:T(8,128)}), f32[16,16,512]{2,1,0:T(8,128)}, u32[]{:S(2)}, u32[]{:S(2)}) %all-to-all-start.1) | async-done | bytes 524320 | tf_op jit(solution)/shard_map/all_to_all | solution.py:523
  127.5 10.7 %upper_solve.1 = (f32[16,16,512]{2,1,0:T(8,128)}, f32[4,16,512]{2,1,0:T(8,128)}, f32[16,512]{1,0:T(8,128)}) custom-call(s32[16]{0:T(128)} %parent_ref.1, f32[16,16,512]{2,1,0:T(8,128)} %all-to-all-done.1.incoming_ref, s32[16,1,1024]{2,1,0:T(1,128)} %broadcast_in_dim.62.slot_ref, s32[16,1,512]{2,1,0:T(1,128)} %broadcast_in_dim.66.index_ref, ...), custom_call_target="tpu_custom_call" | custom-call | tf_op jit(solution)/shard_map/upper_solve/pallas_call | solution.py:428
  138.2 4.9 %all-to-all-start.2 = ((f32[16,16,512]{2,1,0:T(8,128)}), f32[16,16,512]{2,1,0:T(8,128)S(1)}, u32[]{:S(2)}, u32[]{:S(2)}) async-start(f32[16,16,512]{2,1,0:T(8,128)} %get-tuple-element.42), calls=%async_computation.2 | async-start | bytes 1048576 | tf_op jit(solution)/shard_map/all_to_all | solution.py:532
  143.2 7.0 %leaf_pivot.1 = (f32[4,256,256]{2,1,0:T(8,128)}, bf16[4,512,256]{2,1,0:T(8,128)(2,1)}, bf16[4,512,256]{2,1,0:T(8,128)(2,1)}) custom-call(s32[1]{0:T(128)S(6)} %copy.19.count_ref, f32[256,1024]{1,0:T(8,128)} %bitcast.29, f32[32,56,1024]{2,1,0:T(8,128)} %bitcast.27), custom_call_target="tpu_custom_call" | custom-call | tf_op jit(solution)/shard_map/leaf_pivot/pallas_call | solution.py:175
  150.3 0.7 copy.16
  151.0 2.3 %all-to-all-done.2 = f32[16,16,512]{2,1,0:T(8,128)S(1)} async-done(((f32[16,16,512]{2,1,0:T(8,128)}), f32[16,16,512]{2,1,0:T(8,128)S(1)}, u32[]{:S(2)}, u32[]{:S(2)}) %all-to-all-start.2) | async-done | bytes 524320 | tf_op jit(solution)/shard_map/all_to_all | solution.py:532
  153.3 0.8 copy-done.4
  154.1 5.2 %leaf_last.1 = f32[256,1024]{1,0:T(8,128)} custom-call(s32[1]{0:T(128)S(6)} %copy.19.count_ref, f32[4,256,256]{2,1,0:T(8,128)} %get-tuple-element.41.part_hbm, f32[256,512]{1,0:T(8,128)} %bitcast.31, bf16[4,512,256]{2,1,0:T(8,128)(2,1)} %get-tuple-element.43.high_hbm, bf16[4,512,256]{2,1,0:T(8,128)(2,1)} %get-tuple-element.44.low_hbm), custom_call_target="tpu_custom_call" | custom-call | tf_op jit(solution)/shard_map/leaf_last/pallas_call | solution.py:229
  (20 shorter events, 0.1 us)
Async XLA Ops:
  7.2 1.8 %copy-start = (f32[4,32,512]{2,1,0:T(8,128)S(1)}, f32[4,32,512]{2,1,0:T(8,128)}, u32[]{:S(2)}) copy-start(f32[4,32,512]{2,1,0:T(8,128)} %param.16) | copy-start | bytes 786436
  7.2 96.5 %all-gather.3.cloned.1.call-start = ((), (), s32[]{:S(2)}) async-start(), calls=%async_computation.3 | async-start | bytes 7569408 | tf_op jit(solution)/shard_map/all_gather | solution.py:513
  37.7 10.1 %collective-permute-start = (f32[16,8,512]{2,1,0:T(8,128)S(1)}, f32[16,8,512]{2,1,0:T(8,128)S(1)}, u32[]{:S(2)}, u32[]{:S(2)}) collective-permute-start(f32[16,8,512]{2,1,0:T(8,128)S(1)} %all_to_all.15), channel_id=1, source_target_pairs={{0,32},{1,129},{32,64},{33,161},{64,96},{65,193},{96,0},{97,225},{... | collective-permute-start | bytes 786440 | tf_op jit(solution)/shard_map/ppermute | solution.py:470
  40.9 7.5 %collective-permute-start.1 = (f32[16,8,512]{2,1,0:T(8,128)S(1)}, f32[16,8,512]{2,1,0:T(8,128)S(1)}, u32[]{:S(2)}, u32[]{:S(2)}) collective-permute-start(f32[16,8,512]{2,1,0:T(8,128)S(1)} %all_to_all.15), channel_id=1, source_target_pairs={{0,96},{1,385},{32,0},{33,417},{64,32},{65,449},{96,64},{97,481},{... | collective-permute-start | bytes 786440 | tf_op jit(solution)/shard_map/ppermute | solution.py:470
  44.2 8.6 %collective-permute-start.2 = (f32[16,8,512]{2,1,0:T(8,128)S(1)}, f32[16,8,512]{2,1,0:T(8,128)S(1)}, u32[]{:S(2)}, u32[]{:S(2)}) collective-permute-start(f32[16,8,512]{2,1,0:T(8,128)S(1)} %all_to_all.15), channel_id=1, source_target_pairs={{0,64},{1,257},{32,96},{33,289},{64,0},{65,321},{96,32},{97,353},{... | collective-permute-start | bytes 786440 | tf_op jit(solution)/shard_map/ppermute | solution.py:470
  52.9 63.5 %copy-start.5 = (s32[16,512]{1,0:T(8,128)S(1)}, s32[16,512]{1,0:T(8,128)}, u32[]{:S(2)}) copy-start(s32[16,512]{1,0:T(8,128)} %param.14) | copy-start | bytes 98308
  52.9 64.2 %copy-start.7 = (s32[4,512]{1,0:T(4,128)S(1)}, s32[4,512]{1,0:T(4,128)}, u32[]{:S(2)}) copy-start(s32[4,512]{1,0:T(4,128)} %param.17) | copy-start | bytes 24580
  52.9 65.4 %copy-start.1 = (f32[4,16,8,512]{3,2,1,0:T(8,128)}, f32[4,16,8,512]{3,2,1,0:T(8,128)S(1)}, u32[]{:S(2)}) copy-start(f32[4,16,8,512]{3,2,1,0:T(8,128)S(1)} %pad_maximum_fusion.refs_0_) | copy-start | bytes 3145732
  52.9 19.4 %collective-permute-start.3 = (f32[4,16,8,512]{3,2,1,0:T(8,128)S(1)}, f32[4,16,8,512]{3,2,1,0:T(8,128)S(1)}, u32[]{:S(2)}, u32[]{:S(2)}) collective-permute-start(f32[4,16,8,512]{3,2,1,0:T(8,128)S(1)} %pad_maximum_fusion.refs_0_), channel_id=1, source_target_pairs={{0,128},{1,33},{32,160},{33,65},{64,192},{65,97},{96,224},{97,1},{... | collective-permute-start | bytes 3145736 | tf_op jit(solution)/shard_map/ppermute | solution.py:470
  56.1 16.3 %collective-permute-start.4 = (f32[4,16,8,512]{3,2,1,0:T(8,128)S(1)}, f32[4,16,8,512]{3,2,1,0:T(8,128)S(1)}, u32[]{:S(2)}, u32[]{:S(2)}) collective-permute-start(f32[4,16,8,512]{3,2,1,0:T(8,128)S(1)} %pad_maximum_fusion.refs_0_), channel_id=1, source_target_pairs={{0,384},{1,97},{32,416},{33,1},{64,448},{65,33},{96,480},{97,65},{... | collective-permute-start | bytes 3145736 | tf_op jit(solution)/shard_map/ppermute | solution.py:470
  72.4 45.9 %copy-start.2 = (f32[4,16,8,512]{3,2,1,0:T(8,128)}, f32[4,16,8,512]{3,2,1,0:T(8,128)S(1)}, u32[]{:S(2)}) copy-start(f32[4,16,8,512]{3,2,1,0:T(8,128)S(1)} %collective-permute-done.3.refs_1_) | copy-start | bytes 3145732
  72.4 45.9 %copy-start.3 = (f32[4,16,8,512]{3,2,1,0:T(8,128)}, f32[4,16,8,512]{3,2,1,0:T(8,128)S(1)}, u32[]{:S(2)}) copy-start(f32[4,16,8,512]{3,2,1,0:T(8,128)S(1)} %collective-permute-done.4.refs_2_) | copy-start | bytes 3145732
  73.3 34.2 %collective-permute-start.5 = (f32[2,16,8,512]{3,2,1,0:T(8,128)}, f32[2,16,8,512]{3,2,1,0:T(8,128)}, u32[]{:S(2)}, u32[]{:S(2)}) collective-permute-start(f32[2,16,8,512]{3,2,1,0:T(8,128)} %slice.6), channel_id=1, source_target_pairs={{0,128},{1,33},{32,160},{33,65},{64,192},{65,97},{96,224},{97,1},{... | collective-permute-start | bytes 1572872 | tf_op jit(solution)/shard_map/ppermute | solution.py:470
  76.9 30.7 %collective-permute-start.6 = (f32[2,16,8,512]{3,2,1,0:T(8,128)}, f32[2,16,8,512]{3,2,1,0:T(8,128)}, u32[]{:S(2)}, u32[]{:S(2)}) collective-permute-start(f32[2,16,8,512]{3,2,1,0:T(8,128)} %slice.7), channel_id=1, source_target_pairs={{0,384},{1,97},{32,416},{33,1},{64,448},{65,33},{96,480},{97,65},{... | collective-permute-start | bytes 1572872 | tf_op jit(solution)/shard_map/ppermute | solution.py:470
  80.6 37.6 %collective-permute-start.7 = (f32[4,16,8,512]{3,2,1,0:T(8,128)S(1)}, f32[4,16,8,512]{3,2,1,0:T(8,128)}, u32[]{:S(2)}, u32[]{:S(2)}) collective-permute-start(f32[4,16,8,512]{3,2,1,0:T(8,128)S(1)} %pad_maximum_fusion.refs_0_), channel_id=1, source_target_pairs={{0,1},{1,0},{2,3},{3,2},{4,5},{5,4},{6,7},{7,6},{8,9},{9,8},{10,11... | collective-permute-start | bytes 3145736 | tf_op jit(solution)/shard_map/ppermute | solution.py:459
  95.1 23.2 %collective-permute-start.8 = (f32[4,16,8,512]{3,2,1,0:T(8,128)S(1)}, f32[4,16,8,512]{3,2,1,0:T(8,128)}, u32[]{:S(2)}, u32[]{:S(2)}) collective-permute-start(f32[4,16,8,512]{3,2,1,0:T(8,128)S(1)} %collective-permute-done.3.refs_1_), channel_id=1, source_target_pairs={{0,1},{1,0},{2,3},{3,2},{4,5},{5,4},{6,7},{7,6},{8,9},{9,8},{10,11... | collective-permute-start | bytes 3145736 | tf_op jit(solution)/shard_map/ppermute | solution.py:459
  97.0 21.3 %collective-permute-start.9 = (f32[4,16,8,512]{3,2,1,0:T(8,128)S(1)}, f32[4,16,8,512]{3,2,1,0:T(8,128)}, u32[]{:S(2)}, u32[]{:S(2)}) collective-permute-start(f32[4,16,8,512]{3,2,1,0:T(8,128)S(1)} %collective-permute-done.4.refs_2_), channel_id=1, source_target_pairs={{0,1},{1,0},{2,3},{3,2},{4,5},{5,4},{6,7},{7,6},{8,9},{9,8},{10,11... | collective-permute-start | bytes 3145736 | tf_op jit(solution)/shard_map/ppermute | solution.py:459
  107.5 10.7 %collective-permute-start.10 = (f32[2,16,8,512]{3,2,1,0:T(8,128)}, f32[2,16,8,512]{3,2,1,0:T(8,128)}, u32[]{:S(2)}, u32[]{:S(2)}) collective-permute-start(f32[2,16,8,512]{3,2,1,0:T(8,128)} %collective-permute-done.5.refs_3_), channel_id=1, source_target_pairs={{0,1},{1,0},{2,3},{3,2},{4,5},{5,4},{6,7},{7,6},{8,9},{9,8},{10,11... | collective-permute-start | bytes 1572872 | tf_op jit(solution)/shard_map/ppermute | solution.py:459
  109.5 8.8 %collective-permute-start.11 = (f32[2,16,8,512]{3,2,1,0:T(8,128)}, f32[2,16,8,512]{3,2,1,0:T(8,128)}, u32[]{:S(2)}, u32[]{:S(2)}) collective-permute-start(f32[2,16,8,512]{3,2,1,0:T(8,128)} %collective-permute-done.6.refs_4_), channel_id=1, source_target_pairs={{0,1},{1,0},{2,3},{3,2},{4,5},{5,4},{6,7},{7,6},{8,9},{9,8},{10,11... | collective-permute-start | bytes 1572872 | tf_op jit(solution)/shard_map/ppermute | solution.py:459
  111.9 15.6 %all-to-all-start.1 = ((f32[16,16,512]{2,1,0:T(8,128)}), f32[16,16,512]{2,1,0:T(8,128)}, u32[]{:S(2)}, u32[]{:S(2)}) async-start(f32[16,16,512]{2,1,0:T(8,128)} %bitcast.30), calls=%async_computation.1 | async-start | bytes 1048576 | tf_op jit(solution)/shard_map/all_to_all | solution.py:523
  138.2 12.0 %copy-start.6 = (f32[4,16,512]{2,1,0:T(8,128)S(1)}, f32[4,16,512]{2,1,0:T(8,128)}, u32[]{:S(2)}) copy-start(f32[4,16,512]{2,1,0:T(8,128)} %get-tuple-element.45) | copy-start | bytes 393220
  138.2 15.1 %all-to-all-start.2 = ((f32[16,16,512]{2,1,0:T(8,128)}), f32[16,16,512]{2,1,0:T(8,128)S(1)}, u32[]{:S(2)}, u32[]{:S(2)}) async-start(f32[16,16,512]{2,1,0:T(8,128)} %get-tuple-element.42), calls=%async_computation.2 | async-start | bytes 1048576 | tf_op jit(solution)/shard_map/all_to_all | solution.py:532
  153.3 0.8 copy-start.4
Sparse Core Ops, SparseCore 0:
  10.1 87.5 all-gather.2

commit v3 on v2

--- a/solution.py
+++ b/solution.py
@@ -23,14 +23,14 @@
     return lax.dot_general(a, b, (((1,), (0,)), ((), ())), preferred_element_type=F32)
 
 
-def three_products(dot, a, b):
-    return dot(a[0], b[0]) + (dot(a[1], b[0]) + dot(a[0], b[1]))
-
-
-def stacked_products(dot, a, b):
-    rows = a[0].shape[0]
-    both = dot(jnp.concatenate([a[0], a[1]], axis=0), b[0])
-    return both[:rows] + (both[rows:] + dot(a[0], b[1]))
+def stack2(pair):
+    return jnp.concatenate(pair, axis=0)
+
+
+def stacked_products(dot, both, b):
+    rows = both.shape[0] // 2
+    first = dot(both, b[0])
+    return first[:rows] + (first[rows:] + dot(both[:rows], b[1]))
 
 
 def params(mebibytes):
@@ -94,12 +94,12 @@
     copy.start()
     load.wait()
     cols = lax.broadcasted_iota(jnp.int32, rhs_ref.shape, 1)
-    rhs = split2(jnp.where(cols < count_ref[0], rhs_ref[...], 0.0))
+    rhs = stack2(split2(jnp.where(cols < count_ref[0], rhs_ref[...], 0.0)))
     copy.wait()
     rows = buffer[...].reshape(528, 1024)
     for block in range(2):
         first = 16 + 256 * block
-        border_ref[:, 256 * block : 256 * (block + 1)] = three_products(
+        border_ref[:, 256 * block : 256 * (block + 1)] = stacked_products(
             dot_nt, rhs, split2(rows[first : first + 256])
         )
 
@@ -135,7 +135,7 @@
     count = count_ref[0]
     load.wait()
     cols = lax.broadcasted_iota(jnp.int32, rhs_ref.shape, 1)
-    rhs = split2(jnp.where(cols < count, rhs_ref[...], 0.0))
+    rhs = stack2(split2(jnp.where(cols < count, rhs_ref[...], 0.0)))
     copy.wait()
     top = buffer[...].reshape(1056, 1024)
     solved = []
@@ -149,17 +149,17 @@
         high, low = split2(values)
         high_ref[first:wide, :wide] = high
         low_ref[first:wide, :wide] = low
-        solved.append(three_products(dot_nt, (rhs[0][:, :wide], rhs[1][:, :wide]), (high, low)))
-    solved = split2(jnp.concatenate(solved, axis=1))
+        solved.append(stacked_products(dot_nt, rhs[:, :wide], (high, low)))
+    solved = stack2(split2(jnp.concatenate(solved, axis=1)))
     border_copy.wait()
     border = border_buffer[...].reshape(528, 1024)
     stores = []
     for block in range(4):
         first, wide = 256 * block, 256 * (block + 1)
         border_high_ref[block], border_low_ref[block] = split2(border[16:, first:wide])
-        part_ref[block] = three_products(
+        part_ref[block] = stacked_products(
             dot_nn,
-            (solved[0][:, first:], solved[1][:, first:]),
+            solved[:, first:],
             (high_ref[first:, first:wide], low_ref[first:, first:wide]),
         )
         stores += [
@@ -211,11 +211,11 @@
     ]
     for group in copies:
         start_all(group)
-    border = split2(border_ref[...])
+    border = stack2(split2(border_ref[...]))
     stores = []
     for block in range(4):
         wait_all(copies[block])
-        answer = part_ref[block] + three_products(dot_nn, border, (high_ref[block], low_ref[block]))
+        answer = part_ref[block] + stacked_products(dot_nn, border, (high_ref[block], low_ref[block]))
         cols = 256 * block + lax.broadcasted_iota(jnp.int32, answer.shape, 1)
         out_ref[block] = jnp.where(cols < count_ref[0], answer, 0.0)
         stores.append(
@@ -239,21 +239,39 @@
             pltpu.SemaphoreType.DMA((4, 3)),
             pltpu.SemaphoreType.DMA((4,)),
         ],
-        compiler_params=params(60),
+        compiler_params=params(59),
         name="leaf_last",
     )(count, part, border, high, low)
+
+
+LANE_GATHER = lax.GatherDimensionNumbers(
+    offset_dims=(),
+    collapsed_slice_dims=(1,),
+    start_index_map=(1,),
+    operand_batching_dims=(0,),
+    start_indices_batching_dims=(0,),
+)
+
+
+def take_lanes(value, lane):
+    return lax.gather(
+        value, lane[..., None], LANE_GATHER, slice_sizes=(1, 1), mode=lax.GatherScatterMode.PROMISE_IN_BOUNDS
+    )
 
 
 def pick(values, index_row):
     out = []
     for block in range(index_row.shape[1] // LANES):
-        index = jnp.broadcast_to(index_row[:, block * LANES : (block + 1) * LANES], (16, LANES))
-        lane, source = index & (LANES - 1), index >> 7
-        total = jnp.zeros((16, LANES), F32)
-        for at, value in enumerate(values):
-            taken = jnp.take_along_axis(value, lane, axis=1)
-            total = jnp.where(source == at, taken, total)
-        out.append(total)
+        index = jnp.broadcast_to(index_row[:, block * LANES : (block + 1) * LANES], (8, LANES))
+        lane, found = index & (LANES - 1), index >= 0
+        bits = [(index & (LANES << bit)) != 0 for bit in range(len(values).bit_length() - 1)]
+        halves = []
+        for half in range(2):
+            level = [take_lanes(value[8 * half : 8 * half + 8], lane) for value in values]
+            for bit in bits:
+                level = [jnp.where(bit, odd, even) for even, odd in zip(level[::2], level[1::2])]
+            halves.append(jnp.where(found, level[0], 0.0))
+        out.append(jnp.concatenate(halves, axis=0))
     return out
 
 
@@ -262,20 +280,37 @@
 
 
 OFFSETS = (0, -1, 1, -2)
+TILES = [min(4, z // 2 + 1) for z in range(NZ)]
+FIRST_TILE = [sum(TILES[:z]) for z in range(NZ)]
+PACKED = sum(TILES)
+
+
+def pack_kernel(line_ref, out_ref):
+    for z in range(NZ):
+        for tile in range(TILES[z]):
+            out_ref[FIRST_TILE[z] + tile] = line_ref[z, :, tile * LANES : (tile + 1) * LANES]
+
+
+def pack(line):
+    return pl.pallas_call(
+        pack_kernel,
+        out_shape=jax.ShapeDtypeStruct((PACKED, 8, LANES), F32),
+        in_specs=[full_vmem()],
+        out_specs=full_vmem(),
+        compiler_params=params(60),
+        name="pack",
+    )(line)
 
 
 def upper_operator_kernel(place_ref, *refs):
-    own_refs, other_refs, line_ref = refs[:5], refs[5:10], refs[10]
-    high_hbm, low_hbm, root_high_hbm, root_low_hbm = refs[11:15]
-    buffer, root_buffer, high_ref, low_ref, root_high_ref, root_low_ref, sem, root_sem, out_sem = refs[15:]
+    own_refs, other_refs, line_ref = refs[:4], refs[4:8], refs[8]
+    high_hbm, low_hbm, root_high_hbm, root_low_hbm = refs[9:13]
+    buffer, root_buffer, high_ref, low_ref, root_high_ref, root_low_ref, sem, root_sem, out_sem = refs[13:]
     y, x, c = place_ref[0], place_ref[1], place_ref[2]
     for piece_refs, parity in ((own_refs, c), (other_refs, 1 - c)):
         for outer in range(4):
             for inner in range(4):
-                if outer < 3:
-                    source = piece_refs[outer].at[inner]
-                else:
-                    source = piece_refs[3 + inner // 2].at[inner % 2]
+                source = piece_refs[outer].at[inner]
                 along_y = jnp.where(parity == 0, OFFSETS[outer], OFFSETS[inner])
                 along_x = jnp.where(parity == 0, OFFSETS[inner], OFFSETS[outer])
                 group = jnp.where(parity == 0, outer, inner)
@@ -291,48 +326,67 @@
         for half in range(2)
     ]
     start_all(root_copies)
-    stores = []
-
-    def send(value_ref, to_ref, at):
-        stores.append(pltpu.make_async_copy(value_ref, to_ref, out_sem.at[at]))
-        stores[-1].start()
-
-    for group in range(4):
+
+    def out_copies(group):
+        offset = jnp.int32(OFFSETS[0])
+        for at in range(1, 4):
+            offset = jnp.where(group == at, OFFSETS[at], offset)
+        sep = lax.rem(y + offset + 8, 4)
+        return sep, [
+            pltpu.make_async_copy(high_ref.at[sep], high_hbm.at[sep], out_sem.at[2 * group]),
+            pltpu.make_async_copy(low_ref.at[sep], low_hbm.at[sep], out_sem.at[2 * group + 1]),
+        ]
+
+    def one_group(group, _):
         for _ in range(8):
             pltpu.make_async_copy(own_refs[0].at[0], buffer.at[0, 0, 0], sem.at[group]).wait()
-        sep = lax.rem(y + OFFSETS[group] + 8, 4)
-
-        def rows(z, parity):
-            return jnp.concatenate([buffer[sep, q, parity, z] for q in range(4)], axis=0)
-
-        def pivot_rows(z, _):
+        sep, copies = out_copies(group)
+
+        def rows(parity, first, tiles):
+            return jnp.concatenate([
+                jnp.concatenate([buffer[sep, q, parity, first + tile] for tile in range(tiles)], axis=1)
+                for q in range(4)
+            ], axis=0)
+
+        for z in range(8):
+            width = TILES[z] * LANES
             for parity in range(2):
-                shard = 2 * z + parity
-                row_ids = shard * 32 + lax.broadcasted_iota(jnp.int32, (32, 512), 0)
-                col_ids = lax.broadcasted_iota(jnp.int32, (32, 512), 1)
-                value = lower_unit(rows(z, parity), row_ids, col_ids)
-                to = pl.ds(pl.multiple_of(shard * 32, 32), 32)
-                high_ref[sep, to], low_ref[sep, to] = split2(value)
-            return 0
+                first_row = 32 * (2 * z + parity)
+                row_ids = first_row + lax.broadcasted_iota(jnp.int32, (32, width), 0)
+                col_ids = lax.broadcasted_iota(jnp.int32, (32, width), 1)
+                value = lower_unit(rows(parity, FIRST_TILE[z], TILES[z]), row_ids, col_ids)
+                high, low = split2(value)
+                to = slice(first_row, first_row + 32)
+                high_ref[sep, to, :width] = high
+                low_ref[sep, to, :width] = low
+                if width < 512:
+                    high_ref[sep, to, width:] = jnp.zeros((32, 512 - width), BF16)
+                    low_ref[sep, to, width:] = jnp.zeros((32, 512 - width), BF16)
 
         def border_rows(z, _):
             for parity in range(2):
                 to = pl.ds(pl.multiple_of((2 * z + parity) * 32, 32), 32)
-                high_ref[sep, to], low_ref[sep, to] = split2(rows(z, parity))
+                high_ref[sep, to], low_ref[sep, to] = split2(rows(parity, FIRST_TILE[8] + 4 * (z - 8), 4))
             return 0
 
-        lax.fori_loop(0, 8, pivot_rows, 0)
         lax.fori_loop(8, 16, border_rows, 0)
-        send(high_ref.at[sep], high_hbm.at[sep], 2 * group)
-        send(low_ref.at[sep], low_hbm.at[sep], 2 * group + 1)
+        start_all(copies)
+        return 0
+
+    lax.fori_loop(0, 4, one_group, 0)
     wait_all(root_copies)
     row_ids = lax.broadcasted_iota(jnp.int32, (512, 512), 0)
     col_ids = lax.broadcasted_iota(jnp.int32, (512, 512), 1)
     value = lower_unit(root_buffer[...].reshape(512, 512), row_ids, col_ids)
     root_high_ref[...], root_low_ref[...] = split2(value)
-    send(root_high_ref, root_high_hbm, 8)
-    send(root_low_ref, root_low_hbm, 9)
-    wait_all(stores)
+    root_stores = [
+        pltpu.make_async_copy(root_high_ref, root_high_hbm, out_sem.at[8]),
+        pltpu.make_async_copy(root_low_ref, root_low_hbm, out_sem.at[9]),
+    ]
+    start_all(root_stores)
+    for group in range(4):
+        wait_all(out_copies(group)[1])
+    wait_all(root_stores)
 
 
 def lower_unit(value, row_ids, col_ids):
@@ -348,10 +402,10 @@
             jax.ShapeDtypeStruct((512, 512), BF16),
             jax.ShapeDtypeStruct((512, 512), BF16),
         ),
-        in_specs=[full_smem()] + [in_hbm()] * 11,
+        in_specs=[full_smem()] + [in_hbm()] * 9,
         out_specs=(in_hbm(),) * 4,
         scratch_shapes=[
-            pltpu.VMEM((NY, NX, NC, NZ, 8, 512), F32),
+            pltpu.VMEM((NY, NX, NC, PACKED, 8, LANES), F32),
             pltpu.VMEM((32, 16, 512), F32),
             pltpu.VMEM((4, 1024, 512), BF16),
             pltpu.VMEM((4, 1024, 512), BF16),
@@ -398,22 +452,28 @@
     root_total = root_rhs_ref[...]
     for sep in range(4):
         wait_all(loads[sep])
-        pivot = split2(sep_rhs_ref[sep] + updates[sep, :, :512])
-        forward = stacked_products(dot_nt, pivot, (high_ref[sep], low_ref[sep]))
-        solved[sep] = forward[:, :512]
-        border = forward[:, 512:] + updates[sep, :, 512:]
+        pivot = stack2(split2(sep_rhs_ref[sep] + updates[sep, :, :512]))
+        solved[sep, :, :256] = stacked_products(
+            dot_nt, pivot[:, :256], (high_ref[sep, :256, :256], low_ref[sep, :256, :256])
+        )
+        forward = stacked_products(dot_nt, pivot, (high_ref[sep, 256:], low_ref[sep, 256:]))
+        solved[sep, :, 256:] = forward[:, :256]
+        border = forward[:, 256:] + updates[sep, :, 512:]
         root_total = root_total + jnp.concatenate(pick(blocks(border), sep_slot_ref[sep]), axis=1)
     wait_all(loads[4])
     root = (root_high_ref[...], root_low_ref[...])
-    root_solved = stacked_products(dot_nt, split2(root_total), root)
-    root_answer = stacked_products(dot_nn, split2(root_solved), root)
+    root_solved = stacked_products(dot_nt, stack2(split2(root_total)), root)
+    root_answer = stacked_products(dot_nn, stack2(split2(root_solved)), root)
     root_out_ref[...] = root_answer
     for sep in range(4):
         border = jnp.concatenate(pick(blocks(root_answer), sep_index_ref[sep]), axis=1)
-        joined = split2(jnp.concatenate([solved[sep], border], axis=1))
-        answer = stacked_products(dot_nn, joined, (high_ref[sep], low_ref[sep]))
-        sep_out_ref[sep] = answer
-        full[sep, :, :512] = answer
+        joined = stack2(split2(jnp.concatenate([solved[sep], border], axis=1)))
+        left = stacked_products(dot_nn, joined, (high_ref[sep, :, :256], low_ref[sep, :, :256]))
+        right = stacked_products(dot_nn, joined[:, 256:], (high_ref[sep, 256:, 256:], low_ref[sep, 256:, 256:]))
+        sep_out_ref[sep, :, :256] = left
+        sep_out_ref[sep, :, 256:] = right
+        full[sep, :, :256] = left
+        full[sep, :, 256:512] = right
         full[sep, :, 512:] = border
 
     def gather(leaf, _):
@@ -474,10 +534,7 @@
     ahead = along_plane(value, 1, first)
     back = along_plane(value, -1, first)
     ahead, back, beside = lax.optimization_barrier((ahead, back, beside))
-    half = value.shape[0] // 2
-    far_low = along_plane(ahead[:half], 1, first)
-    far_high = along_plane(back[half:], -1, first)
-    return (value, ahead, back, far_low, far_high), beside
+    return (value, ahead, back, along_plane(ahead, 1, first)), beside
 
 
 def gather_line(separator_factor, y, x):
@@ -487,9 +544,14 @@
     )
 
 
-def spread_line(line, beside):
-    rows = jnp.stack([line, along_plane(line, 1, True), along_plane(line, -1, True), along_plane(line, 2, True)])
-    return gather_plane(rows, False, beside)
+def spread_line(line, beside_first, beside_second):
+    parts = [line, along_plane(line, 1, True), along_plane(line, -1, True), along_plane(line, 2, True)]
+    parts, beside_first = lax.optimization_barrier((parts, beside_first))
+    rows = jnp.stack(parts)
+    swapped = swap_cores(rows)
+    own, (beside_second, swapped) = gather_plane(rows, False, (beside_second, swapped))
+    other = (swapped, swap_cores(own[1]), swap_cores(own[2]))
+    return own, other, beside_first, beside_second
 
 
 def local(
@@ -512,14 +574,11 @@
     place = jnp.stack([y, x, c]).astype(jnp.int32)
     line = lax.all_gather(join(leaf_factor[0], root_factor), ("z", "c"), axis=0, tiled=False)
     sep_line = gather_line(separator_factor, y, x)
-    (rows, ahead, back, far_low, far_high), slots = spread_line(sep_line, slots)
-    near_swapped = (swap_cores(rows), swap_cores(ahead), swap_cores(back))
-
-    line, sep_slots, sep_rhs = lax.optimization_barrier((line, sep_slots, sep_rhs))
+    own_set, other_set, (sep_slots, sep_rhs), slots = spread_line(pack(sep_line), (sep_slots, sep_rhs), slots)
+
     border = leaf_border(pivot_count, rhs, line)
-    far_low, far_high, line, border = lax.optimization_barrier((far_low, far_high, line, border))
-    own_set = (rows, ahead, back, far_low, far_high)
-    other_set = near_swapped + (swap_cores(far_low), swap_cores(far_high))
+    far, line, border = lax.optimization_barrier((own_set[3], line, border))
+    own_set, other_set = own_set[:3] + (far,), other_set + (swap_cores(far),)
     incoming = lax.all_to_all(
         border.reshape(16, 16, 512), ("y", "x"), split_axis=0, concat_axis=0, tiled=True
     )

time: 167 us -> 163 us (0.976)
  blocking collectives: 28.7 us -> 0 us
  starting transfers between devices: 55.6 us -> 68.2 us
  waiting for transfers between devices: 14.8 us -> 23.4 us
    all_to_all x1 -> x0, blocking collectives: 28.7 us -> none  [gather_line(): lax.all_to_all(jnp.broadcast_to(mine, (NZ, 8, 512)), 'z', split_axis=0, c...]
    all_to_all x0 -> x1, starting transfers between devices: none -> 15.7 us  [gather_line(): lax.all_to_all(jnp.broadcast_to(mine, (NZ, 8, 512)), 'z', split_axis=0, c...]
    all_to_all x0 -> x1, waiting for transfers between devices: none -> 11.5 us  [gather_line(): lax.all_to_all(jnp.broadcast_to(mine, (NZ, 8, 512)), 'z', split_axis=0, c...]
    ppermute x7 -> x6, waiting for transfers between devices: 10.5 us -> 2.7 us  [along_plane(): return lax.ppermute(value, ('y', 'x', 'c'), pairs)]
    all_gather x1, waiting for transfers between devices: 0.02 us -> 4.97 us  [local(): lax.all_gather(join(leaf_factor[0], root_factor), ('z', 'c'), axis=0, til...]
    ppermute x7 -> x6, starting transfers between devices: 23.1 us -> 18.5 us  [along_plane(): return lax.ppermute(value, ('y', 'x', 'c'), pairs)]
    all_to_all x1, starting transfers between devices: 4.5 us -> 6.74 us  [local(): lax.all_to_all(border.reshape(16, 16, 512), ('y', 'x'), split_axis=0, con...]
    slice x2 -> x0, local copies, waits for them, and re-layouts: 1.75 us -> none  [the longest x1 0.92 us: gather_plane(): far_low = along_plane(ahead[:half], 1, first)]
  transfers between devices with their start and end apart: 15 -> 14, of which waited for: 5 -> 5; matrix products, arithmetic and copies ran while one was open for 9% -> 10% of each run, Pallas kernels for 11% -> 12%
where the time goes in v3:
time: 163 us; the launch traced here: 162 us
  starting transfers between devices  68.2 us (42%)
  Pallas kernels  37.4 us (23%)
  waiting for transfers between devices  23.4 us (14%)
  between operations  15 us (9%)
  other arithmetic  9.82 us (6%)
  local copies, waits for them, and re-layouts  7.92 us (5%)
    ppermute x4, starting transfers between devices, swap_cores(): return lax.ppermute(value, 'c', [(0, 1), (1, 0)])  22.2 us
    ppermute x6, starting transfers between devices, along_plane(): return lax.ppermute(value, ('y', 'x', 'c'), pairs)  18.5 us
    all_to_all x1, starting transfers between devices, gather_line(): lax.all_to_all(jnp.broadcast_to(mine, (NZ, 8, 512)), 'z', split_axis=0, c...  15.7 us
    all_to_all x1, waiting for transfers between devices, gather_line(): lax.all_to_all(jnp.broadcast_to(mine, (NZ, 8, 512)), 'z', split_axis=0, c...  11.5 us
    pallas_call x1, Pallas kernels, upper_solve(): pl.pallas_call(upper_kernel, out_shape=(jax.ShapeDtypeStruct((16, 16, 512...  11.1 us
    reduce_max x2, other arithmetic, inverse_rows(): return jnp.max(jnp.where(index[:, :, None] == slot, place, -1), axis=1)  8.21 us
    pallas_call x1, Pallas kernels, leaf_pivot(): pl.pallas_call(leaf_pivot_kernel, out_shape=(jax.ShapeDtypeStruct((4, 256...  7.06 us
    pallas_call x1, Pallas kernels, upper_operators(): pl.pallas_call(upper_operator_kernel, out_shape=(jax.ShapeDtypeStruct((4,...  6.98 us
  transfers between devices with their start and end apart: 14, of which 5 were waited for; matrix products, arithmetic and copies ran while one was open for 10% of the time, Pallas kernels for 12%

profile of v3, /device:TPU:1, one launch (start us, length us, event | category | flops | bytes accessed | tf_op | source)
XLA Modules:
  0.0 161.8 jit_solution(6401831145081737232)
XLA Ops:
  7.2 0.0 copy-start
  7.2 0.0 copy-start.10
  7.2 0.0 copy-start.8
  7.2 0.0 all-gather.3.cloned.1.call-start
  7.2 1.7 %join.1 = f32[56,1024]{1,0:T(8,128)} custom-call(f32[48,1024]{1,0:T(8,128)} %bitcast.38, f32[16,512]{1,0:T(8,128)} %root_ref.1), custom_call_target="tpu_custom_call" | custom-call | tf_op jit(solution)/shard_map/join/pallas_call | solution.py:76
  8.9 0.0 all-gather.3.cloned.1.call-update
  9.0 0.7 broadcast_in_dim.59
  9.7 15.7 %all-to-all-start = ((f32[16,8,512]{2,1,0:T(8,128)}), f32[16,8,512]{2,1,0:T(8,128)S(1)}, u32[]{:S(2)}, u32[]{:S(2)}) async-start(f32[16,8,512]{2,1,0:T(8,128)} %broadcast_in_dim.59), calls=%async_computation | async-start | bytes 524288 | tf_op jit(solution)/shard_map/all_to_all | solution.py:542
  25.5 1.6 copy.18
  27.1 11.5 %all-to-all-done.line_ref = f32[16,8,512]{2,1,0:T(8,128)S(1)} async-done(((f32[16,8,512]{2,1,0:T(8,128)}), f32[16,8,512]{2,1,0:T(8,128)S(1)}, u32[]{:S(2)}, u32[]{:S(2)}) %all-to-all-start) | async-done | bytes 262176 | tf_op jit(solution)/shard_map/all_to_all | solution.py:542
  38.6 0.7 copy-done.4
  39.3 1.6 %pack.1 = f32[52,8,128]{2,1,0:T(8,128)} custom-call(f32[16,8,512]{2,1,0:T(8,128)} %copy-done.4), custom_call_target="tpu_custom_call" | custom-call | tf_op jit(solution)/shard_map/pack/pallas_call | solution.py:295
  40.9 3.2 %collective-permute-start = (f32[52,8,128]{2,1,0:T(8,128)}, f32[52,8,128]{2,1,0:T(8,128)S(1)}, u32[]{:S(2)}, u32[]{:S(2)}) collective-permute-start(f32[52,8,128]{2,1,0:T(8,128)} %pack.1), channel_id=1, source_target_pairs={{0,32},{1,129},{32,64},{33,161},{64,96},{65,193},{96,0},{97,225},{... | collective-permute-start | bytes 638984 | tf_op jit(solution)/shard_map/ppermute | solution.py:530
  44.2 3.3 %collective-permute-start.1 = (f32[52,8,128]{2,1,0:T(8,128)}, f32[52,8,128]{2,1,0:T(8,128)S(1)}, u32[]{:S(2)}, u32[]{:S(2)}) collective-permute-start(f32[52,8,128]{2,1,0:T(8,128)} %pack.1), channel_id=1, source_target_pairs={{0,96},{1,385},{32,0},{33,417},{64,32},{65,449},{96,64},{97,481},{... | collective-permute-start | bytes 638984 | tf_op jit(solution)/shard_map/ppermute | solution.py:530
  47.5 3.5 %collective-permute-start.2 = (f32[52,8,128]{2,1,0:T(8,128)}, f32[52,8,128]{2,1,0:T(8,128)S(1)}, u32[]{:S(2)}, u32[]{:S(2)}) collective-permute-start(f32[52,8,128]{2,1,0:T(8,128)} %pack.1), channel_id=1, source_target_pairs={{0,64},{1,257},{32,96},{33,289},{64,0},{65,321},{96,32},{97,353},{... | collective-permute-start | bytes 638984 | tf_op jit(solution)/shard_map/ppermute | solution.py:530
  51.1 1.4 select_reduce_fusion.1
  52.5 0.6 broadcast_in_dim.62.sep_slot_ref
  53.1 0.0 collective-permute-done
  53.1 0.0 collective-permute-done.1
  53.1 2.7 %collective-permute-done.2 = f32[52,8,128]{2,1,0:T(8,128)S(1)} collective-permute-done((f32[52,8,128]{2,1,0:T(8,128)}, f32[52,8,128]{2,1,0:T(8,128)S(1)}, u32[]{:S(2)}, u32[]{:S(2)}) %collective-permute-start.2) | collective-permute-done | bytes 213024 | tf_op jit(solution)/shard_map/ppermute | solution.py:530
  55.8 1.0 pad_maximum_fusion.refs_0_
  56.8 0.0 copy-start.1
  56.8 3.1 %collective-permute-start.3 = (f32[4,52,8,128]{3,2,1,0:T(8,128)S(1)}, f32[4,52,8,128]{3,2,1,0:T(8,128)S(1)}, u32[]{:S(2)}, u32[]{:S(2)}) collective-permute-start(f32[4,52,8,128]{3,2,1,0:T(8,128)S(1)} %pad_maximum_fusion.refs_0_), channel_id=1, source_target_pairs={{0,128},{1,33},{32,160},{33,65},{64,192},{65,97},{96,224},{97,1},{... | collective-permute-start | bytes 2555912 | tf_op jit(solution)/shard_map/ppermute | solution.py:530
  60.0 3.3 %collective-permute-start.4 = (f32[4,52,8,128]{3,2,1,0:T(8,128)S(1)}, f32[4,52,8,128]{3,2,1,0:T(8,128)S(1)}, u32[]{:S(2)}, u32[]{:S(2)}) collective-permute-start(f32[4,52,8,128]{3,2,1,0:T(8,128)S(1)} %pad_maximum_fusion.refs_0_), channel_id=1, source_target_pairs={{0,384},{1,97},{32,416},{33,1},{64,448},{65,33},{96,480},{97,65},{... | collective-permute-start | bytes 2555912 | tf_op jit(solution)/shard_map/ppermute | solution.py:530
  63.3 13.2 %collective-permute-start.5 = (f32[4,52,8,128]{3,2,1,0:T(8,128)S(1)}, f32[4,52,8,128]{3,2,1,0:T(8,128)S(1)}, u32[]{:S(2)}, u32[]{:S(2)}) collective-permute-start(f32[4,52,8,128]{3,2,1,0:T(8,128)S(1)} %pad_maximum_fusion.refs_0_), channel_id=1, source_target_pairs={{0,1},{1,0},{2,3},{3,2},{4,5},{5,4},{6,7},{7,6},{8,9},{9,8},{10,11... | collective-permute-start | bytes 2555912 | tf_op jit(solution)/shard_map/ppermute | solution.py:519
  76.5 6.8 %select_reduce_fusion = s32[16,1024]{1,0:T(8,128)S(1)} fusion(s32[16,512]{1,0:T(8,128)} %param.14), kind=kLoop, calls=%fused_computation | loop fusion | flops 25149440 | bytes 98304 | tf_op jit(solution)/shard_map/reduce_max | solution.py:515
  83.3 0.7 broadcast_in_dim.65.slot_ref
  84.0 0.0 collective-permute-done.3.refs_1_
  84.0 1.9 %collective-permute-start.6 = (f32[4,52,8,128]{3,2,1,0:T(8,128)S(1)}, f32[4,52,8,128]{3,2,1,0:T(8,128)}, u32[]{:S(2)}, u32[]{:S(2)}) collective-permute-start(f32[4,52,8,128]{3,2,1,0:T(8,128)S(1)} %collective-permute-done.3.refs_1_), channel_id=1, source_target_pairs={{0,128},{1,33},{32,160},{33,65},{64,192},{65,97},{96,224},{97,1},{... | collective-permute-start | bytes 2555912 | tf_op jit(solution)/shard_map/ppermute | solution.py:530
  86.6 5.0 %collective-permute-start.7 = (f32[4,52,8,128]{3,2,1,0:T(8,128)S(1)}, f32[4,52,8,128]{3,2,1,0:T(8,128)}, u32[]{:S(2)}, u32[]{:S(2)}) collective-permute-start(f32[4,52,8,128]{3,2,1,0:T(8,128)S(1)} %collective-permute-done.3.refs_1_), channel_id=1, source_target_pairs={{0,1},{1,0},{2,3},{3,2},{4,5},{5,4},{6,7},{7,6},{8,9},{9,8},{10,11... | collective-permute-start | bytes 2555912 | tf_op jit(solution)/shard_map/ppermute | solution.py:519
  91.5 1.9 %collective-permute-start.8 = (f32[4,52,8,128]{3,2,1,0:T(8,128)S(1)}, f32[4,52,8,128]{3,2,1,0:T(8,128)}, u32[]{:S(2)}, u32[]{:S(2)}) collective-permute-start(f32[4,52,8,128]{3,2,1,0:T(8,128)S(1)} %collective-permute-done.4.refs_2_), channel_id=1, source_target_pairs={{0,1},{1,0},{2,3},{3,2},{4,5},{5,4},{6,7},{7,6},{8,9},{9,8},{10,11... | collective-permute-start | bytes 2555912 | tf_op jit(solution)/shard_map/ppermute | solution.py:519
  93.5 5.0 %all-gather.3.cloned.1.call-done = f32[1792,1024]{1,0:T(8,128)} async-done(((f32[56,1024]{1,0:T(8,128)}), f32[1792,1024]{1,0:T(8,128)}) %all-gather.3.cloned.1.call-update) | async-done | bytes 7340048 | tf_op jit(solution)/shard_map/all_gather | solution.py:575
  98.5 3.8 %leaf_border.1 = f32[256,512]{1,0:T(8,128)} custom-call(s32[1]{0:T(128)S(6)} %copy.19.count_ref, f32[256,1024]{1,0:T(8,128)} %bitcast.28, f32[32,56,1024]{2,1,0:T(8,128)} %bitcast.25), custom_call_target="tpu_custom_call" | custom-call | tf_op jit(solution)/shard_map/leaf_border/pallas_call | solution.py:108
  102.2 2.2 %collective-permute-start.9 = (f32[4,52,8,128]{3,2,1,0:T(8,128)}, f32[4,52,8,128]{3,2,1,0:T(8,128)}, u32[]{:S(2)}, u32[]{:S(2)}) collective-permute-start(f32[4,52,8,128]{3,2,1,0:T(8,128)} %collective-permute-done.6.refs_3_), channel_id=1, source_target_pairs={{0,1},{1,0},{2,3},{3,2},{4,5},{5,4},{6,7},{7,6},{8,9},{9,8},{10,11... | collective-permute-start | bytes 2555912 | tf_op jit(solution)/shard_map/ppermute | solution.py:519
  104.4 6.7 %all-to-all-start.1 = ((f32[16,16,512]{2,1,0:T(8,128)}), f32[16,16,512]{2,1,0:T(8,128)S(1)}, u32[]{:S(2)}, u32[]{:S(2)}) async-start(f32[16,16,512]{2,1,0:T(8,128)} %bitcast.30), calls=%async_computation.1 | async-start | bytes 1048576 | tf_op jit(solution)/shard_map/all_to_all | solution.py:582
  111.2 0.6 broadcast_in_dim.66.index_ref
  111.8 0.6 broadcast_in_dim.67.sep_index_ref
  112.4 0.6 pad_add_fusion.place_ref
  113.1 7.0 %upper_operators.1 = (bf16[4,1024,512]{2,1,0:T(8,128)(2,1)}, bf16[4,1024,512]{2,1,0:T(8,128)(2,1)}, bf16[512,512]{1,0:T(8,128)(2,1)}, bf16[512,512]{1,0:T(8,128)(2,1)}) custom-call(s32[3]{0:T(128)} %pad_add_fusion.place_ref, f32[4,52,8,128]{3,2,1,0:T(8,128)} %copy-done.1, f32[4,52,8,128]{3,2,1,0:T(8,128)} %copy-done.5, f32[4,52,8,128]{3,2,1,0:T(8,128)} %copy-done.6, ...), custom_call_target="tpu_custom_call" | custom-call | tf_op jit(solution)/shard_map/upper_operators/pallas_call | solution.py:397
  120.1 2.0 %all-to-all-done.1.incoming_ref = f32[16,16,512]{2,1,0:T(8,128)S(1)} async-done(((f32[16,16,512]{2,1,0:T(8,128)}), f32[16,16,512]{2,1,0:T(8,128)S(1)}, u32[]{:S(2)}, u32[]{:S(2)}) %all-to-all-start.1) | async-done | bytes 524320 | tf_op jit(solution)/shard_map/all_to_all | solution.py:582
  122.0 0.8 copy-done.2
  122.8 11.1 %upper_solve.1 = (f32[16,16,512]{2,1,0:T(8,128)}, f32[4,16,512]{2,1,0:T(8,128)}, f32[16,512]{1,0:T(8,128)}) custom-call(s32[16]{0:T(128)} %parent_ref.1, f32[16,16,512]{2,1,0:T(8,128)} %copy-done.2, s32[16,1,1024]{2,1,0:T(1,128)} %broadcast_in_dim.65.slot_ref, s32[16,1,512]{2,1,0:T(1,128)} %broadcast_in_dim.66.index_ref, f32[4,16,512]{2,1,0:T(8,128)} %bitcast.34, ...), custom_call_target="tpu_custom_call" | custom-call | tf_op jit(solution)/shard_map/upper_solve/pallas_call | solution.py:488
  133.9 4.9 %all-to-all-start.2 = ((f32[16,16,512]{2,1,0:T(8,128)}), f32[16,16,512]{2,1,0:T(8,128)S(1)}, u32[]{:S(2)}, u32[]{:S(2)}) async-start(f32[16,16,512]{2,1,0:T(8,128)} %get-tuple-element.48), calls=%async_computation.2 | async-start | bytes 1048576 | tf_op jit(solution)/shard_map/all_to_all | solution.py:591
  138.8 7.1 %leaf_pivot.1 = (f32[4,256,256]{2,1,0:T(8,128)}, bf16[4,512,256]{2,1,0:T(8,128)(2,1)}, bf16[4,512,256]{2,1,0:T(8,128)(2,1)}) custom-call(s32[1]{0:T(128)S(6)} %copy.19.count_ref, f32[256,1024]{1,0:T(8,128)} %bitcast.29, f32[32,56,1024]{2,1,0:T(8,128)} %bitcast.27), custom_call_target="tpu_custom_call" | custom-call | tf_op jit(solution)/shard_map/leaf_pivot/pallas_call | solution.py:175
  145.9 0.7 copy.16
  146.6 2.2 %all-to-all-done.2 = f32[16,16,512]{2,1,0:T(8,128)S(1)} async-done(((f32[16,16,512]{2,1,0:T(8,128)}), f32[16,16,512]{2,1,0:T(8,128)S(1)}, u32[]{:S(2)}, u32[]{:S(2)}) %all-to-all-start.2) | async-done | bytes 524320 | tf_op jit(solution)/shard_map/all_to_all | solution.py:591
  148.9 0.8 copy-done.3
  149.7 5.2 %leaf_last.1 = f32[256,1024]{1,0:T(8,128)} custom-call(s32[1]{0:T(128)S(6)} %copy.19.count_ref, f32[4,256,256]{2,1,0:T(8,128)} %get-tuple-element.47.part_hbm, f32[256,512]{1,0:T(8,128)} %bitcast.31, bf16[4,512,256]{2,1,0:T(8,128)(2,1)} %get-tuple-element.49.high_hbm, bf16[4,512,256]{2,1,0:T(8,128)(2,1)} %get-tuple-element.50.low_hbm), custom_call_target="tpu_custom_call" | custom-call | tf_op jit(solution)/shard_map/leaf_last/pallas_call | solution.py:229
  (22 shorter events, 0.1 us)
Async XLA Ops:
  7.2 1.8 %copy-start = (f32[4,32,512]{2,1,0:T(8,128)S(1)}, f32[4,32,512]{2,1,0:T(8,128)}, u32[]{:S(2)}) copy-start(f32[4,32,512]{2,1,0:T(8,128)} %param.16) | copy-start | bytes 786436
  7.2 104.6 %copy-start.10 = (s32[4,512]{1,0:T(4,128)S(1)}, s32[4,512]{1,0:T(4,128)}, u32[]{:S(2)}) copy-start(s32[4,512]{1,0:T(4,128)} %param.17) | copy-start | bytes 24580
  7.2 104.0 %copy-start.8 = (s32[16,512]{1,0:T(8,128)S(1)}, s32[16,512]{1,0:T(8,128)}, u32[]{:S(2)}) copy-start(s32[16,512]{1,0:T(8,128)} %param.14) | copy-start | bytes 98308
  7.2 91.2 %all-gather.3.cloned.1.call-start = ((), (), s32[]{:S(2)}) async-start(), calls=%async_computation.3 | async-start | bytes 7569408 | tf_op jit(solution)/shard_map/all_gather | solution.py:575
  9.7 28.9 %all-to-all-start = ((f32[16,8,512]{2,1,0:T(8,128)}), f32[16,8,512]{2,1,0:T(8,128)S(1)}, u32[]{:S(2)}, u32[]{:S(2)}) async-start(f32[16,8,512]{2,1,0:T(8,128)} %broadcast_in_dim.59), calls=%async_computation | async-start | bytes 524288 | tf_op jit(solution)/shard_map/all_to_all | solution.py:542
  38.6 0.7 copy-start.4
  40.9 12.2 %collective-permute-start = (f32[52,8,128]{2,1,0:T(8,128)}, f32[52,8,128]{2,1,0:T(8,128)S(1)}, u32[]{:S(2)}, u32[]{:S(2)}) collective-permute-start(f32[52,8,128]{2,1,0:T(8,128)} %pack.1), channel_id=1, source_target_pairs={{0,32},{1,129},{32,64},{33,161},{64,96},{65,193},{96,0},{97,225},{... | collective-permute-start | bytes 638984 | tf_op jit(solution)/shard_map/ppermute | solution.py:530
  44.2 9.0 %collective-permute-start.1 = (f32[52,8,128]{2,1,0:T(8,128)}, f32[52,8,128]{2,1,0:T(8,128)S(1)}, u32[]{:S(2)}, u32[]{:S(2)}) collective-permute-start(f32[52,8,128]{2,1,0:T(8,128)} %pack.1), channel_id=1, source_target_pairs={{0,96},{1,385},{32,0},{33,417},{64,32},{65,449},{96,64},{97,481},{... | collective-permute-start | bytes 638984 | tf_op jit(solution)/shard_map/ppermute | solution.py:530
  47.5 8.3 %collective-permute-start.2 = (f32[52,8,128]{2,1,0:T(8,128)}, f32[52,8,128]{2,1,0:T(8,128)S(1)}, u32[]{:S(2)}, u32[]{:S(2)}) collective-permute-start(f32[52,8,128]{2,1,0:T(8,128)} %pack.1), channel_id=1, source_target_pairs={{0,64},{1,257},{32,96},{33,289},{64,0},{65,321},{96,32},{97,353},{... | collective-permute-start | bytes 638984 | tf_op jit(solution)/shard_map/ppermute | solution.py:530
  56.8 56.2 %copy-start.1 = (f32[4,52,8,128]{3,2,1,0:T(8,128)}, f32[4,52,8,128]{3,2,1,0:T(8,128)S(1)}, u32[]{:S(2)}) copy-start(f32[4,52,8,128]{3,2,1,0:T(8,128)S(1)} %pad_maximum_fusion.refs_0_) | copy-start | bytes 2555908
  56.8 27.1 %collective-permute-start.3 = (f32[4,52,8,128]{3,2,1,0:T(8,128)S(1)}, f32[4,52,8,128]{3,2,1,0:T(8,128)S(1)}, u32[]{:S(2)}, u32[]{:S(2)}) collective-permute-start(f32[4,52,8,128]{3,2,1,0:T(8,128)S(1)} %pad_maximum_fusion.refs_0_), channel_id=1, source_target_pairs={{0,128},{1,33},{32,160},{33,65},{64,192},{65,97},{96,224},{97,1},{... | collective-permute-start | bytes 2555912 | tf_op jit(solution)/shard_map/ppermute | solution.py:530
  60.0 24.0 %collective-permute-start.4 = (f32[4,52,8,128]{3,2,1,0:T(8,128)S(1)}, f32[4,52,8,128]{3,2,1,0:T(8,128)S(1)}, u32[]{:S(2)}, u32[]{:S(2)}) collective-permute-start(f32[4,52,8,128]{3,2,1,0:T(8,128)S(1)} %pad_maximum_fusion.refs_0_), channel_id=1, source_target_pairs={{0,384},{1,97},{32,416},{33,1},{64,448},{65,33},{96,480},{97,65},{... | collective-permute-start | bytes 2555912 | tf_op jit(solution)/shard_map/ppermute | solution.py:530
  63.3 20.7 %collective-permute-start.5 = (f32[4,52,8,128]{3,2,1,0:T(8,128)S(1)}, f32[4,52,8,128]{3,2,1,0:T(8,128)S(1)}, u32[]{:S(2)}, u32[]{:S(2)}) collective-permute-start(f32[4,52,8,128]{3,2,1,0:T(8,128)S(1)} %pad_maximum_fusion.refs_0_), channel_id=1, source_target_pairs={{0,1},{1,0},{2,3},{3,2},{4,5},{5,4},{6,7},{7,6},{8,9},{9,8},{10,11... | collective-permute-start | bytes 2555912 | tf_op jit(solution)/shard_map/ppermute | solution.py:519
  84.0 29.1 %copy-start.5 = (f32[4,52,8,128]{3,2,1,0:T(8,128)}, f32[4,52,8,128]{3,2,1,0:T(8,128)S(1)}, u32[]{:S(2)}) copy-start(f32[4,52,8,128]{3,2,1,0:T(8,128)S(1)} %collective-permute-done.3.refs_1_) | copy-start | bytes 2555908
  84.0 29.1 %copy-start.6 = (f32[4,52,8,128]{3,2,1,0:T(8,128)}, f32[4,52,8,128]{3,2,1,0:T(8,128)S(1)}, u32[]{:S(2)}) copy-start(f32[4,52,8,128]{3,2,1,0:T(8,128)S(1)} %collective-permute-done.4.refs_2_) | copy-start | bytes 2555908
  84.0 2.6 %copy-start.7 = (f32[4,52,8,128]{3,2,1,0:T(8,128)}, f32[4,52,8,128]{3,2,1,0:T(8,128)S(1)}, u32[]{:S(2)}) copy-start(f32[4,52,8,128]{3,2,1,0:T(8,128)S(1)} %collective-permute-done.5.refs_4_) | copy-start | bytes 2555908
  84.0 18.2 %collective-permute-start.6 = (f32[4,52,8,128]{3,2,1,0:T(8,128)S(1)}, f32[4,52,8,128]{3,2,1,0:T(8,128)}, u32[]{:S(2)}, u32[]{:S(2)}) collective-permute-start(f32[4,52,8,128]{3,2,1,0:T(8,128)S(1)} %collective-permute-done.3.refs_1_), channel_id=1, source_target_pairs={{0,128},{1,33},{32,160},{33,65},{64,192},{65,97},{96,224},{97,1},{... | collective-permute-start | bytes 2555912 | tf_op jit(solution)/shard_map/ppermute | solution.py:530
  86.6 26.4 %collective-permute-start.7 = (f32[4,52,8,128]{3,2,1,0:T(8,128)S(1)}, f32[4,52,8,128]{3,2,1,0:T(8,128)}, u32[]{:S(2)}, u32[]{:S(2)}) collective-permute-start(f32[4,52,8,128]{3,2,1,0:T(8,128)S(1)} %collective-permute-done.3.refs_1_), channel_id=1, source_target_pairs={{0,1},{1,0},{2,3},{3,2},{4,5},{5,4},{6,7},{7,6},{8,9},{9,8},{10,11... | collective-permute-start | bytes 2555912 | tf_op jit(solution)/shard_map/ppermute | solution.py:519
  91.5 21.5 %collective-permute-start.8 = (f32[4,52,8,128]{3,2,1,0:T(8,128)S(1)}, f32[4,52,8,128]{3,2,1,0:T(8,128)}, u32[]{:S(2)}, u32[]{:S(2)}) collective-permute-start(f32[4,52,8,128]{3,2,1,0:T(8,128)S(1)} %collective-permute-done.4.refs_2_), channel_id=1, source_target_pairs={{0,1},{1,0},{2,3},{3,2},{4,5},{5,4},{6,7},{7,6},{8,9},{9,8},{10,11... | collective-permute-start | bytes 2555912 | tf_op jit(solution)/shard_map/ppermute | solution.py:519
  102.2 10.8 %collective-permute-start.9 = (f32[4,52,8,128]{3,2,1,0:T(8,128)}, f32[4,52,8,128]{3,2,1,0:T(8,128)}, u32[]{:S(2)}, u32[]{:S(2)}) collective-permute-start(f32[4,52,8,128]{3,2,1,0:T(8,128)} %collective-permute-done.6.refs_3_), channel_id=1, source_target_pairs={{0,1},{1,0},{2,3},{3,2},{4,5},{5,4},{6,7},{7,6},{8,9},{9,8},{10,11... | collective-permute-start | bytes 2555912 | tf_op jit(solution)/shard_map/ppermute | solution.py:519
  104.4 17.6 %all-to-all-start.1 = ((f32[16,16,512]{2,1,0:T(8,128)}), f32[16,16,512]{2,1,0:T(8,128)S(1)}, u32[]{:S(2)}, u32[]{:S(2)}) async-start(f32[16,16,512]{2,1,0:T(8,128)} %bitcast.30), calls=%async_computation.1 | async-start | bytes 1048576 | tf_op jit(solution)/shard_map/all_to_all | solution.py:582
  122.0 0.8 copy-start.2
  133.9 12.0 %copy-start.9 = (f32[4,16,512]{2,1,0:T(8,128)S(1)}, f32[4,16,512]{2,1,0:T(8,128)}, u32[]{:S(2)}) copy-start(f32[4,16,512]{2,1,0:T(8,128)} %get-tuple-element.51) | copy-start | bytes 393220
  133.9 15.0 %all-to-all-start.2 = ((f32[16,16,512]{2,1,0:T(8,128)}), f32[16,16,512]{2,1,0:T(8,128)S(1)}, u32[]{:S(2)}, u32[]{:S(2)}) async-start(f32[16,16,512]{2,1,0:T(8,128)} %get-tuple-element.48), calls=%async_computation.2 | async-start | bytes 1048576 | tf_op jit(solution)/shard_map/all_to_all | solution.py:591
  148.9 0.8 copy-start.3
Sparse Core Ops, SparseCore 0:
  10.2 88.2 all-gather.2

commit v4 on v3

--- a/solution.py
+++ b/solution.py
@@ -88,20 +88,20 @@
 
 
 def leaf_border_kernel(count_ref, rhs_hbm, line_ref, border_ref, rhs_ref, buffer, sem, rhs_sem):
-    copy = leaf_copy(line_ref, buffer, 21, 11, sem)
+    copies = [
+        leaf_copy(line_ref, buffer.at[pl.ds(0, 6)], 21, 6, sem.at[0]),
+        leaf_copy(line_ref, buffer.at[pl.ds(6, 5)], 27, 5, sem.at[1]),
+    ]
     load = pltpu.make_async_copy(rhs_hbm, rhs_ref, rhs_sem)
     load.start()
-    copy.start()
+    start_all(copies)
     load.wait()
     cols = lax.broadcasted_iota(jnp.int32, rhs_ref.shape, 1)
     rhs = stack2(split2(jnp.where(cols < count_ref[0], rhs_ref[...], 0.0)))
-    copy.wait()
-    rows = buffer[...].reshape(528, 1024)
     for block in range(2):
-        first = 16 + 256 * block
-        border_ref[:, 256 * block : 256 * (block + 1)] = stacked_products(
-            dot_nt, rhs, split2(rows[first : first + 256])
-        )
+        copies[block].wait()
+        rows = buffer[5 * block : 5 * block + 6].reshape(288, 1024)[16 * (block + 1) : 16 * (block + 1) + 256]
+        border_ref[:, 256 * block : 256 * (block + 1)] = stacked_products(dot_nt, rhs, split2(rows))
 
 
 def leaf_border(count, rhs, line):
@@ -113,7 +113,7 @@
         scratch_shapes=[
             pltpu.VMEM((256, 1024), F32),
             pltpu.VMEM((11, 48, 1024), F32),
-            pltpu.SemaphoreType.DMA,
+            pltpu.SemaphoreType.DMA((2,)),
             pltpu.SemaphoreType.DMA,
         ],
         compiler_params=params(60),
@@ -199,9 +199,11 @@
 
 
 def leaf_last_kernel(
-    count_ref, part_hbm, border_ref, high_hbm, low_hbm, out_hbm,
-    part_ref, high_ref, low_ref, out_ref, sem, out_sem,
+    count_ref, part_hbm, border_hbm, high_hbm, low_hbm, out_hbm,
+    part_ref, border_ref, high_ref, low_ref, out_ref, sem, border_sem, out_sem,
 ):
+    load = pltpu.make_async_copy(border_hbm, border_ref, border_sem)
+    load.start()
     copies = [
         [
             pltpu.make_async_copy(source.at[block], to.at[block], sem.at[block, at])
@@ -211,6 +213,7 @@
     ]
     for group in copies:
         start_all(group)
+    load.wait()
     border = stack2(split2(border_ref[...]))
     stores = []
     for block in range(4):
@@ -229,17 +232,19 @@
     return pl.pallas_call(
         leaf_last_kernel,
         out_shape=jax.ShapeDtypeStruct((256, 1024), F32),
-        in_specs=[full_smem(), in_hbm(), full_vmem(), in_hbm(), in_hbm()],
+        in_specs=[full_smem()] + [in_hbm()] * 4,
         out_specs=in_hbm(),
         scratch_shapes=[
             pltpu.VMEM((4, 256, 256), F32),
+            pltpu.VMEM((256, 512), F32),
             pltpu.VMEM((4, 512, 256), BF16),
             pltpu.VMEM((4, 512, 256), BF16),
             pltpu.VMEM((4, 256, 256), F32),
             pltpu.SemaphoreType.DMA((4, 3)),
+            pltpu.SemaphoreType.DMA,
             pltpu.SemaphoreType.DMA((4,)),
         ],
-        compiler_params=params(59),
+        compiler_params=params(60),
         name="leaf_last",
     )(count, part, border, high, low)
 
@@ -421,11 +426,25 @@
 
 
 def upper_kernel(
-    parent_ref, incoming_ref, slot_ref, index_ref, sep_rhs_ref, sep_slot_ref, sep_index_ref, root_rhs_ref,
+    parent_ref, incoming_hbm, slot_hbm, index_hbm, sep_rhs_hbm, sep_slot_hbm, sep_index_hbm, root_rhs_hbm,
     high_hbm, low_hbm, root_high_hbm, root_low_hbm,
     down_ref, sep_out_ref, root_out_ref,
-    updates, solved, full, high_ref, low_ref, root_high_ref, root_low_ref, sem,
+    incoming_ref, slot_ref, index_ref, sep_rhs_ref, sep_slot_ref, sep_index_ref, root_rhs_ref,
+    updates, solved, full, high_ref, low_ref, root_high_ref, root_low_ref, first_sem, sem,
 ):
+    first_loads = [
+        pltpu.make_async_copy(slot_hbm, slot_ref, first_sem.at[0]),
+        pltpu.make_async_copy(incoming_hbm.at[pl.ds(0, 4)], incoming_ref.at[pl.ds(0, 4)], first_sem.at[1]),
+        pltpu.make_async_copy(incoming_hbm.at[pl.ds(4, 12)], incoming_ref.at[pl.ds(4, 12)], first_sem.at[2]),
+    ]
+    small_loads = [
+        pltpu.make_async_copy(source, to, first_sem.at[3 + at])
+        for at, (source, to) in enumerate((
+            (sep_rhs_hbm, sep_rhs_ref), (sep_slot_hbm, sep_slot_ref), (root_rhs_hbm, root_rhs_ref),
+            (sep_index_hbm, sep_index_ref), (index_hbm, index_ref),
+        ))
+    ]
+    start_all(first_loads + small_loads)
     loads = []
     for sep in range(4):
         loads.append([
@@ -442,42 +461,40 @@
 
     def spread(leaf, _):
         to = parent_ref[leaf]
-        picked = pick(blocks(incoming_ref[leaf]), slot_ref[leaf])
+        picked = pick(blocks(incoming_ref[leaf]), slot_ref[pl.ds(leaf, 1), :])
         for at, value in enumerate(picked):
             part = slice(at * LANES, (at + 1) * LANES)
             updates[to, :, part] = updates[to, :, part] + value
         return 0
 
-    lax.fori_loop(0, 16, spread, 0, unroll=4)
+    wait_all(first_loads[:2])
+    lax.fori_loop(0, 4, spread, 0, unroll=4)
+    first_loads[2].wait()
+    lax.fori_loop(4, 16, spread, 0, unroll=4)
+    wait_all(small_loads)
     root_total = root_rhs_ref[...]
     for sep in range(4):
         wait_all(loads[sep])
         pivot = stack2(split2(sep_rhs_ref[sep] + updates[sep, :, :512]))
-        solved[sep, :, :256] = stacked_products(
-            dot_nt, pivot[:, :256], (high_ref[sep, :256, :256], low_ref[sep, :256, :256])
-        )
-        forward = stacked_products(dot_nt, pivot, (high_ref[sep, 256:], low_ref[sep, 256:]))
-        solved[sep, :, 256:] = forward[:, :256]
-        border = forward[:, 256:] + updates[sep, :, 512:]
-        root_total = root_total + jnp.concatenate(pick(blocks(border), sep_slot_ref[sep]), axis=1)
+        forward = stacked_products(dot_nt, pivot, (high_ref[sep], low_ref[sep]))
+        solved[sep] = forward[:, :512]
+        border = forward[:, 512:] + updates[sep, :, 512:]
+        root_total = root_total + jnp.concatenate(pick(blocks(border), sep_slot_ref[sep : sep + 1, :]), axis=1)
     wait_all(loads[4])
     root = (root_high_ref[...], root_low_ref[...])
     root_solved = stacked_products(dot_nt, stack2(split2(root_total)), root)
     root_answer = stacked_products(dot_nn, stack2(split2(root_solved)), root)
     root_out_ref[...] = root_answer
     for sep in range(4):
-        border = jnp.concatenate(pick(blocks(root_answer), sep_index_ref[sep]), axis=1)
+        border = jnp.concatenate(pick(blocks(root_answer), sep_index_ref[sep : sep + 1, :]), axis=1)
         joined = stack2(split2(jnp.concatenate([solved[sep], border], axis=1)))
-        left = stacked_products(dot_nn, joined, (high_ref[sep, :, :256], low_ref[sep, :, :256]))
-        right = stacked_products(dot_nn, joined[:, 256:], (high_ref[sep, 256:, 256:], low_ref[sep, 256:, 256:]))
-        sep_out_ref[sep, :, :256] = left
-        sep_out_ref[sep, :, 256:] = right
-        full[sep, :, :256] = left
-        full[sep, :, 256:512] = right
+        answer = stacked_products(dot_nn, joined, (high_ref[sep], low_ref[sep]))
+        sep_out_ref[sep] = answer
+        full[sep, :, :512] = answer
         full[sep, :, 512:] = border
 
     def gather(leaf, _):
-        picked = pick(blocks(full[parent_ref[leaf]]), index_ref[leaf])
+        picked = pick(blocks(full[parent_ref[leaf]]), index_ref[pl.ds(leaf, 1), :])
         down_ref[leaf] = jnp.concatenate(picked, axis=1)
         return 0
 
@@ -492,9 +509,16 @@
             jax.ShapeDtypeStruct((4, 16, 512), F32),
             jax.ShapeDtypeStruct((16, 512), F32),
         ),
-        in_specs=[full_smem()] + [full_vmem()] * 7 + [in_hbm()] * 4,
+        in_specs=[full_smem()] + [in_hbm()] * 11,
         out_specs=(full_vmem(),) * 3,
         scratch_shapes=[
+            pltpu.VMEM((16, 16, 512), F32),
+            pltpu.VMEM((16, 1024), jnp.int32),
+            pltpu.VMEM((16, 512), jnp.int32),
+            pltpu.VMEM((4, 16, 512), F32),
+            pltpu.VMEM((4, 512), jnp.int32),
+            pltpu.VMEM((4, 512), jnp.int32),
+            pltpu.VMEM((16, 512), F32),
             pltpu.VMEM((4, 16, 1024), F32),
             pltpu.VMEM((4, 16, 512), F32),
             pltpu.VMEM((4, 16, 1024), F32),
@@ -502,6 +526,7 @@
             pltpu.VMEM((4, 1024, 512), BF16),
             pltpu.VMEM((512, 512), BF16),
             pltpu.VMEM((512, 512), BF16),
+            pltpu.SemaphoreType.DMA((8,)),
             pltpu.SemaphoreType.DMA((5, 2)),
         ],
         compiler_params=params(60),
@@ -567,8 +592,8 @@
     root_factor,
 ):
     rhs = leaf_rhs[0]
-    slots = inverse_rows(leaf_index, 1024)[:, None, :]
-    sep_slots = inverse_rows(separator_index, 512)[:, None, :]
+    slots = inverse_rows(leaf_index, 1024)
+    sep_slots = inverse_rows(separator_index, 512)
     sep_rhs = jnp.transpose(separator_rhs[0], (1, 0, 2))
     y, x, c = lax.axis_index("y"), lax.axis_index("x"), lax.axis_index("c")
     place = jnp.stack([y, x, c]).astype(jnp.int32)
@@ -584,8 +609,8 @@
     )
     operators = upper_operators(place, own_set, other_set, line)
     down, sep_answer, root_answer = upper_solve(
-        parent, incoming, slots, leaf_index[:, None, :], sep_rhs, sep_slots,
-        separator_index[:, None, :], root_rhs[0], operators,
+        parent, incoming, slots, leaf_index, sep_rhs, sep_slots,
+        separator_index, root_rhs[0], operators,
     )
     line, down = lax.optimization_barrier((line, down))
     received = lax.all_to_all(down, ("y", "x"), split_axis=0, concat_axis=0, tiled=True)

time: 163 us -> 163 us (level)
  starting transfers between devices: 68.2 us -> 63.9 us
  waiting for transfers between devices: 23.4 us -> 26.9 us
  Pallas kernels: 37.4 us -> 39.1 us
    ppermute x6, waiting for transfers between devices: 2.7 us -> 7.96 us  [along_plane(): return lax.ppermute(value, ('y', 'x', 'c'), pairs)]
    broadcast_in_dim x4 -> x0, local copies, waits for them, and re-layouts: 2.48 us -> none  [the longest x1 0.66 us: local(): slots = inverse_rows(leaf_index, 1024)[:, None, :]]
    all_gather x1, waiting for transfers between devices: 4.97 us -> 2.98 us  [local(): lax.all_gather(join(leaf_factor[0], root_factor), ('z', 'c'), axis=0, til...]
    all_to_all x1, starting transfers between devices: 6.74 us -> 4.98 us  [local(): lax.all_to_all(border.reshape(16, 16, 512), ('y', 'x'), split_axis=0, con...]
    unnamed x24 -> x16, local copies, waits for them, and re-layouts: 4.7 us -> 5.57 us
  transfers between devices with their start and end apart: 14 -> 14, of which waited for: 5 -> 7; matrix products, arithmetic and copies ran while one was open for 10% -> 9% of each run, Pallas kernels for 12% -> 13%
where the time goes in v4:
time: 163 us; the launch traced here: 162 us
  starting transfers between devices  63.9 us (39%)
  Pallas kernels  39.1 us (24%)
  waiting for transfers between devices  26.9 us (17%)
  between operations  14.9 us (9%)
  other arithmetic  11 us (7%)
  local copies, waits for them, and re-layouts  6.31 us (4%)
    ppermute x4, starting transfers between devices, swap_cores(): return lax.ppermute(value, 'c', [(0, 1), (1, 0)])  21.8 us
    ppermute x6, starting transfers between devices, along_plane(): return lax.ppermute(value, ('y', 'x', 'c'), pairs)  17.5 us
    all_to_all x1, starting transfers between devices, gather_line(): lax.all_to_all(jnp.broadcast_to(mine, (NZ, 8, 512)), 'z', split_axis=0, c...  15.7 us
    pallas_call x1, Pallas kernels, upper_solve(): pl.pallas_call(upper_kernel, out_shape=(jax.ShapeDtypeStruct((16, 16, 512...  12 us
    all_to_all x1, waiting for transfers between devices, gather_line(): lax.all_to_all(jnp.broadcast_to(mine, (NZ, 8, 512)), 'z', split_axis=0, c...  11.5 us
    reduce_max x2, other arithmetic, inverse_rows(): return jnp.max(jnp.where(index[:, :, None] == slot, place, -1), axis=1)  9.43 us
    ppermute x6, waiting for transfers between devices, along_plane(): return lax.ppermute(value, ('y', 'x', 'c'), pairs)  7.96 us
    pallas_call x1, Pallas kernels, leaf_pivot(): pl.pallas_call(leaf_pivot_kernel, out_shape=(jax.ShapeDtypeStruct((4, 256...  7.04 us
  transfers between devices with their start and end apart: 14, of which 7 were waited for; matrix products, arithmetic and copies ran while one was open for 9% of the time, Pallas kernels for 13%

profile of v4, /device:TPU:1, one launch (start us, length us, event | category | flops | bytes accessed | tf_op | source)
XLA Modules:
  0.0 162.2 jit_solution(3481763304364882002)
XLA Ops:
  7.2 0.0 copy-start
  7.2 0.0 all-gather.3.cloned.1.call-start
  7.2 1.7 %join.1 = f32[56,1024]{1,0:T(8,128)} custom-call(f32[48,1024]{1,0:T(8,128)} %bitcast.38, f32[16,512]{1,0:T(8,128)} %root_ref.1), custom_call_target="tpu_custom_call" | custom-call | tf_op jit(solution)/shard_map/join/pallas_call | solution.py:76
  8.9 0.0 all-gather.3.cloned.1.call-update
  8.9 0.7 broadcast_in_dim.47
  9.7 15.7 %all-to-all-start = ((f32[16,8,512]{2,1,0:T(8,128)}), f32[16,8,512]{2,1,0:T(8,128)S(1)}, u32[]{:S(2)}, u32[]{:S(2)}) async-start(f32[16,8,512]{2,1,0:T(8,128)} %broadcast_in_dim.47), calls=%async_computation | async-start | bytes 524288 | tf_op jit(solution)/shard_map/all_to_all | solution.py:567
  25.4 1.6 copy.18
  27.0 11.5 %all-to-all-done.line_ref = f32[16,8,512]{2,1,0:T(8,128)S(1)} async-done(((f32[16,8,512]{2,1,0:T(8,128)}), f32[16,8,512]{2,1,0:T(8,128)S(1)}, u32[]{:S(2)}, u32[]{:S(2)}) %all-to-all-start) | async-done | bytes 262176 | tf_op jit(solution)/shard_map/all_to_all | solution.py:567
  38.6 0.7 copy-done.4
  39.3 1.7 %pack.1 = f32[52,8,128]{2,1,0:T(8,128)} custom-call(f32[16,8,512]{2,1,0:T(8,128)} %copy-done.4), custom_call_target="tpu_custom_call" | custom-call | tf_op jit(solution)/shard_map/pack/pallas_call | solution.py:300
  40.9 4.8 %collective-permute-start.2 = (f32[52,8,128]{2,1,0:T(8,128)}, f32[52,8,128]{2,1,0:T(8,128)S(1)}, u32[]{:S(2)}, u32[]{:S(2)}) collective-permute-start(f32[52,8,128]{2,1,0:T(8,128)} %pack.1), channel_id=1, source_target_pairs={{0,64},{1,257},{32,96},{33,289},{64,0},{65,321},{96,32},{97,353},{... | collective-permute-start | bytes 638984 | tf_op jit(solution)/shard_map/ppermute | solution.py:555
  45.7 2.7 %collective-permute-start.1 = (f32[52,8,128]{2,1,0:T(8,128)}, f32[52,8,128]{2,1,0:T(8,128)S(1)}, u32[]{:S(2)}, u32[]{:S(2)}) collective-permute-start(f32[52,8,128]{2,1,0:T(8,128)} %pack.1), channel_id=1, source_target_pairs={{0,96},{1,385},{32,0},{33,417},{64,32},{65,449},{96,64},{97,481},{... | collective-permute-start | bytes 638984 | tf_op jit(solution)/shard_map/ppermute | solution.py:555
  48.4 2.6 %collective-permute-start = (f32[52,8,128]{2,1,0:T(8,128)}, f32[52,8,128]{2,1,0:T(8,128)S(1)}, u32[]{:S(2)}, u32[]{:S(2)}) collective-permute-start(f32[52,8,128]{2,1,0:T(8,128)} %pack.1), channel_id=1, source_target_pairs={{0,32},{1,129},{32,64},{33,161},{64,96},{65,193},{96,0},{97,225},{... | collective-permute-start | bytes 638984 | tf_op jit(solution)/shard_map/ppermute | solution.py:555
  51.0 2.0 %select_reduce_fusion.1.sep_slot_hbm = s32[4,512]{1,0:T(4,128)} fusion(s32[4,512]{1,0:T(4,128)} %sep_index_hbm.1), kind=kLoop, calls=%fused_computation.2 | loop fusion | flops 3143680 | bytes 16384 | tf_op jit(solution)/shard_map/reduce_max | solution.py:540
  53.1 0.0 collective-permute-done.2
  53.1 0.0 collective-permute-done.1
  53.1 3.7 %collective-permute-done = f32[52,8,128]{2,1,0:T(8,128)S(1)} collective-permute-done((f32[52,8,128]{2,1,0:T(8,128)}, f32[52,8,128]{2,1,0:T(8,128)S(1)}, u32[]{:S(2)}, u32[]{:S(2)}) %collective-permute-start) | collective-permute-done | bytes 213024 | tf_op jit(solution)/shard_map/ppermute | solution.py:555
  56.7 1.0 pad_maximum_fusion.refs_0_
  57.7 0.0 copy-start.1
  57.8 10.5 %collective-permute-start.5 = (f32[4,52,8,128]{3,2,1,0:T(8,128)S(1)}, f32[4,52,8,128]{3,2,1,0:T(8,128)S(1)}, u32[]{:S(2)}, u32[]{:S(2)}) collective-permute-start(f32[4,52,8,128]{3,2,1,0:T(8,128)S(1)} %pad_maximum_fusion.refs_0_), channel_id=1, source_target_pairs={{0,1},{1,0},{2,3},{3,2},{4,5},{5,4},{6,7},{7,6},{8,9},{9,8},{10,11... | collective-permute-start | bytes 2555912 | tf_op jit(solution)/shard_map/ppermute | solution.py:544
  68.3 1.9 %collective-permute-start.4 = (f32[4,52,8,128]{3,2,1,0:T(8,128)S(1)}, f32[4,52,8,128]{3,2,1,0:T(8,128)S(1)}, u32[]{:S(2)}, u32[]{:S(2)}) collective-permute-start(f32[4,52,8,128]{3,2,1,0:T(8,128)S(1)} %pad_maximum_fusion.refs_0_), channel_id=1, source_target_pairs={{0,384},{1,97},{32,416},{33,1},{64,448},{65,33},{96,480},{97,65},{... | collective-permute-start | bytes 2555912 | tf_op jit(solution)/shard_map/ppermute | solution.py:555
  70.2 3.4 %collective-permute-start.3 = (f32[4,52,8,128]{3,2,1,0:T(8,128)S(1)}, f32[4,52,8,128]{3,2,1,0:T(8,128)}, u32[]{:S(2)}, u32[]{:S(2)}) collective-permute-start(f32[4,52,8,128]{3,2,1,0:T(8,128)S(1)} %pad_maximum_fusion.refs_0_), channel_id=1, source_target_pairs={{0,128},{1,33},{32,160},{33,65},{64,192},{65,97},{96,224},{97,1},{... | collective-permute-start | bytes 2555912 | tf_op jit(solution)/shard_map/ppermute | solution.py:555
  73.6 7.4 %select_reduce_fusion.slot_hbm = s32[16,1024]{1,0:T(8,128)} fusion(s32[16,512]{1,0:T(8,128)} %index_hbm.1), kind=kLoop, calls=%fused_computation | loop fusion | flops 25149440 | bytes 98304 | tf_op jit(solution)/shard_map/reduce_max | solution.py:540
  81.0 0.0 collective-permute-done.5.refs_4_
  81.0 1.1 collective-permute-done.4.refs_2_
  82.1 3.1 %collective-permute-done.3.refs_1_ = f32[4,52,8,128]{3,2,1,0:T(8,128)} collective-permute-done((f32[4,52,8,128]{3,2,1,0:T(8,128)S(1)}, f32[4,52,8,128]{3,2,1,0:T(8,128)}, u32[]{:S(2)}, u32[]{:S(2)}) %collective-permute-start.3) | collective-permute-done | bytes 852000 | tf_op jit(solution)/shard_map/ppermute | solution.py:555
  85.3 2.1 %collective-permute-start.6 = (f32[4,52,8,128]{3,2,1,0:T(8,128)}, f32[4,52,8,128]{3,2,1,0:T(8,128)}, u32[]{:S(2)}, u32[]{:S(2)}) collective-permute-start(f32[4,52,8,128]{3,2,1,0:T(8,128)} %collective-permute-done.3.refs_1_), channel_id=1, source_target_pairs={{0,128},{1,33},{32,160},{33,65},{64,192},{65,97},{96,224},{97,1},{... | collective-permute-start | bytes 2555912 | tf_op jit(solution)/shard_map/ppermute | solution.py:555
  88.1 5.5 %collective-permute-start.7 = (f32[4,52,8,128]{3,2,1,0:T(8,128)}, f32[4,52,8,128]{3,2,1,0:T(8,128)}, u32[]{:S(2)}, u32[]{:S(2)}) collective-permute-start(f32[4,52,8,128]{3,2,1,0:T(8,128)} %collective-permute-done.3.refs_1_), channel_id=1, source_target_pairs={{0,1},{1,0},{2,3},{3,2},{4,5},{5,4},{6,7},{7,6},{8,9},{9,8},{10,11... | collective-permute-start | bytes 2555912 | tf_op jit(solution)/shard_map/ppermute | solution.py:544
  93.6 1.9 %collective-permute-start.8 = (f32[4,52,8,128]{3,2,1,0:T(8,128)S(1)}, f32[4,52,8,128]{3,2,1,0:T(8,128)}, u32[]{:S(2)}, u32[]{:S(2)}) collective-permute-start(f32[4,52,8,128]{3,2,1,0:T(8,128)S(1)} %collective-permute-done.4.refs_2_), channel_id=1, source_target_pairs={{0,1},{1,0},{2,3},{3,2},{4,5},{5,4},{6,7},{7,6},{8,9},{9,8},{10,11... | collective-permute-start | bytes 2555912 | tf_op jit(solution)/shard_map/ppermute | solution.py:544
  95.5 3.0 %all-gather.3.cloned.1.call-done = f32[1792,1024]{1,0:T(8,128)} async-done(((f32[56,1024]{1,0:T(8,128)}), f32[1792,1024]{1,0:T(8,128)}) %all-gather.3.cloned.1.call-update) | async-done | bytes 7340048 | tf_op jit(solution)/shard_map/all_gather | solution.py:600
  98.5 4.7 %leaf_border.1 = f32[256,512]{1,0:T(8,128)} custom-call(s32[1]{0:T(128)S(6)} %copy.19.count_ref, f32[256,1024]{1,0:T(8,128)} %bitcast.28, f32[32,56,1024]{2,1,0:T(8,128)} %bitcast.25), custom_call_target="tpu_custom_call" | custom-call | tf_op jit(solution)/shard_map/leaf_border/pallas_call | solution.py:108
  103.2 0.0 collective-permute-done.6.refs_3_
  103.2 3.9 %collective-permute-start.9 = (f32[4,52,8,128]{3,2,1,0:T(8,128)}, f32[4,52,8,128]{3,2,1,0:T(8,128)}, u32[]{:S(2)}, u32[]{:S(2)}) collective-permute-start(f32[4,52,8,128]{3,2,1,0:T(8,128)} %collective-permute-done.6.refs_3_), channel_id=1, source_target_pairs={{0,1},{1,0},{2,3},{3,2},{4,5},{5,4},{6,7},{7,6},{8,9},{9,8},{10,11... | collective-permute-start | bytes 2555912 | tf_op jit(solution)/shard_map/ppermute | solution.py:544
  107.1 5.0 %all-to-all-start.1 = ((f32[16,16,512]{2,1,0:T(8,128)}), f32[16,16,512]{2,1,0:T(8,128)S(1)}, u32[]{:S(2)}, u32[]{:S(2)}) async-start(f32[16,16,512]{2,1,0:T(8,128)} %bitcast.30), calls=%async_computation.1 | async-start | bytes 1048576 | tf_op jit(solution)/shard_map/all_to_all | solution.py:607
  112.1 0.6 pad_add_fusion.place_ref
  112.7 0.0 collective-permute-done.8.refs_6_
  112.7 0.0 collective-permute-done.7.refs_5_
  112.7 0.0 collective-permute-done.9.refs_7_
  112.8 7.0 %upper_operators.1 = (bf16[4,1024,512]{2,1,0:T(8,128)(2,1)}, bf16[4,1024,512]{2,1,0:T(8,128)(2,1)}, bf16[512,512]{1,0:T(8,128)(2,1)}, bf16[512,512]{1,0:T(8,128)(2,1)}) custom-call(s32[3]{0:T(128)} %pad_add_fusion.place_ref, f32[4,52,8,128]{3,2,1,0:T(8,128)} %copy-done.1, f32[4,52,8,128]{3,2,1,0:T(8,128)} %collective-permute-done.3.refs_1_, ...), custom_call_target="tpu_custom_call" | custom-call | tf_op jit(solution)/shard_map/upper_operators/pallas_call | solution.py:402
  119.7 3.2 %all-to-all-done.1.incoming_hbm = f32[16,16,512]{2,1,0:T(8,128)S(1)} async-done(((f32[16,16,512]{2,1,0:T(8,128)}), f32[16,16,512]{2,1,0:T(8,128)S(1)}, u32[]{:S(2)}, u32[]{:S(2)}) %all-to-all-start.1) | async-done | bytes 524320 | tf_op jit(solution)/shard_map/all_to_all | solution.py:607
  123.0 0.8 copy-done.2
  123.7 12.0 %upper_solve.1 = (f32[16,16,512]{2,1,0:T(8,128)}, f32[4,16,512]{2,1,0:T(8,128)}, f32[16,512]{1,0:T(8,128)}) custom-call(s32[16]{0:T(128)} %parent_ref.1, f32[16,16,512]{2,1,0:T(8,128)} %copy-done.2, s32[16,1024]{1,0:T(8,128)} %select_reduce_fusion.slot_hbm, s32[16,512]{1,0:T(8,128)} %index_hbm.1, f32[4,16,512]{2,1,0:T(8,128)} %bitcast.34, ...), custom_call_target="tpu_custom_call" | custom-call | tf_op jit(solution)/shard_map/upper_solve/pallas_call | solution.py:505
  135.8 3.8 %all-to-all-start.2 = ((f32[16,16,512]{2,1,0:T(8,128)}), f32[16,16,512]{2,1,0:T(8,128)S(1)}, u32[]{:S(2)}, u32[]{:S(2)}) async-start(f32[16,16,512]{2,1,0:T(8,128)} %get-tuple-element.48), calls=%async_computation.2 | async-start | bytes 1048576 | tf_op jit(solution)/shard_map/all_to_all | solution.py:616
  139.6 1.6 %copy.16 = f32[1,16,4,512]{3,2,1,0:T(4,128)} copy(f32[1,16,4,512]{3,1,2,0:T(8,128)} %bitcast.39) | data formatting | bytes 262144
  141.2 7.0 %leaf_pivot.1 = (f32[4,256,256]{2,1,0:T(8,128)}, bf16[4,512,256]{2,1,0:T(8,128)(2,1)}, bf16[4,512,256]{2,1,0:T(8,128)(2,1)}) custom-call(s32[1]{0:T(128)S(6)} %copy.19.count_ref, f32[256,1024]{1,0:T(8,128)} %bitcast.29, f32[32,56,1024]{2,1,0:T(8,128)} %bitcast.27), custom_call_target="tpu_custom_call" | custom-call | tf_op jit(solution)/shard_map/leaf_pivot/pallas_call | solution.py:175
  148.3 1.2 all-to-all-done.2
  149.4 0.8 copy-done.3
  150.2 5.1 %leaf_last.1 = f32[256,1024]{1,0:T(8,128)} custom-call(s32[1]{0:T(128)S(6)} %copy.19.count_ref, f32[4,256,256]{2,1,0:T(8,128)} %get-tuple-element.47.part_hbm, f32[256,512]{1,0:T(8,128)} %bitcast.31, bf16[4,512,256]{2,1,0:T(8,128)(2,1)} %get-tuple-element.49.high_hbm, bf16[4,512,256]{2,1,0:T(8,128)(2,1)} %get-tuple-element.50.low_hbm), custom_call_target="tpu_custom_call" | custom-call | tf_op jit(solution)/shard_map/leaf_last/pallas_call | solution.py:232
  (10 shorter events, 0.0 us)
Async XLA Ops:
  7.2 1.7 %copy-start = (f32[4,32,512]{2,1,0:T(8,128)S(1)}, f32[4,32,512]{2,1,0:T(8,128)}, u32[]{:S(2)}) copy-start(f32[4,32,512]{2,1,0:T(8,128)} %param.16) | copy-start | bytes 786436
  7.2 91.3 %all-gather.3.cloned.1.call-start = ((), (), s32[]{:S(2)}) async-start(), calls=%async_computation.3 | async-start | bytes 7569408 | tf_op jit(solution)/shard_map/all_gather | solution.py:600
  9.7 28.9 %all-to-all-start = ((f32[16,8,512]{2,1,0:T(8,128)}), f32[16,8,512]{2,1,0:T(8,128)S(1)}, u32[]{:S(2)}, u32[]{:S(2)}) async-start(f32[16,8,512]{2,1,0:T(8,128)} %broadcast_in_dim.47), calls=%async_computation | async-start | bytes 524288 | tf_op jit(solution)/shard_map/all_to_all | solution.py:567
  38.6 0.7 copy-start.4
  40.9 12.2 %collective-permute-start.2 = (f32[52,8,128]{2,1,0:T(8,128)}, f32[52,8,128]{2,1,0:T(8,128)S(1)}, u32[]{:S(2)}, u32[]{:S(2)}) collective-permute-start(f32[52,8,128]{2,1,0:T(8,128)} %pack.1), channel_id=1, source_target_pairs={{0,64},{1,257},{32,96},{33,289},{64,0},{65,321},{96,32},{97,353},{... | collective-permute-start | bytes 638984 | tf_op jit(solution)/shard_map/ppermute | solution.py:555
  45.7 7.3 %collective-permute-start.1 = (f32[52,8,128]{2,1,0:T(8,128)}, f32[52,8,128]{2,1,0:T(8,128)S(1)}, u32[]{:S(2)}, u32[]{:S(2)}) collective-permute-start(f32[52,8,128]{2,1,0:T(8,128)} %pack.1), channel_id=1, source_target_pairs={{0,96},{1,385},{32,0},{33,417},{64,32},{65,449},{96,64},{97,481},{... | collective-permute-start | bytes 638984 | tf_op jit(solution)/shard_map/ppermute | solution.py:555
  48.4 8.3 %collective-permute-start = (f32[52,8,128]{2,1,0:T(8,128)}, f32[52,8,128]{2,1,0:T(8,128)S(1)}, u32[]{:S(2)}, u32[]{:S(2)}) collective-permute-start(f32[52,8,128]{2,1,0:T(8,128)} %pack.1), channel_id=1, source_target_pairs={{0,32},{1,129},{32,64},{33,161},{64,96},{65,193},{96,0},{97,225},{... | collective-permute-start | bytes 638984 | tf_op jit(solution)/shard_map/ppermute | solution.py:555
  57.7 55.0 %copy-start.1 = (f32[4,52,8,128]{3,2,1,0:T(8,128)}, f32[4,52,8,128]{3,2,1,0:T(8,128)S(1)}, u32[]{:S(2)}) copy-start(f32[4,52,8,128]{3,2,1,0:T(8,128)S(1)} %pad_maximum_fusion.refs_0_) | copy-start | bytes 2555908
  57.8 23.2 %collective-permute-start.5 = (f32[4,52,8,128]{3,2,1,0:T(8,128)S(1)}, f32[4,52,8,128]{3,2,1,0:T(8,128)S(1)}, u32[]{:S(2)}, u32[]{:S(2)}) collective-permute-start(f32[4,52,8,128]{3,2,1,0:T(8,128)S(1)} %pad_maximum_fusion.refs_0_), channel_id=1, source_target_pairs={{0,1},{1,0},{2,3},{3,2},{4,5},{5,4},{6,7},{7,6},{8,9},{9,8},{10,11... | collective-permute-start | bytes 2555912 | tf_op jit(solution)/shard_map/ppermute | solution.py:544
  68.3 13.8 %collective-permute-start.4 = (f32[4,52,8,128]{3,2,1,0:T(8,128)S(1)}, f32[4,52,8,128]{3,2,1,0:T(8,128)S(1)}, u32[]{:S(2)}, u32[]{:S(2)}) collective-permute-start(f32[4,52,8,128]{3,2,1,0:T(8,128)S(1)} %pad_maximum_fusion.refs_0_), channel_id=1, source_target_pairs={{0,384},{1,97},{32,416},{33,1},{64,448},{65,33},{96,480},{97,65},{... | collective-permute-start | bytes 2555912 | tf_op jit(solution)/shard_map/ppermute | solution.py:555
  70.2 15.0 %collective-permute-start.3 = (f32[4,52,8,128]{3,2,1,0:T(8,128)S(1)}, f32[4,52,8,128]{3,2,1,0:T(8,128)}, u32[]{:S(2)}, u32[]{:S(2)}) collective-permute-start(f32[4,52,8,128]{3,2,1,0:T(8,128)S(1)} %pad_maximum_fusion.refs_0_), channel_id=1, source_target_pairs={{0,128},{1,33},{32,160},{33,65},{64,192},{65,97},{96,224},{97,1},{... | collective-permute-start | bytes 2555912 | tf_op jit(solution)/shard_map/ppermute | solution.py:555
  81.0 31.8 %copy-start.5 = (f32[4,52,8,128]{3,2,1,0:T(8,128)}, f32[4,52,8,128]{3,2,1,0:T(8,128)S(1)}, u32[]{:S(2)}) copy-start(f32[4,52,8,128]{3,2,1,0:T(8,128)S(1)} %collective-permute-done.5.refs_4_) | copy-start | bytes 2555908
  82.1 30.6 %copy-start.6 = (f32[4,52,8,128]{3,2,1,0:T(8,128)}, f32[4,52,8,128]{3,2,1,0:T(8,128)S(1)}, u32[]{:S(2)}) copy-start(f32[4,52,8,128]{3,2,1,0:T(8,128)S(1)} %collective-permute-done.4.refs_2_) | copy-start | bytes 2555908
  85.3 18.0 %collective-permute-start.6 = (f32[4,52,8,128]{3,2,1,0:T(8,128)}, f32[4,52,8,128]{3,2,1,0:T(8,128)}, u32[]{:S(2)}, u32[]{:S(2)}) collective-permute-start(f32[4,52,8,128]{3,2,1,0:T(8,128)} %collective-permute-done.3.refs_1_), channel_id=1, source_target_pairs={{0,128},{1,33},{32,160},{33,65},{64,192},{65,97},{96,224},{97,1},{... | collective-permute-start | bytes 2555912 | tf_op jit(solution)/shard_map/ppermute | solution.py:555
  88.1 24.7 %collective-permute-start.7 = (f32[4,52,8,128]{3,2,1,0:T(8,128)}, f32[4,52,8,128]{3,2,1,0:T(8,128)}, u32[]{:S(2)}, u32[]{:S(2)}) collective-permute-start(f32[4,52,8,128]{3,2,1,0:T(8,128)} %collective-permute-done.3.refs_1_), channel_id=1, source_target_pairs={{0,1},{1,0},{2,3},{3,2},{4,5},{5,4},{6,7},{7,6},{8,9},{9,8},{10,11... | collective-permute-start | bytes 2555912 | tf_op jit(solution)/shard_map/ppermute | solution.py:544
  93.6 19.1 %collective-permute-start.8 = (f32[4,52,8,128]{3,2,1,0:T(8,128)S(1)}, f32[4,52,8,128]{3,2,1,0:T(8,128)}, u32[]{:S(2)}, u32[]{:S(2)}) collective-permute-start(f32[4,52,8,128]{3,2,1,0:T(8,128)S(1)} %collective-permute-done.4.refs_2_), channel_id=1, source_target_pairs={{0,1},{1,0},{2,3},{3,2},{4,5},{5,4},{6,7},{7,6},{8,9},{9,8},{10,11... | collective-permute-start | bytes 2555912 | tf_op jit(solution)/shard_map/ppermute | solution.py:544
  103.2 9.5 %collective-permute-start.9 = (f32[4,52,8,128]{3,2,1,0:T(8,128)}, f32[4,52,8,128]{3,2,1,0:T(8,128)}, u32[]{:S(2)}, u32[]{:S(2)}) collective-permute-start(f32[4,52,8,128]{3,2,1,0:T(8,128)} %collective-permute-done.6.refs_3_), channel_id=1, source_target_pairs={{0,1},{1,0},{2,3},{3,2},{4,5},{5,4},{6,7},{7,6},{8,9},{9,8},{10,11... | collective-permute-start | bytes 2555912 | tf_op jit(solution)/shard_map/ppermute | solution.py:544
  107.1 15.8 %all-to-all-start.1 = ((f32[16,16,512]{2,1,0:T(8,128)}), f32[16,16,512]{2,1,0:T(8,128)S(1)}, u32[]{:S(2)}, u32[]{:S(2)}) async-start(f32[16,16,512]{2,1,0:T(8,128)} %bitcast.30), calls=%async_computation.1 | async-start | bytes 1048576 | tf_op jit(solution)/shard_map/all_to_all | solution.py:607
  122.9 0.8 copy-start.2
  135.8 13.6 %all-to-all-start.2 = ((f32[16,16,512]{2,1,0:T(8,128)}), f32[16,16,512]{2,1,0:T(8,128)S(1)}, u32[]{:S(2)}, u32[]{:S(2)}) async-start(f32[16,16,512]{2,1,0:T(8,128)} %get-tuple-element.48), calls=%async_computation.2 | async-start | bytes 1048576 | tf_op jit(solution)/shard_map/all_to_all | solution.py:616
  149.4 0.8 copy-start.3
Sparse Core Ops, SparseCore 0:
  10.1 88.3 all-gather.2

commit v5 on v3

--- a/solution.py
+++ b/solution.py
@@ -453,12 +453,9 @@
     for sep in range(4):
         wait_all(loads[sep])
         pivot = stack2(split2(sep_rhs_ref[sep] + updates[sep, :, :512]))
-        solved[sep, :, :256] = stacked_products(
-            dot_nt, pivot[:, :256], (high_ref[sep, :256, :256], low_ref[sep, :256, :256])
-        )
-        forward = stacked_products(dot_nt, pivot, (high_ref[sep, 256:], low_ref[sep, 256:]))
-        solved[sep, :, 256:] = forward[:, :256]
-        border = forward[:, 256:] + updates[sep, :, 512:]
+        forward = stacked_products(dot_nt, pivot, (high_ref[sep], low_ref[sep]))
+        solved[sep] = forward[:, :512]
+        border = forward[:, 512:] + updates[sep, :, 512:]
         root_total = root_total + jnp.concatenate(pick(blocks(border), sep_slot_ref[sep]), axis=1)
     wait_all(loads[4])
     root = (root_high_ref[...], root_low_ref[...])
@@ -468,12 +465,9 @@
     for sep in range(4):
         border = jnp.concatenate(pick(blocks(root_answer), sep_index_ref[sep]), axis=1)
         joined = stack2(split2(jnp.concatenate([solved[sep], border], axis=1)))
-        left = stacked_products(dot_nn, joined, (high_ref[sep, :, :256], low_ref[sep, :, :256]))
-        right = stacked_products(dot_nn, joined[:, 256:], (high_ref[sep, 256:, 256:], low_ref[sep, 256:, 256:]))
-        sep_out_ref[sep, :, :256] = left
-        sep_out_ref[sep, :, 256:] = right
-        full[sep, :, :256] = left
-        full[sep, :, 256:512] = right
+        answer = stacked_products(dot_nn, joined, (high_ref[sep], low_ref[sep]))
+        sep_out_ref[sep] = answer
+        full[sep, :, :512] = answer
         full[sep, :, 512:] = border
 
     def gather(leaf, _):
@@ -530,13 +524,6 @@
     return lax.ppermute(value, ("y", "x", "c"), pairs)
 
 
-def gather_plane(value, first, beside):
-    ahead = along_plane(value, 1, first)
-    back = along_plane(value, -1, first)
-    ahead, back, beside = lax.optimization_barrier((ahead, back, beside))
-    return (value, ahead, back, along_plane(ahead, 1, first)), beside
-
-
 def gather_line(separator_factor, y, x):
     mine = lax.dynamic_slice(separator_factor, (y, 8 * x, 0), (1, 8, 512))
     return lax.all_to_all(
@@ -544,14 +531,11 @@
     )
 
 
-def spread_line(line, beside_first, beside_second):
-    parts = [line, along_plane(line, 1, True), along_plane(line, -1, True), along_plane(line, 2, True)]
-    parts, beside_first = lax.optimization_barrier((parts, beside_first))
-    rows = jnp.stack(parts)
-    swapped = swap_cores(rows)
-    own, (beside_second, swapped) = gather_plane(rows, False, (beside_second, swapped))
-    other = (swapped, swap_cores(own[1]), swap_cores(own[2]))
-    return own, other, beside_first, beside_second
+def spread_line(line):
+    rows = jnp.stack([line, along_plane(line, 1, True), along_plane(line, -1, True), along_plane(line, 2, True)])
+    ahead, back = along_plane(rows, 1, False), along_plane(rows, -1, False)
+    own = (rows, ahead, back, along_plane(ahead, 1, False))
+    return own, tuple(swap_cores(part) for part in own)
 
 
 def local(
@@ -574,11 +558,10 @@
     place = jnp.stack([y, x, c]).astype(jnp.int32)
     line = lax.all_gather(join(leaf_factor[0], root_factor), ("z", "c"), axis=0, tiled=False)
     sep_line = gather_line(separator_factor, y, x)
-    own_set, other_set, (sep_slots, sep_rhs), slots = spread_line(pack(sep_line), (sep_slots, sep_rhs), slots)
-
+    sep_line, slots, sep_slots, sep_rhs = lax.optimization_barrier((sep_line, slots, sep_slots, sep_rhs))
+    own_set, other_set = spread_line(pack(sep_line))
     border = leaf_border(pivot_count, rhs, line)
-    far, line, border = lax.optimization_barrier((own_set[3], line, border))
-    own_set, other_set = own_set[:3] + (far,), other_set + (swap_cores(far),)
+    line, border = lax.optimization_barrier((line, border))
     incoming = lax.all_to_all(
         border.reshape(16, 16, 512), ("y", "x"), split_axis=0, concat_axis=0, tiled=True
     )

time: 163 us -> 161 us (0.988)
  waiting for transfers between devices: 23.4 us -> 21.2 us
    ppermute x6, waiting for transfers between devices: 2.7 us -> 14.6 us  [along_plane(): return lax.ppermute(value, ('y', 'x', 'c'), pairs)]
    all_to_all x1, waiting for transfers between devices: 11.5 us -> 2.06 us  [gather_line(): lax.all_to_all(jnp.broadcast_to(mine, (NZ, 8, 512)), 'z', split_axis=0, c...]
    all_gather x1, waiting for transfers between devices: 4.97 us -> 0.02 us  [local(): lax.all_gather(join(leaf_factor[0], root_factor), ('z', 'c'), axis=0, til...]
    ppermute x4, starting transfers between devices: 22.2 us -> 25.7 us  [swap_cores(): return lax.ppermute(value, 'c', [(0, 1), (1, 0)])]
    all_to_all x1, starting transfers between devices: 6.74 us -> 3.73 us  [local(): lax.all_to_all(border.reshape(16, 16, 512), ('y', 'x'), split_axis=0, con...]
    unnamed x24 -> x22, local copies, waits for them, and re-layouts: 4.7 us -> 4.68 us
  transfers between devices with their start and end apart: 14 -> 14, of which waited for: 5 -> 6; matrix products, arithmetic and copies ran while one was open for 10% -> 10% of each run, Pallas kernels for 12% -> 12%
where the time goes in v5:
time: 161 us; the launch traced here: 160 us
  starting transfers between devices  68.7 us (43%)
  Pallas kernels  37 us (23%)
  waiting for transfers between devices  21.2 us (13%)
  between operations  15 us (9%)
  other arithmetic  9.82 us (6%)
  local copies, waits for them, and re-layouts  7.93 us (5%)
    ppermute x4, starting transfers between devices, swap_cores(): return lax.ppermute(value, 'c', [(0, 1), (1, 0)])  25.7 us
    ppermute x6, starting transfers between devices, along_plane(): return lax.ppermute(value, ('y', 'x', 'c'), pairs)  18.7 us
    all_to_all x1, starting transfers between devices, gather_line(): lax.all_to_all(jnp.broadcast_to(mine, (NZ, 8, 512)), 'z', split_axis=0, c...  15.7 us
    ppermute x6, waiting for transfers between devices, along_plane(): return lax.ppermute(value, ('y', 'x', 'c'), pairs)  14.6 us
    pallas_call x1, Pallas kernels, upper_solve(): pl.pallas_call(upper_kernel, out_shape=(jax.ShapeDtypeStruct((16, 16, 512...  10.6 us
    reduce_max x2, other arithmetic, inverse_rows(): return jnp.max(jnp.where(index[:, :, None] == slot, place, -1), axis=1)  8.19 us
    pallas_call x1, Pallas kernels, leaf_pivot(): pl.pallas_call(leaf_pivot_kernel, out_shape=(jax.ShapeDtypeStruct((4, 256...  7.07 us
    pallas_call x1, Pallas kernels, upper_operators(): pl.pallas_call(upper_operator_kernel, out_shape=(jax.ShapeDtypeStruct((4,...  6.98 us
  transfers between devices with their start and end apart: 14, of which 6 were waited for; matrix products, arithmetic and copies ran while one was open for 10% of the time, Pallas kernels for 12%

profile of v5, /device:TPU:1, one launch (start us, length us, event | category | flops | bytes accessed | tf_op | source)
XLA Modules:
  0.0 159.7 jit_solution(4353986192481914341)
XLA Ops:
  7.2 0.0 copy-start
  7.2 0.0 copy-start.7
  7.2 0.0 copy-start.9
  7.2 0.0 all-gather.3.cloned.1.call-start
  7.2 1.7 %join.1 = f32[56,1024]{1,0:T(8,128)} custom-call(f32[48,1024]{1,0:T(8,128)} %bitcast.38, f32[16,512]{1,0:T(8,128)} %root_ref.1), custom_call_target="tpu_custom_call" | custom-call | tf_op jit(solution)/shard_map/join/pallas_call | solution.py:76
  8.9 0.0 all-gather.3.cloned.1.call-update
  9.0 0.7 broadcast_in_dim.59
  9.7 15.7 %all-to-all-start.1 = ((f32[16,8,512]{2,1,0:T(8,128)}), f32[16,8,512]{2,1,0:T(8,128)S(1)}, u32[]{:S(2)}, u32[]{:S(2)}) async-start(f32[16,8,512]{2,1,0:T(8,128)} %broadcast_in_dim.59), calls=%async_computation.1 | async-start | bytes 524288 | tf_op jit(solution)/shard_map/all_to_all | solution.py:529
  25.4 1.6 %copy.18 = f32[1,16,4,512]{3,1,2,0:T(8,128)} copy(f32[1,16,4,512]{3,2,1,0:T(4,128)} %param.15) | data formatting | bytes 262144 | tf_op args[5]
  27.0 6.8 %select_reduce_fusion = s32[16,1024]{1,0:T(8,128)S(1)} fusion(s32[16,512]{1,0:T(8,128)} %param.14), kind=kLoop, calls=%fused_computation | loop fusion | flops 25149440 | bytes 98304 | tf_op jit(solution)/shard_map/reduce_max | solution.py:509
  33.8 0.7 broadcast_in_dim.62.slot_ref
  34.5 1.4 select_reduce_fusion.1
  35.9 0.6 broadcast_in_dim.65.sep_slot_ref
  36.5 2.1 %all-to-all-done.1.line_ref = f32[16,8,512]{2,1,0:T(8,128)S(1)} async-done(((f32[16,8,512]{2,1,0:T(8,128)}), f32[16,8,512]{2,1,0:T(8,128)S(1)}, u32[]{:S(2)}, u32[]{:S(2)}) %all-to-all-start.1) | async-done | bytes 262176 | tf_op jit(solution)/shard_map/all_to_all | solution.py:529
  38.6 0.7 copy-done.4
  39.3 1.7 %pack.1 = f32[52,8,128]{2,1,0:T(8,128)} custom-call(f32[16,8,512]{2,1,0:T(8,128)} %copy-done.4), custom_call_target="tpu_custom_call" | custom-call | tf_op jit(solution)/shard_map/pack/pallas_call | solution.py:295
  40.9 3.2 %collective-permute-start = (f32[52,8,128]{2,1,0:T(8,128)}, f32[52,8,128]{2,1,0:T(8,128)S(1)}, u32[]{:S(2)}, u32[]{:S(2)}) collective-permute-start(f32[52,8,128]{2,1,0:T(8,128)} %pack.1), channel_id=1, source_target_pairs={{0,32},{1,129},{32,64},{33,161},{64,96},{65,193},{96,0},{97,225},{... | collective-permute-start | bytes 638984 | tf_op jit(solution)/shard_map/ppermute | solution.py:524
  44.1 3.4 %collective-permute-start.1 = (f32[52,8,128]{2,1,0:T(8,128)}, f32[52,8,128]{2,1,0:T(8,128)S(1)}, u32[]{:S(2)}, u32[]{:S(2)}) collective-permute-start(f32[52,8,128]{2,1,0:T(8,128)} %pack.1), channel_id=1, source_target_pairs={{0,96},{1,385},{32,0},{33,417},{64,32},{65,449},{96,64},{97,481},{... | collective-permute-start | bytes 638984 | tf_op jit(solution)/shard_map/ppermute | solution.py:524
  47.5 3.5 %collective-permute-start.2 = (f32[52,8,128]{2,1,0:T(8,128)}, f32[52,8,128]{2,1,0:T(8,128)S(1)}, u32[]{:S(2)}, u32[]{:S(2)}) collective-permute-start(f32[52,8,128]{2,1,0:T(8,128)} %pack.1), channel_id=1, source_target_pairs={{0,64},{1,257},{32,96},{33,289},{64,0},{65,321},{96,32},{97,353},{... | collective-permute-start | bytes 638984 | tf_op jit(solution)/shard_map/ppermute | solution.py:524
  51.1 0.3 collective-permute-done.1
  51.3 4.5 %collective-permute-done.2 = f32[52,8,128]{2,1,0:T(8,128)S(1)} collective-permute-done((f32[52,8,128]{2,1,0:T(8,128)}, f32[52,8,128]{2,1,0:T(8,128)S(1)}, u32[]{:S(2)}, u32[]{:S(2)}) %collective-permute-start.2) | collective-permute-done | bytes 213024 | tf_op jit(solution)/shard_map/ppermute | solution.py:524
  55.8 1.0 pad_maximum_fusion.refs_0_
  56.8 0.0 copy-start.1
  56.8 3.1 %collective-permute-start.3 = (f32[4,52,8,128]{3,2,1,0:T(8,128)S(1)}, f32[4,52,8,128]{3,2,1,0:T(8,128)S(1)}, u32[]{:S(2)}, u32[]{:S(2)}) collective-permute-start(f32[4,52,8,128]{3,2,1,0:T(8,128)S(1)} %pad_maximum_fusion.refs_0_), channel_id=1, source_target_pairs={{0,128},{1,33},{32,160},{33,65},{64,192},{65,97},{96,224},{97,1},{... | collective-permute-start | bytes 2555912 | tf_op jit(solution)/shard_map/ppermute | solution.py:524
  59.9 3.4 %collective-permute-start.4 = (f32[4,52,8,128]{3,2,1,0:T(8,128)S(1)}, f32[4,52,8,128]{3,2,1,0:T(8,128)S(1)}, u32[]{:S(2)}, u32[]{:S(2)}) collective-permute-start(f32[4,52,8,128]{3,2,1,0:T(8,128)S(1)} %pad_maximum_fusion.refs_0_), channel_id=1, source_target_pairs={{0,384},{1,97},{32,416},{33,1},{64,448},{65,33},{96,480},{97,65},{... | collective-permute-start | bytes 2555912 | tf_op jit(solution)/shard_map/ppermute | solution.py:524
  63.3 9.9 %collective-permute-done.3.refs_1_ = f32[4,52,8,128]{3,2,1,0:T(8,128)S(1)} collective-permute-done((f32[4,52,8,128]{3,2,1,0:T(8,128)S(1)}, f32[4,52,8,128]{3,2,1,0:T(8,128)S(1)}, u32[]{:S(2)}, u32[]{:S(2)}) %collective-permute-start.3) | collective-permute-done | bytes 852000 | tf_op jit(solution)/shard_map/ppermute | solution.py:524
  73.2 2.1 %collective-permute-start.5 = (f32[4,52,8,128]{3,2,1,0:T(8,128)S(1)}, f32[4,52,8,128]{3,2,1,0:T(8,128)}, u32[]{:S(2)}, u32[]{:S(2)}) collective-permute-start(f32[4,52,8,128]{3,2,1,0:T(8,128)S(1)} %collective-permute-done.3.refs_1_), channel_id=1, source_target_pairs={{0,128},{1,33},{32,160},{33,65},{64,192},{65,97},{96,224},{97,1},{... | collective-permute-start | bytes 2555912 | tf_op jit(solution)/shard_map/ppermute | solution.py:524
  75.3 12.6 %collective-permute-start.6 = (f32[4,52,8,128]{3,2,1,0:T(8,128)S(1)}, f32[4,52,8,128]{3,2,1,0:T(8,128)}, u32[]{:S(2)}, u32[]{:S(2)}) collective-permute-start(f32[4,52,8,128]{3,2,1,0:T(8,128)S(1)} %pad_maximum_fusion.refs_0_), channel_id=1, source_target_pairs={{0,1},{1,0},{2,3},{3,2},{4,5},{5,4},{6,7},{7,6},{8,9},{9,8},{10,11... | collective-permute-start | bytes 2555912 | tf_op jit(solution)/shard_map/ppermute | solution.py:513
  87.9 1.9 %collective-permute-start.7 = (f32[4,52,8,128]{3,2,1,0:T(8,128)S(1)}, f32[4,52,8,128]{3,2,1,0:T(8,128)}, u32[]{:S(2)}, u32[]{:S(2)}) collective-permute-start(f32[4,52,8,128]{3,2,1,0:T(8,128)S(1)} %collective-permute-done.3.refs_1_), channel_id=1, source_target_pairs={{0,1},{1,0},{2,3},{3,2},{4,5},{5,4},{6,7},{7,6},{8,9},{9,8},{10,11... | collective-permute-start | bytes 2555912 | tf_op jit(solution)/shard_map/ppermute | solution.py:513
  89.8 2.4 %collective-permute-start.8 = (f32[4,52,8,128]{3,2,1,0:T(8,128)S(1)}, f32[4,52,8,128]{3,2,1,0:T(8,128)}, u32[]{:S(2)}, u32[]{:S(2)}) collective-permute-start(f32[4,52,8,128]{3,2,1,0:T(8,128)S(1)} %collective-permute-done.4.refs_2_), channel_id=1, source_target_pairs={{0,1},{1,0},{2,3},{3,2},{4,5},{5,4},{6,7},{7,6},{8,9},{9,8},{10,11... | collective-permute-start | bytes 2555912 | tf_op jit(solution)/shard_map/ppermute | solution.py:513
  92.2 0.0 collective-permute-done.5.refs_3_
  92.2 8.8 %collective-permute-start.9 = (f32[4,52,8,128]{3,2,1,0:T(8,128)}, f32[4,52,8,128]{3,2,1,0:T(8,128)}, u32[]{:S(2)}, u32[]{:S(2)}) collective-permute-start(f32[4,52,8,128]{3,2,1,0:T(8,128)} %collective-permute-done.5.refs_3_), channel_id=1, source_target_pairs={{0,1},{1,0},{2,3},{3,2},{4,5},{5,4},{6,7},{7,6},{8,9},{9,8},{10,11... | collective-permute-start | bytes 2555912 | tf_op jit(solution)/shard_map/ppermute | solution.py:513
  101.7 0.0 all-gather.3.cloned.1.call-done
  101.8 3.8 %leaf_border.1 = f32[256,512]{1,0:T(8,128)} custom-call(s32[1]{0:T(128)S(6)} %copy.19.count_ref, f32[256,1024]{1,0:T(8,128)} %bitcast.28, f32[32,56,1024]{2,1,0:T(8,128)} %bitcast.25), custom_call_target="tpu_custom_call" | custom-call | tf_op jit(solution)/shard_map/leaf_border/pallas_call | solution.py:108
  105.6 3.7 %all-to-all-start = ((f32[16,16,512]{2,1,0:T(8,128)}), f32[16,16,512]{2,1,0:T(8,128)S(1)}, u32[]{:S(2)}, u32[]{:S(2)}) async-start(f32[16,16,512]{2,1,0:T(8,128)} %bitcast.30), calls=%async_computation | async-start | bytes 1048576 | tf_op jit(solution)/shard_map/all_to_all | solution.py:565
  109.3 0.6 broadcast_in_dim.66.index_ref
  110.0 0.6 broadcast_in_dim.67.sep_index_ref
  110.6 0.6 pad_add_fusion.place_ref
  111.2 7.0 %upper_operators.1 = (bf16[4,1024,512]{2,1,0:T(8,128)(2,1)}, bf16[4,1024,512]{2,1,0:T(8,128)(2,1)}, bf16[512,512]{1,0:T(8,128)(2,1)}, bf16[512,512]{1,0:T(8,128)(2,1)}) custom-call(s32[3]{0:T(128)} %pad_add_fusion.place_ref, f32[4,52,8,128]{3,2,1,0:T(8,128)} %copy-done.1, f32[4,52,8,128]{3,2,1,0:T(8,128)} %copy-done.5, f32[4,52,8,128]{3,2,1,0:T(8,128)} %copy-done.6, ...), custom_call_target="tpu_custom_call" | custom-call | tf_op jit(solution)/shard_map/upper_operators/pallas_call | solution.py:397
  118.2 2.1 %all-to-all-done.incoming_ref = f32[16,16,512]{2,1,0:T(8,128)S(1)} async-done(((f32[16,16,512]{2,1,0:T(8,128)}), f32[16,16,512]{2,1,0:T(8,128)S(1)}, u32[]{:S(2)}, u32[]{:S(2)}) %all-to-all-start) | async-done | bytes 524320 | tf_op jit(solution)/shard_map/all_to_all | solution.py:565
  120.4 0.8 copy-done.2
  121.2 10.6 %upper_solve.1 = (f32[16,16,512]{2,1,0:T(8,128)}, f32[4,16,512]{2,1,0:T(8,128)}, f32[16,512]{1,0:T(8,128)}) custom-call(s32[16]{0:T(128)} %parent_ref.1, f32[16,16,512]{2,1,0:T(8,128)} %copy-done.2, s32[16,1,1024]{2,1,0:T(1,128)} %broadcast_in_dim.62.slot_ref, s32[16,1,512]{2,1,0:T(1,128)} %broadcast_in_dim.66.index_ref, f32[4,16,512]{2,1,0:T(8,128)} %bitcast.34, ...), custom_call_target="tpu_custom_call" | custom-call | tf_op jit(solution)/shard_map/upper_solve/pallas_call | solution.py:482
  131.8 4.8 %all-to-all-start.2 = ((f32[16,16,512]{2,1,0:T(8,128)}), f32[16,16,512]{2,1,0:T(8,128)S(1)}, u32[]{:S(2)}, u32[]{:S(2)}) async-start(f32[16,16,512]{2,1,0:T(8,128)} %get-tuple-element.34), calls=%async_computation.2 | async-start | bytes 1048576 | tf_op jit(solution)/shard_map/all_to_all | solution.py:574
  136.6 7.1 %leaf_pivot.1 = (f32[4,256,256]{2,1,0:T(8,128)}, bf16[4,512,256]{2,1,0:T(8,128)(2,1)}, bf16[4,512,256]{2,1,0:T(8,128)(2,1)}) custom-call(s32[1]{0:T(128)S(6)} %copy.19.count_ref, f32[256,1024]{1,0:T(8,128)} %bitcast.29, f32[32,56,1024]{2,1,0:T(8,128)} %bitcast.27), custom_call_target="tpu_custom_call" | custom-call | tf_op jit(solution)/shard_map/leaf_pivot/pallas_call | solution.py:175
  143.7 0.7 copy.16
  144.4 2.3 %all-to-all-done.2 = f32[16,16,512]{2,1,0:T(8,128)S(1)} async-done(((f32[16,16,512]{2,1,0:T(8,128)}), f32[16,16,512]{2,1,0:T(8,128)S(1)}, u32[]{:S(2)}, u32[]{:S(2)}) %all-to-all-start.2) | async-done | bytes 524320 | tf_op jit(solution)/shard_map/all_to_all | solution.py:574
  146.8 0.8 copy-done.3
  147.6 5.2 %leaf_last.1 = f32[256,1024]{1,0:T(8,128)} custom-call(s32[1]{0:T(128)S(6)} %copy.19.count_ref, f32[4,256,256]{2,1,0:T(8,128)} %get-tuple-element.33.part_hbm, f32[256,512]{1,0:T(8,128)} %bitcast.31, bf16[4,512,256]{2,1,0:T(8,128)(2,1)} %get-tuple-element.35.high_hbm, bf16[4,512,256]{2,1,0:T(8,128)(2,1)} %get-tuple-element.36.low_hbm), custom_call_target="tpu_custom_call" | custom-call | tf_op jit(solution)/shard_map/leaf_last/pallas_call | solution.py:229
  (20 shorter events, 0.1 us)
Async XLA Ops:
  7.2 1.8 %copy-start = (f32[4,32,512]{2,1,0:T(8,128)S(1)}, f32[4,32,512]{2,1,0:T(8,128)}, u32[]{:S(2)}) copy-start(f32[4,32,512]{2,1,0:T(8,128)} %param.16) | copy-start | bytes 786436
  7.2 102.1 %copy-start.7 = (s32[16,512]{1,0:T(8,128)S(1)}, s32[16,512]{1,0:T(8,128)}, u32[]{:S(2)}) copy-start(s32[16,512]{1,0:T(8,128)} %param.14) | copy-start | bytes 98308
  7.2 102.8 %copy-start.9 = (s32[4,512]{1,0:T(4,128)S(1)}, s32[4,512]{1,0:T(4,128)}, u32[]{:S(2)}) copy-start(s32[4,512]{1,0:T(4,128)} %param.17) | copy-start | bytes 24580
  7.2 94.6 %all-gather.3.cloned.1.call-start = ((), (), s32[]{:S(2)}) async-start(), calls=%async_computation.3 | async-start | bytes 7569408 | tf_op jit(solution)/shard_map/all_gather | solution.py:559
  9.7 28.9 %all-to-all-start.1 = ((f32[16,8,512]{2,1,0:T(8,128)}), f32[16,8,512]{2,1,0:T(8,128)S(1)}, u32[]{:S(2)}, u32[]{:S(2)}) async-start(f32[16,8,512]{2,1,0:T(8,128)} %broadcast_in_dim.59), calls=%async_computation.1 | async-start | bytes 524288 | tf_op jit(solution)/shard_map/all_to_all | solution.py:529
  38.6 0.7 copy-start.4
  40.9 10.1 %collective-permute-start = (f32[52,8,128]{2,1,0:T(8,128)}, f32[52,8,128]{2,1,0:T(8,128)S(1)}, u32[]{:S(2)}, u32[]{:S(2)}) collective-permute-start(f32[52,8,128]{2,1,0:T(8,128)} %pack.1), channel_id=1, source_target_pairs={{0,32},{1,129},{32,64},{33,161},{64,96},{65,193},{96,0},{97,225},{... | collective-permute-start | bytes 638984 | tf_op jit(solution)/shard_map/ppermute | solution.py:524
  44.1 7.2 %collective-permute-start.1 = (f32[52,8,128]{2,1,0:T(8,128)}, f32[52,8,128]{2,1,0:T(8,128)S(1)}, u32[]{:S(2)}, u32[]{:S(2)}) collective-permute-start(f32[52,8,128]{2,1,0:T(8,128)} %pack.1), channel_id=1, source_target_pairs={{0,96},{1,385},{32,0},{33,417},{64,32},{65,449},{96,64},{97,481},{... | collective-permute-start | bytes 638984 | tf_op jit(solution)/shard_map/ppermute | solution.py:524
  47.5 8.3 %collective-permute-start.2 = (f32[52,8,128]{2,1,0:T(8,128)}, f32[52,8,128]{2,1,0:T(8,128)S(1)}, u32[]{:S(2)}, u32[]{:S(2)}) collective-permute-start(f32[52,8,128]{2,1,0:T(8,128)} %pack.1), channel_id=1, source_target_pairs={{0,64},{1,257},{32,96},{33,289},{64,0},{65,321},{96,32},{97,353},{... | collective-permute-start | bytes 638984 | tf_op jit(solution)/shard_map/ppermute | solution.py:524
  56.8 54.4 %copy-start.1 = (f32[4,52,8,128]{3,2,1,0:T(8,128)}, f32[4,52,8,128]{3,2,1,0:T(8,128)S(1)}, u32[]{:S(2)}) copy-start(f32[4,52,8,128]{3,2,1,0:T(8,128)S(1)} %pad_maximum_fusion.refs_0_) | copy-start | bytes 2555908
  56.8 16.4 %collective-permute-start.3 = (f32[4,52,8,128]{3,2,1,0:T(8,128)S(1)}, f32[4,52,8,128]{3,2,1,0:T(8,128)S(1)}, u32[]{:S(2)}, u32[]{:S(2)}) collective-permute-start(f32[4,52,8,128]{3,2,1,0:T(8,128)S(1)} %pad_maximum_fusion.refs_0_), channel_id=1, source_target_pairs={{0,128},{1,33},{32,160},{33,65},{64,192},{65,97},{96,224},{97,1},{... | collective-permute-start | bytes 2555912 | tf_op jit(solution)/shard_map/ppermute | solution.py:524
  59.9 29.9 %collective-permute-start.4 = (f32[4,52,8,128]{3,2,1,0:T(8,128)S(1)}, f32[4,52,8,128]{3,2,1,0:T(8,128)S(1)}, u32[]{:S(2)}, u32[]{:S(2)}) collective-permute-start(f32[4,52,8,128]{3,2,1,0:T(8,128)S(1)} %pad_maximum_fusion.refs_0_), channel_id=1, source_target_pairs={{0,384},{1,97},{32,416},{33,1},{64,448},{65,33},{96,480},{97,65},{... | collective-permute-start | bytes 2555912 | tf_op jit(solution)/shard_map/ppermute | solution.py:524
  73.2 38.1 %copy-start.5 = (f32[4,52,8,128]{3,2,1,0:T(8,128)}, f32[4,52,8,128]{3,2,1,0:T(8,128)S(1)}, u32[]{:S(2)}) copy-start(f32[4,52,8,128]{3,2,1,0:T(8,128)S(1)} %collective-permute-done.3.refs_1_) | copy-start | bytes 2555908
  73.2 19.1 %collective-permute-start.5 = (f32[4,52,8,128]{3,2,1,0:T(8,128)S(1)}, f32[4,52,8,128]{3,2,1,0:T(8,128)}, u32[]{:S(2)}, u32[]{:S(2)}) collective-permute-start(f32[4,52,8,128]{3,2,1,0:T(8,128)S(1)} %collective-permute-done.3.refs_1_), channel_id=1, source_target_pairs={{0,128},{1,33},{32,160},{33,65},{64,192},{65,97},{96,224},{97,1},{... | collective-permute-start | bytes 2555912 | tf_op jit(solution)/shard_map/ppermute | solution.py:524
  75.3 35.9 %collective-permute-start.6 = (f32[4,52,8,128]{3,2,1,0:T(8,128)S(1)}, f32[4,52,8,128]{3,2,1,0:T(8,128)}, u32[]{:S(2)}, u32[]{:S(2)}) collective-permute-start(f32[4,52,8,128]{3,2,1,0:T(8,128)S(1)} %pad_maximum_fusion.refs_0_), channel_id=1, source_target_pairs={{0,1},{1,0},{2,3},{3,2},{4,5},{5,4},{6,7},{7,6},{8,9},{9,8},{10,11... | collective-permute-start | bytes 2555912 | tf_op jit(solution)/shard_map/ppermute | solution.py:513
  87.9 23.3 %collective-permute-start.7 = (f32[4,52,8,128]{3,2,1,0:T(8,128)S(1)}, f32[4,52,8,128]{3,2,1,0:T(8,128)}, u32[]{:S(2)}, u32[]{:S(2)}) collective-permute-start(f32[4,52,8,128]{3,2,1,0:T(8,128)S(1)} %collective-permute-done.3.refs_1_), channel_id=1, source_target_pairs={{0,1},{1,0},{2,3},{3,2},{4,5},{5,4},{6,7},{7,6},{8,9},{9,8},{10,11... | collective-permute-start | bytes 2555912 | tf_op jit(solution)/shard_map/ppermute | solution.py:513
  89.8 21.4 %copy-start.6 = (f32[4,52,8,128]{3,2,1,0:T(8,128)}, f32[4,52,8,128]{3,2,1,0:T(8,128)S(1)}, u32[]{:S(2)}) copy-start(f32[4,52,8,128]{3,2,1,0:T(8,128)S(1)} %collective-permute-done.4.refs_2_) | copy-start | bytes 2555908
  89.8 21.4 %collective-permute-start.8 = (f32[4,52,8,128]{3,2,1,0:T(8,128)S(1)}, f32[4,52,8,128]{3,2,1,0:T(8,128)}, u32[]{:S(2)}, u32[]{:S(2)}) collective-permute-start(f32[4,52,8,128]{3,2,1,0:T(8,128)S(1)} %collective-permute-done.4.refs_2_), channel_id=1, source_target_pairs={{0,1},{1,0},{2,3},{3,2},{4,5},{5,4},{6,7},{7,6},{8,9},{9,8},{10,11... | collective-permute-start | bytes 2555912 | tf_op jit(solution)/shard_map/ppermute | solution.py:513
  92.2 19.0 %collective-permute-start.9 = (f32[4,52,8,128]{3,2,1,0:T(8,128)}, f32[4,52,8,128]{3,2,1,0:T(8,128)}, u32[]{:S(2)}, u32[]{:S(2)}) collective-permute-start(f32[4,52,8,128]{3,2,1,0:T(8,128)} %collective-permute-done.5.refs_3_), channel_id=1, source_target_pairs={{0,1},{1,0},{2,3},{3,2},{4,5},{5,4},{6,7},{7,6},{8,9},{9,8},{10,11... | collective-permute-start | bytes 2555912 | tf_op jit(solution)/shard_map/ppermute | solution.py:513
  105.6 14.8 %all-to-all-start = ((f32[16,16,512]{2,1,0:T(8,128)}), f32[16,16,512]{2,1,0:T(8,128)S(1)}, u32[]{:S(2)}, u32[]{:S(2)}) async-start(f32[16,16,512]{2,1,0:T(8,128)} %bitcast.30), calls=%async_computation | async-start | bytes 1048576 | tf_op jit(solution)/shard_map/all_to_all | solution.py:565
  120.4 0.8 copy-start.2
  131.8 11.9 %copy-start.8 = (f32[4,16,512]{2,1,0:T(8,128)S(1)}, f32[4,16,512]{2,1,0:T(8,128)}, u32[]{:S(2)}) copy-start(f32[4,16,512]{2,1,0:T(8,128)} %get-tuple-element.37) | copy-start | bytes 393220
  131.8 14.9 %all-to-all-start.2 = ((f32[16,16,512]{2,1,0:T(8,128)}), f32[16,16,512]{2,1,0:T(8,128)S(1)}, u32[]{:S(2)}, u32[]{:S(2)}) async-start(f32[16,16,512]{2,1,0:T(8,128)} %get-tuple-element.34), calls=%async_computation.2 | async-start | bytes 1048576 | tf_op jit(solution)/shard_map/all_to_all | solution.py:574
  146.8 0.8 copy-start.3
Sparse Core Ops, SparseCore 0:
  10.2 88.1 all-gather.2

commit v6 on v5

--- a/solution.py
+++ b/solution.py
@@ -534,8 +534,7 @@
 def spread_line(line):
     rows = jnp.stack([line, along_plane(line, 1, True), along_plane(line, -1, True), along_plane(line, 2, True)])
     ahead, back = along_plane(rows, 1, False), along_plane(rows, -1, False)
-    own = (rows, ahead, back, along_plane(ahead, 1, False))
-    return own, tuple(swap_cores(part) for part in own)
+    return rows, ahead, back, along_plane(ahead, 1, False)
 
 
 def local(
@@ -559,9 +558,11 @@
     line = lax.all_gather(join(leaf_factor[0], root_factor), ("z", "c"), axis=0, tiled=False)
     sep_line = gather_line(separator_factor, y, x)
     sep_line, slots, sep_slots, sep_rhs = lax.optimization_barrier((sep_line, slots, sep_slots, sep_rhs))
-    own_set, other_set = spread_line(pack(sep_line))
+    own_set = spread_line(pack(sep_line))
+    other_set = tuple(swap_cores(part) for part in own_set[:3])
     border = leaf_border(pivot_count, rhs, line)
-    line, border = lax.optimization_barrier((line, border))
+    far, line, border = lax.optimization_barrier((own_set[3], line, border))
+    own_set, other_set = own_set[:3] + (far,), other_set + (swap_cores(far),)
     incoming = lax.all_to_all(
         border.reshape(16, 16, 512), ("y", "x"), split_axis=0, concat_axis=0, tiled=True
     )

time: 161 us -> 163 us (1.012)
  waiting for transfers between devices: 21.2 us -> 26.2 us
  starting transfers between devices: 68.7 us -> 65.4 us
    ppermute x4, starting transfers between devices: 25.7 us -> 19.1 us  [swap_cores(): return lax.ppermute(value, 'c', [(0, 1), (1, 0)])]
    all_gather x1, waiting for transfers between devices: 0.02 us -> 5.43 us  [local(): lax.all_gather(join(leaf_factor[0], root_factor), ('z', 'c'), axis=0, til...]
    all_to_all x1, starting transfers between devices: 3.73 us -> 6.81 us  [local(): lax.all_to_all(border.reshape(16, 16, 512), ('y', 'x'), split_axis=0, con...]
  transfers between devices with their start and end apart: 14 -> 14, of which waited for: 6 -> 7; matrix products, arithmetic and copies ran while one was open for 10% -> 10% of each run, Pallas kernels for 12% -> 12%
where the time goes in v6:
time: 163 us; the launch traced here: 161 us
  starting transfers between devices  65.4 us (40%)
  Pallas kernels  36.9 us (23%)
  waiting for transfers between devices  26.2 us (16%)
  between operations  15 us (9%)
  other arithmetic  9.82 us (6%)
  local copies, waits for them, and re-layouts  7.93 us (5%)
    ppermute x4, starting transfers between devices, swap_cores(): return lax.ppermute(value, 'c', [(0, 1), (1, 0)])  19.1 us
    ppermute x6, starting transfers between devices, along_plane(): return lax.ppermute(value, ('y', 'x', 'c'), pairs)  18.7 us
    all_to_all x1, starting transfers between devices, gather_line(): lax.all_to_all(jnp.broadcast_to(mine, (NZ, 8, 512)), 'z', split_axis=0, c...  15.7 us
    ppermute x6, waiting for transfers between devices, along_plane(): return lax.ppermute(value, ('y', 'x', 'c'), pairs)  14.6 us
    pallas_call x1, Pallas kernels, upper_solve(): pl.pallas_call(upper_kernel, out_shape=(jax.ShapeDtypeStruct((16, 16, 512...  10.6 us
    reduce_max x2, other arithmetic, inverse_rows(): return jnp.max(jnp.where(index[:, :, None] == slot, place, -1), axis=1)  8.19 us
    pallas_call x1, Pallas kernels, leaf_pivot(): pl.pallas_call(leaf_pivot_kernel, out_shape=(jax.ShapeDtypeStruct((4, 256...  7.07 us
    pallas_call x1, Pallas kernels, upper_operators(): pl.pallas_call(upper_operator_kernel, out_shape=(jax.ShapeDtypeStruct((4,...  6.97 us
  transfers between devices with their start and end apart: 14, of which 7 were waited for; matrix products, arithmetic and copies ran while one was open for 10% of the time, Pallas kernels for 12%

profile of v6, /device:TPU:1, one launch (start us, length us, event | category | flops | bytes accessed | tf_op | source)
XLA Modules:
  0.0 161.3 jit_solution(7977599732363446328)
XLA Ops:
  7.2 0.0 copy-start
  7.2 0.0 copy-start.7
  7.2 0.0 copy-start.9
  7.2 0.0 all-gather.3.cloned.1.call-start
  7.2 1.7 %join.1 = f32[56,1024]{1,0:T(8,128)} custom-call(f32[48,1024]{1,0:T(8,128)} %bitcast.38, f32[16,512]{1,0:T(8,128)} %root_ref.1), custom_call_target="tpu_custom_call" | custom-call | tf_op jit(solution)/shard_map/join/pallas_call | solution.py:76
  8.9 0.0 all-gather.3.cloned.1.call-update
  9.0 0.7 broadcast_in_dim.59
  9.7 15.7 %all-to-all-start = ((f32[16,8,512]{2,1,0:T(8,128)}), f32[16,8,512]{2,1,0:T(8,128)S(1)}, u32[]{:S(2)}, u32[]{:S(2)}) async-start(f32[16,8,512]{2,1,0:T(8,128)} %broadcast_in_dim.59), calls=%async_computation | async-start | bytes 524288 | tf_op jit(solution)/shard_map/all_to_all | solution.py:529
  25.4 1.6 copy.18
  27.0 6.8 %select_reduce_fusion = s32[16,1024]{1,0:T(8,128)S(1)} fusion(s32[16,512]{1,0:T(8,128)} %param.14), kind=kLoop, calls=%fused_computation | loop fusion | flops 25149440 | bytes 98304 | tf_op jit(solution)/shard_map/reduce_max | solution.py:509
  33.8 0.7 broadcast_in_dim.62.slot_ref
  34.5 1.4 select_reduce_fusion.1
  35.9 0.6 broadcast_in_dim.65.sep_slot_ref
  36.5 2.1 %all-to-all-done.line_ref = f32[16,8,512]{2,1,0:T(8,128)S(1)} async-done(((f32[16,8,512]{2,1,0:T(8,128)}), f32[16,8,512]{2,1,0:T(8,128)S(1)}, u32[]{:S(2)}, u32[]{:S(2)}) %all-to-all-start) | async-done | bytes 262176 | tf_op jit(solution)/shard_map/all_to_all | solution.py:529
  38.6 0.7 copy-done.4
  39.3 1.7 %pack.1 = f32[52,8,128]{2,1,0:T(8,128)} custom-call(f32[16,8,512]{2,1,0:T(8,128)} %copy-done.4), custom_call_target="tpu_custom_call" | custom-call | tf_op jit(solution)/shard_map/pack/pallas_call | solution.py:295
  40.9 3.2 %collective-permute-start = (f32[52,8,128]{2,1,0:T(8,128)}, f32[52,8,128]{2,1,0:T(8,128)S(1)}, u32[]{:S(2)}, u32[]{:S(2)}) collective-permute-start(f32[52,8,128]{2,1,0:T(8,128)} %pack.1), channel_id=1, source_target_pairs={{0,32},{1,129},{32,64},{33,161},{64,96},{65,193},{96,0},{97,225},{... | collective-permute-start | bytes 638984 | tf_op jit(solution)/shard_map/ppermute | solution.py:524
  44.1 3.4 %collective-permute-start.1 = (f32[52,8,128]{2,1,0:T(8,128)}, f32[52,8,128]{2,1,0:T(8,128)S(1)}, u32[]{:S(2)}, u32[]{:S(2)}) collective-permute-start(f32[52,8,128]{2,1,0:T(8,128)} %pack.1), channel_id=1, source_target_pairs={{0,96},{1,385},{32,0},{33,417},{64,32},{65,449},{96,64},{97,481},{... | collective-permute-start | bytes 638984 | tf_op jit(solution)/shard_map/ppermute | solution.py:524
  47.5 3.5 %collective-permute-start.2 = (f32[52,8,128]{2,1,0:T(8,128)}, f32[52,8,128]{2,1,0:T(8,128)S(1)}, u32[]{:S(2)}, u32[]{:S(2)}) collective-permute-start(f32[52,8,128]{2,1,0:T(8,128)} %pack.1), channel_id=1, source_target_pairs={{0,64},{1,257},{32,96},{33,289},{64,0},{65,321},{96,32},{97,353},{... | collective-permute-start | bytes 638984 | tf_op jit(solution)/shard_map/ppermute | solution.py:524
  51.1 0.3 collective-permute-done.1
  51.3 4.5 %collective-permute-done.2 = f32[52,8,128]{2,1,0:T(8,128)S(1)} collective-permute-done((f32[52,8,128]{2,1,0:T(8,128)}, f32[52,8,128]{2,1,0:T(8,128)S(1)}, u32[]{:S(2)}, u32[]{:S(2)}) %collective-permute-start.2) | collective-permute-done | bytes 213024 | tf_op jit(solution)/shard_map/ppermute | solution.py:524
  55.8 1.0 pad_maximum_fusion.refs_0_
  56.8 0.0 copy-start.1
  56.8 3.1 %collective-permute-start.3 = (f32[4,52,8,128]{3,2,1,0:T(8,128)S(1)}, f32[4,52,8,128]{3,2,1,0:T(8,128)S(1)}, u32[]{:S(2)}, u32[]{:S(2)}) collective-permute-start(f32[4,52,8,128]{3,2,1,0:T(8,128)S(1)} %pad_maximum_fusion.refs_0_), channel_id=1, source_target_pairs={{0,128},{1,33},{32,160},{33,65},{64,192},{65,97},{96,224},{97,1},{... | collective-permute-start | bytes 2555912 | tf_op jit(solution)/shard_map/ppermute | solution.py:524
  59.9 3.4 %collective-permute-start.5 = (f32[4,52,8,128]{3,2,1,0:T(8,128)S(1)}, f32[4,52,8,128]{3,2,1,0:T(8,128)S(1)}, u32[]{:S(2)}, u32[]{:S(2)}) collective-permute-start(f32[4,52,8,128]{3,2,1,0:T(8,128)S(1)} %pad_maximum_fusion.refs_0_), channel_id=1, source_target_pairs={{0,384},{1,97},{32,416},{33,1},{64,448},{65,33},{96,480},{97,65},{... | collective-permute-start | bytes 2555912 | tf_op jit(solution)/shard_map/ppermute | solution.py:524
  63.3 9.9 %collective-permute-done.3.refs_1_ = f32[4,52,8,128]{3,2,1,0:T(8,128)S(1)} collective-permute-done((f32[4,52,8,128]{3,2,1,0:T(8,128)S(1)}, f32[4,52,8,128]{3,2,1,0:T(8,128)S(1)}, u32[]{:S(2)}, u32[]{:S(2)}) %collective-permute-start.3) | collective-permute-done | bytes 852000 | tf_op jit(solution)/shard_map/ppermute | solution.py:524
  73.2 2.1 %collective-permute-start.4 = (f32[4,52,8,128]{3,2,1,0:T(8,128)S(1)}, f32[4,52,8,128]{3,2,1,0:T(8,128)}, u32[]{:S(2)}, u32[]{:S(2)}) collective-permute-start(f32[4,52,8,128]{3,2,1,0:T(8,128)S(1)} %collective-permute-done.3.refs_1_), channel_id=1, source_target_pairs={{0,128},{1,33},{32,160},{33,65},{64,192},{65,97},{96,224},{97,1},{... | collective-permute-start | bytes 2555912 | tf_op jit(solution)/shard_map/ppermute | solution.py:524
  75.9 12.6 %collective-permute-start.6 = (f32[4,52,8,128]{3,2,1,0:T(8,128)S(1)}, f32[4,52,8,128]{3,2,1,0:T(8,128)}, u32[]{:S(2)}, u32[]{:S(2)}) collective-permute-start(f32[4,52,8,128]{3,2,1,0:T(8,128)S(1)} %pad_maximum_fusion.refs_0_), channel_id=1, source_target_pairs={{0,1},{1,0},{2,3},{3,2},{4,5},{5,4},{6,7},{7,6},{8,9},{9,8},{10,11... | collective-permute-start | bytes 2555912 | tf_op jit(solution)/shard_map/ppermute | solution.py:513
  88.5 1.9 %collective-permute-start.7 = (f32[4,52,8,128]{3,2,1,0:T(8,128)S(1)}, f32[4,52,8,128]{3,2,1,0:T(8,128)}, u32[]{:S(2)}, u32[]{:S(2)}) collective-permute-start(f32[4,52,8,128]{3,2,1,0:T(8,128)S(1)} %collective-permute-done.3.refs_1_), channel_id=1, source_target_pairs={{0,1},{1,0},{2,3},{3,2},{4,5},{5,4},{6,7},{7,6},{8,9},{9,8},{10,11... | collective-permute-start | bytes 2555912 | tf_op jit(solution)/shard_map/ppermute | solution.py:513
  90.5 2.4 %collective-permute-start.8 = (f32[4,52,8,128]{3,2,1,0:T(8,128)S(1)}, f32[4,52,8,128]{3,2,1,0:T(8,128)}, u32[]{:S(2)}, u32[]{:S(2)}) collective-permute-start(f32[4,52,8,128]{3,2,1,0:T(8,128)S(1)} %collective-permute-done.5.refs_2_), channel_id=1, source_target_pairs={{0,1},{1,0},{2,3},{3,2},{4,5},{5,4},{6,7},{7,6},{8,9},{9,8},{10,11... | collective-permute-start | bytes 2555912 | tf_op jit(solution)/shard_map/ppermute | solution.py:513
  92.9 5.4 %all-gather.3.cloned.1.call-done = f32[1792,1024]{1,0:T(8,128)} async-done(((f32[56,1024]{1,0:T(8,128)}), f32[1792,1024]{1,0:T(8,128)}) %all-gather.3.cloned.1.call-update) | async-done | bytes 7340048 | tf_op jit(solution)/shard_map/all_gather | solution.py:558
  98.3 3.8 %leaf_border.1 = f32[256,512]{1,0:T(8,128)} custom-call(s32[1]{0:T(128)S(6)} %copy.19.count_ref, f32[256,1024]{1,0:T(8,128)} %bitcast.28, f32[32,56,1024]{2,1,0:T(8,128)} %bitcast.25), custom_call_target="tpu_custom_call" | custom-call | tf_op jit(solution)/shard_map/leaf_border/pallas_call | solution.py:108
  102.1 0.0 collective-permute-done.4.refs_3_
  102.1 2.2 %collective-permute-start.9 = (f32[4,52,8,128]{3,2,1,0:T(8,128)}, f32[4,52,8,128]{3,2,1,0:T(8,128)}, u32[]{:S(2)}, u32[]{:S(2)}) collective-permute-start(f32[4,52,8,128]{3,2,1,0:T(8,128)} %collective-permute-done.4.refs_3_), channel_id=1, source_target_pairs={{0,1},{1,0},{2,3},{3,2},{4,5},{5,4},{6,7},{7,6},{8,9},{9,8},{10,11... | collective-permute-start | bytes 2555912 | tf_op jit(solution)/shard_map/ppermute | solution.py:513
  104.3 6.8 %all-to-all-start.1 = ((f32[16,16,512]{2,1,0:T(8,128)}), f32[16,16,512]{2,1,0:T(8,128)S(1)}, u32[]{:S(2)}, u32[]{:S(2)}) async-start(f32[16,16,512]{2,1,0:T(8,128)} %bitcast.30), calls=%async_computation.1 | async-start | bytes 1048576 | tf_op jit(solution)/shard_map/all_to_all | solution.py:566
  111.1 0.6 broadcast_in_dim.66.index_ref
  111.7 0.6 broadcast_in_dim.67.sep_index_ref
  112.4 0.6 pad_add_fusion.place_ref
  113.0 7.0 %upper_operators.1 = (bf16[4,1024,512]{2,1,0:T(8,128)(2,1)}, bf16[4,1024,512]{2,1,0:T(8,128)(2,1)}, bf16[512,512]{1,0:T(8,128)(2,1)}, bf16[512,512]{1,0:T(8,128)(2,1)}) custom-call(s32[3]{0:T(128)} %pad_add_fusion.place_ref, f32[4,52,8,128]{3,2,1,0:T(8,128)} %copy-done.1, f32[4,52,8,128]{3,2,1,0:T(8,128)} %copy-done.5, f32[4,52,8,128]{3,2,1,0:T(8,128)} %copy-done.6, ...), custom_call_target="tpu_custom_call" | custom-call | tf_op jit(solution)/shard_map/upper_operators/pallas_call | solution.py:397
  120.0 1.9 %all-to-all-done.1.incoming_ref = f32[16,16,512]{2,1,0:T(8,128)S(1)} async-done(((f32[16,16,512]{2,1,0:T(8,128)}), f32[16,16,512]{2,1,0:T(8,128)S(1)}, u32[]{:S(2)}, u32[]{:S(2)}) %all-to-all-start.1) | async-done | bytes 524320 | tf_op jit(solution)/shard_map/all_to_all | solution.py:566
  121.9 0.8 copy-done.2
  122.7 10.6 %upper_solve.1 = (f32[16,16,512]{2,1,0:T(8,128)}, f32[4,16,512]{2,1,0:T(8,128)}, f32[16,512]{1,0:T(8,128)}) custom-call(s32[16]{0:T(128)} %parent_ref.1, f32[16,16,512]{2,1,0:T(8,128)} %copy-done.2, s32[16,1,1024]{2,1,0:T(1,128)} %broadcast_in_dim.62.slot_ref, s32[16,1,512]{2,1,0:T(1,128)} %broadcast_in_dim.66.index_ref, f32[4,16,512]{2,1,0:T(8,128)} %bitcast.34, ...), custom_call_target="tpu_custom_call" | custom-call | tf_op jit(solution)/shard_map/upper_solve/pallas_call | solution.py:482
  133.4 5.0 %all-to-all-start.2 = ((f32[16,16,512]{2,1,0:T(8,128)}), f32[16,16,512]{2,1,0:T(8,128)S(1)}, u32[]{:S(2)}, u32[]{:S(2)}) async-start(f32[16,16,512]{2,1,0:T(8,128)} %get-tuple-element.36), calls=%async_computation.2 | async-start | bytes 1048576 | tf_op jit(solution)/shard_map/all_to_all | solution.py:575
  138.4 7.1 %leaf_pivot.1 = (f32[4,256,256]{2,1,0:T(8,128)}, bf16[4,512,256]{2,1,0:T(8,128)(2,1)}, bf16[4,512,256]{2,1,0:T(8,128)(2,1)}) custom-call(s32[1]{0:T(128)S(6)} %copy.19.count_ref, f32[256,1024]{1,0:T(8,128)} %bitcast.29, f32[32,56,1024]{2,1,0:T(8,128)} %bitcast.27), custom_call_target="tpu_custom_call" | custom-call | tf_op jit(solution)/shard_map/leaf_pivot/pallas_call | solution.py:175
  145.5 0.7 copy.16
  146.2 2.2 %all-to-all-done.2 = f32[16,16,512]{2,1,0:T(8,128)S(1)} async-done(((f32[16,16,512]{2,1,0:T(8,128)}), f32[16,16,512]{2,1,0:T(8,128)S(1)}, u32[]{:S(2)}, u32[]{:S(2)}) %all-to-all-start.2) | async-done | bytes 524320 | tf_op jit(solution)/shard_map/all_to_all | solution.py:575
  148.4 0.8 copy-done.3
  149.2 5.2 %leaf_last.1 = f32[256,1024]{1,0:T(8,128)} custom-call(s32[1]{0:T(128)S(6)} %copy.19.count_ref, f32[4,256,256]{2,1,0:T(8,128)} %get-tuple-element.35.part_hbm, f32[256,512]{1,0:T(8,128)} %bitcast.31, bf16[4,512,256]{2,1,0:T(8,128)(2,1)} %get-tuple-element.37.high_hbm, bf16[4,512,256]{2,1,0:T(8,128)(2,1)} %get-tuple-element.38.low_hbm), custom_call_target="tpu_custom_call" | custom-call | tf_op jit(solution)/shard_map/leaf_last/pallas_call | solution.py:229
  (20 shorter events, 0.1 us)
Async XLA Ops:
  7.2 1.8 %copy-start = (f32[4,32,512]{2,1,0:T(8,128)S(1)}, f32[4,32,512]{2,1,0:T(8,128)}, u32[]{:S(2)}) copy-start(f32[4,32,512]{2,1,0:T(8,128)} %param.16) | copy-start | bytes 786436
  7.2 103.9 %copy-start.7 = (s32[16,512]{1,0:T(8,128)S(1)}, s32[16,512]{1,0:T(8,128)}, u32[]{:S(2)}) copy-start(s32[16,512]{1,0:T(8,128)} %param.14) | copy-start | bytes 98308
  7.2 104.6 %copy-start.9 = (s32[4,512]{1,0:T(4,128)S(1)}, s32[4,512]{1,0:T(4,128)}, u32[]{:S(2)}) copy-start(s32[4,512]{1,0:T(4,128)} %param.17) | copy-start | bytes 24580
  7.2 91.1 %all-gather.3.cloned.1.call-start = ((), (), s32[]{:S(2)}) async-start(), calls=%async_computation.3 | async-start | bytes 7569408 | tf_op jit(solution)/shard_map/all_gather | solution.py:558
  9.7 28.9 %all-to-all-start = ((f32[16,8,512]{2,1,0:T(8,128)}), f32[16,8,512]{2,1,0:T(8,128)S(1)}, u32[]{:S(2)}, u32[]{:S(2)}) async-start(f32[16,8,512]{2,1,0:T(8,128)} %broadcast_in_dim.59), calls=%async_computation | async-start | bytes 524288 | tf_op jit(solution)/shard_map/all_to_all | solution.py:529
  38.6 0.7 copy-start.4
  40.9 10.1 %collective-permute-start = (f32[52,8,128]{2,1,0:T(8,128)}, f32[52,8,128]{2,1,0:T(8,128)S(1)}, u32[]{:S(2)}, u32[]{:S(2)}) collective-permute-start(f32[52,8,128]{2,1,0:T(8,128)} %pack.1), channel_id=1, source_target_pairs={{0,32},{1,129},{32,64},{33,161},{64,96},{65,193},{96,0},{97,225},{... | collective-permute-start | bytes 638984 | tf_op jit(solution)/shard_map/ppermute | solution.py:524
  44.1 7.2 %collective-permute-start.1 = (f32[52,8,128]{2,1,0:T(8,128)}, f32[52,8,128]{2,1,0:T(8,128)S(1)}, u32[]{:S(2)}, u32[]{:S(2)}) collective-permute-start(f32[52,8,128]{2,1,0:T(8,128)} %pack.1), channel_id=1, source_target_pairs={{0,96},{1,385},{32,0},{33,417},{64,32},{65,449},{96,64},{97,481},{... | collective-permute-start | bytes 638984 | tf_op jit(solution)/shard_map/ppermute | solution.py:524
  47.5 8.3 %collective-permute-start.2 = (f32[52,8,128]{2,1,0:T(8,128)}, f32[52,8,128]{2,1,0:T(8,128)S(1)}, u32[]{:S(2)}, u32[]{:S(2)}) collective-permute-start(f32[52,8,128]{2,1,0:T(8,128)} %pack.1), channel_id=1, source_target_pairs={{0,64},{1,257},{32,96},{33,289},{64,0},{65,321},{96,32},{97,353},{... | collective-permute-start | bytes 638984 | tf_op jit(solution)/shard_map/ppermute | solution.py:524
  56.8 56.2 %copy-start.1 = (f32[4,52,8,128]{3,2,1,0:T(8,128)}, f32[4,52,8,128]{3,2,1,0:T(8,128)S(1)}, u32[]{:S(2)}) copy-start(f32[4,52,8,128]{3,2,1,0:T(8,128)S(1)} %pad_maximum_fusion.refs_0_) | copy-start | bytes 2555908
  56.8 16.4 %collective-permute-start.3 = (f32[4,52,8,128]{3,2,1,0:T(8,128)S(1)}, f32[4,52,8,128]{3,2,1,0:T(8,128)S(1)}, u32[]{:S(2)}, u32[]{:S(2)}) collective-permute-start(f32[4,52,8,128]{3,2,1,0:T(8,128)S(1)} %pad_maximum_fusion.refs_0_), channel_id=1, source_target_pairs={{0,128},{1,33},{32,160},{33,65},{64,192},{65,97},{96,224},{97,1},{... | collective-permute-start | bytes 2555912 | tf_op jit(solution)/shard_map/ppermute | solution.py:524
  59.9 30.5 %collective-permute-start.5 = (f32[4,52,8,128]{3,2,1,0:T(8,128)S(1)}, f32[4,52,8,128]{3,2,1,0:T(8,128)S(1)}, u32[]{:S(2)}, u32[]{:S(2)}) collective-permute-start(f32[4,52,8,128]{3,2,1,0:T(8,128)S(1)} %pad_maximum_fusion.refs_0_), channel_id=1, source_target_pairs={{0,384},{1,97},{32,416},{33,1},{64,448},{65,33},{96,480},{97,65},{... | collective-permute-start | bytes 2555912 | tf_op jit(solution)/shard_map/ppermute | solution.py:524
  73.2 39.9 %copy-start.5 = (f32[4,52,8,128]{3,2,1,0:T(8,128)}, f32[4,52,8,128]{3,2,1,0:T(8,128)S(1)}, u32[]{:S(2)}) copy-start(f32[4,52,8,128]{3,2,1,0:T(8,128)S(1)} %collective-permute-done.3.refs_1_) | copy-start | bytes 2555908
  73.2 28.9 %collective-permute-start.4 = (f32[4,52,8,128]{3,2,1,0:T(8,128)S(1)}, f32[4,52,8,128]{3,2,1,0:T(8,128)}, u32[]{:S(2)}, u32[]{:S(2)}) collective-permute-start(f32[4,52,8,128]{3,2,1,0:T(8,128)S(1)} %collective-permute-done.3.refs_1_), channel_id=1, source_target_pairs={{0,128},{1,33},{32,160},{33,65},{64,192},{65,97},{96,224},{97,1},{... | collective-permute-start | bytes 2555912 | tf_op jit(solution)/shard_map/ppermute | solution.py:524
  75.9 37.1 %collective-permute-start.6 = (f32[4,52,8,128]{3,2,1,0:T(8,128)S(1)}, f32[4,52,8,128]{3,2,1,0:T(8,128)}, u32[]{:S(2)}, u32[]{:S(2)}) collective-permute-start(f32[4,52,8,128]{3,2,1,0:T(8,128)S(1)} %pad_maximum_fusion.refs_0_), channel_id=1, source_target_pairs={{0,1},{1,0},{2,3},{3,2},{4,5},{5,4},{6,7},{7,6},{8,9},{9,8},{10,11... | collective-permute-start | bytes 2555912 | tf_op jit(solution)/shard_map/ppermute | solution.py:513
  88.5 24.5 %collective-permute-start.7 = (f32[4,52,8,128]{3,2,1,0:T(8,128)S(1)}, f32[4,52,8,128]{3,2,1,0:T(8,128)}, u32[]{:S(2)}, u32[]{:S(2)}) collective-permute-start(f32[4,52,8,128]{3,2,1,0:T(8,128)S(1)} %collective-permute-done.3.refs_1_), channel_id=1, source_target_pairs={{0,1},{1,0},{2,3},{3,2},{4,5},{5,4},{6,7},{7,6},{8,9},{9,8},{10,11... | collective-permute-start | bytes 2555912 | tf_op jit(solution)/shard_map/ppermute | solution.py:513
  90.5 22.6 %copy-start.6 = (f32[4,52,8,128]{3,2,1,0:T(8,128)}, f32[4,52,8,128]{3,2,1,0:T(8,128)S(1)}, u32[]{:S(2)}) copy-start(f32[4,52,8,128]{3,2,1,0:T(8,128)S(1)} %collective-permute-done.5.refs_2_) | copy-start | bytes 2555908
  90.5 22.5 %collective-permute-start.8 = (f32[4,52,8,128]{3,2,1,0:T(8,128)S(1)}, f32[4,52,8,128]{3,2,1,0:T(8,128)}, u32[]{:S(2)}, u32[]{:S(2)}) collective-permute-start(f32[4,52,8,128]{3,2,1,0:T(8,128)S(1)} %collective-permute-done.5.refs_2_), channel_id=1, source_target_pairs={{0,1},{1,0},{2,3},{3,2},{4,5},{5,4},{6,7},{7,6},{8,9},{9,8},{10,11... | collective-permute-start | bytes 2555912 | tf_op jit(solution)/shard_map/ppermute | solution.py:513
  102.1 10.9 %collective-permute-start.9 = (f32[4,52,8,128]{3,2,1,0:T(8,128)}, f32[4,52,8,128]{3,2,1,0:T(8,128)}, u32[]{:S(2)}, u32[]{:S(2)}) collective-permute-start(f32[4,52,8,128]{3,2,1,0:T(8,128)} %collective-permute-done.4.refs_3_), channel_id=1, source_target_pairs={{0,1},{1,0},{2,3},{3,2},{4,5},{5,4},{6,7},{7,6},{8,9},{9,8},{10,11... | collective-permute-start | bytes 2555912 | tf_op jit(solution)/shard_map/ppermute | solution.py:513
  104.3 17.7 %all-to-all-start.1 = ((f32[16,16,512]{2,1,0:T(8,128)}), f32[16,16,512]{2,1,0:T(8,128)S(1)}, u32[]{:S(2)}, u32[]{:S(2)}) async-start(f32[16,16,512]{2,1,0:T(8,128)} %bitcast.30), calls=%async_computation.1 | async-start | bytes 1048576 | tf_op jit(solution)/shard_map/all_to_all | solution.py:566
  121.9 0.8 copy-start.2
  133.4 12.1 %copy-start.8 = (f32[4,16,512]{2,1,0:T(8,128)S(1)}, f32[4,16,512]{2,1,0:T(8,128)}, u32[]{:S(2)}) copy-start(f32[4,16,512]{2,1,0:T(8,128)} %get-tuple-element.39) | copy-start | bytes 393220
  133.4 15.1 %all-to-all-start.2 = ((f32[16,16,512]{2,1,0:T(8,128)}), f32[16,16,512]{2,1,0:T(8,128)S(1)}, u32[]{:S(2)}, u32[]{:S(2)}) async-start(f32[16,16,512]{2,1,0:T(8,128)} %get-tuple-element.36), calls=%async_computation.2 | async-start | bytes 1048576 | tf_op jit(solution)/shard_map/all_to_all | solution.py:575
  148.4 0.8 copy-start.3
Sparse Core Ops, SparseCore 0:
  10.2 88.1 all-gather.2
